TPU v7x, 512 devices: a whole 4x8x8 slice. The times are simulated.
512 devices in a mesh: fsdp: 32 (over z_lo, y), mp: 16 (over x, z_hi, core).
Axes of the slice: x: 4, y: 8, z: 8 (z_hi: 2, z_lo: 4; z = z_hi * 4 + z_lo), core: 2. Of those that a mesh axis runs over, the one named last changes fastest.
Arguments:
- tokens: bfloat16 [6144, 3072], P('fsdp'), may hold values from -6 to 6
- pre_act: bfloat16 [6144, 12288], P('fsdp', 'mp'), may hold values from -6 to 6
- grad_act: bfloat16 [6144, 12288], P('fsdp', 'mp'), may hold values from -6 to 6
- w_up: bfloat16 [3072, 12288], P('fsdp', 'mp'), may hold values from -0.109375 to 0.109375
Outputs:
- grad_weight: bfloat16 [3072, 12288], P('fsdp', 'mp')
- grad_input: bfloat16 [6144, 3072], P('fsdp')
All inputs are finite; a program needn't handle non-finite values.
Results may differ from a plain program's by a relative error of at most 0.022.
Values may be sent and summed in bfloat16 or wider, within the bound.
No kernel may reach another device: no remote copies, remote signals or barrier semaphores. Data moves between devices by JAX's collectives and lax.ppermute only.
A program may use at most 64 MiB of HBM per device.

v0:
```python
import math

import jax
import jax.numpy as jnp
from jax import lax
from jax.sharding import PartitionSpec as P


def gelu_slope(hidden):
    coeff = math.sqrt(2.0 / math.pi)
    inner = coeff * (hidden + 0.044715 * hidden * hidden * hidden)
    tangent = jnp.tanh(inner)
    return 0.5 * (1.0 + tangent) + 0.5 * hidden * (1.0 - tangent * tangent) * coeff * (
        1.0 + 3.0 * 0.044715 * hidden * hidden
    )


def shards(tokens, pre_act, grad_act, w_up):
    hidden_grad = (grad_act.astype(jnp.float32) * gelu_slope(pre_act.astype(jnp.float32))).astype(
        jnp.bfloat16
    )
    norm_factor = float(hidden_grad.shape[0] * lax.axis_size("fsdp")) ** (-0.5)
    local_sum = lax.dot_general(
        tokens, hidden_grad, (((0,), (0,)), ((), ())), preferred_element_type=jnp.float32
    )
    received = lax.all_to_all(
        local_sum[None].astype(jnp.bfloat16), "fsdp", split_axis=1, concat_axis=0, tiled=True
    ).astype(jnp.float32)
    weight_sum = jnp.sum(received, axis=0)
    partial_input = lax.dot_general(
        hidden_grad,
        lax.all_gather(w_up, "fsdp", axis=0, tiled=True),
        (((1,), (1,)), ((), ())),
        preferred_element_type=jnp.float32,
    ).astype(jnp.bfloat16)
    grad_weight = (weight_sum * norm_factor).astype(jnp.bfloat16)
    grad_input = lax.psum(partial_input, "mp").astype(jnp.float32).astype(jnp.bfloat16)
    return (grad_weight, grad_input)


def solution(mesh):
    placed = (P("fsdp", None), P("fsdp", "mp"), P("fsdp", "mp"), P("fsdp", "mp"))
    return jax.shard_map(
        shards,
        mesh=mesh,
        in_specs=placed,
        out_specs=(P("fsdp", "mp"), P("fsdp", None)),
        check_vma=False,
    )
```

profile of v0, /device:TPU:1, one launch (start us, length us, event | category | flops | bytes accessed | tf_op | source)
XLA Modules:
  0.0 446.9 jit_solution(6570691295177326035)
XLA Ops:
  7.2 0.0 copy-start
  7.2 0.0 all-gather.2.cloned.1.call-start
  7.2 0.7 all-gather.2.cloned.1.call-update
  7.9 0.5 copy-done
  8.4 4.9 %fusion = bf16[1,3072,768]{1,2,0:T(8,128)(2,1)} fusion(bf16[192,3072]{1,0:T(8,128)(2,1)S(1)} %copy-done, bf16[192,768]{1,0:T(8,128)(2,1)} %param.5, bf16[192,768]{1,0:T(8,128)(2,1)} %param.6), kind=kOutput, calls=%fused_computation.2 | convolution fusion | flops 911425536 | bytes 6488064 | tf_op jit(solution)/shard_map/dot_general | solution.py:23
  13.4 20.4 %copy.7 = bf16[1,3072,768]{2,0,1:T(2,128)(2,1)} copy(bf16[1,3072,768]{1,2,0:T(8,128)(2,1)} %fusion) | data formatting | bytes 9437184 | tf_op jit(solution)/shard_map/convert_element_type | solution.py:27
  33.7 0.5 broadcast.21
  34.2 48.9 %reduce = bf16[3072,768]{1,0:T(8,128)(2,1)} reduce(bf16[3072,1,768]{2,1,0:T(2,128)(2,1)} %bitcast.10, bf16[]{:T(256)} %broadcast.21), dimensions={1}, to_apply=%bitcast.6.reduce_sub_computation | reduce | bytes 9437186
  83.2 7.2 %reshape.11 = bf16[32,2,36864]{2,1,0:T(2,128)(2,1)} reshape(bf16[3072,768]{1,0:T(8,128)(2,1)} %reduce) | data formatting | bytes 9437184
  90.4 0.0 copy-start.1
  90.4 0.0 copy-start.2
  90.4 13.7 %all-to-all-start = ((bf16[32,2,36864]{2,1,0:T(2,128)(2,1)}), bf16[32,2,36864]{2,1,0:T(2,128)(2,1)}, u32[]{:S(2)}, u32[]{:S(2)}) async-start(bf16[32,2,36864]{2,1,0:T(2,128)(2,1)} %reshape.11), calls=%async_computation | async-start | bytes 9437184 | tf_op jit(solution)/shard_map/all_to_all | solution.py:26
  104.1 0.0 all-reduce.2.cloned.1.call-start
  104.2 117.2 %all-gather.2.cloned.1.call-done = bf16[3072,768]{1,0:T(8,128)(2,1)} async-done(((bf16[96,768]{1,0:T(8,128)(2,1)}), bf16[3072,768]{1,0:T(8,128)(2,1)}) %all-gather.2.cloned.1.call-update) | async-done | bytes 4718608 | tf_op jit(solution)/shard_map/all_gather | solution.py:32
  221.4 0.0 copy-done.1
  221.4 0.0 copy-done.2
  221.4 5.2 %convolution_convert_fusion.1 = bf16[192,3072]{1,0:T(8,128)(2,1)} fusion(bf16[3072,768]{1,0:T(8,128)(2,1)} %all-gather.2.cloned.1.call-done, bf16[192,768]{1,0:T(8,128)(2,1)S(1)} %copy-done.1, bf16[192,768]{1,0:T(8,128)(2,1)S(1)} %copy-done.2), kind=kOutput, calls=%fused_computation.3 | convolution fusion | flops 909656064 | bytes 6488064 | tf_op jit(solution)/shard_map/dot_general | solution.py:30
  226.6 0.0 all-reduce.2.cloned.1.call-update
  226.6 6.4 %all-to-all-done = bf16[32,2,36864]{2,1,0:T(2,128)(2,1)} async-done(((bf16[32,2,36864]{2,1,0:T(2,128)(2,1)}), bf16[32,2,36864]{2,1,0:T(2,128)(2,1)}, u32[]{:S(2)}, u32[]{:S(2)}) %all-to-all-start) | async-done | bytes 4718624 | tf_op jit(solution)/shard_map/all_to_all | solution.py:26
  233.0 20.2 %reshape.12 = bf16[3072,1,768]{2,1,0:T(2,128)(2,1)} reshape(bf16[32,2,36864]{2,1,0:T(2,128)(2,1)} %all-to-all-done) | data formatting | bytes 9437184
  253.2 4.5 %copy.8 = bf16[1,3072,768]{2,1,0:T(8,128)(2,1)S(1)} copy(bf16[1,3072,768]{2,0,1:T(2,128)(2,1)} %bitcast.11) | data formatting | bytes 9437184 | tf_op jit(solution)/shard_map/all_to_all | solution.py:26
  257.7 0.7 convert_reduce_fusion
  258.4 0.7 multiply_convert_fusion
  259.1 178.6 %all-reduce.2.cloned.1.call-done = bf16[192,3072]{1,0:T(8,128)(2,1)} async-done(((bf16[192,3072]{1,0:T(8,128)(2,1)}), bf16[192,3072]{1,0:T(8,128)(2,1)}) %all-reduce.2.cloned.1.call-update) | async-done | bytes 1179664 | tf_op jit(solution)/shard_map/psum | solution.py:37
  437.7 2.4 copy.10
Async XLA Ops:
  7.2 1.3 copy-start
  7.2 214.2 %all-gather.2.cloned.1.call-start = ((), (), s32[]{:S(2)}) async-start(), calls=%async_computation.1 | async-start | bytes 4866048 | tf_op jit(solution)/shard_map/all_gather | solution.py:32
  90.4 131.0 %copy-start.1 = (bf16[192,768]{1,0:T(8,128)(2,1)S(1)}, bf16[192,768]{1,0:T(8,128)(2,1)}, u32[]{:S(2)}) copy-start(bf16[192,768]{1,0:T(8,128)(2,1)} %param.5) | copy-start | bytes 884740
  90.4 131.0 %copy-start.2 = (bf16[192,768]{1,0:T(8,128)(2,1)S(1)}, bf16[192,768]{1,0:T(8,128)(2,1)}, u32[]{:S(2)}) copy-start(bf16[192,768]{1,0:T(8,128)(2,1)} %param.6) | copy-start | bytes 884740
  90.4 142.6 %all-to-all-start = ((bf16[32,2,36864]{2,1,0:T(2,128)(2,1)}), bf16[32,2,36864]{2,1,0:T(2,128)(2,1)}, u32[]{:S(2)}, u32[]{:S(2)}) async-start(bf16[32,2,36864]{2,1,0:T(2,128)(2,1)} %reshape.11), calls=%async_computation | async-start | bytes 9437184 | tf_op jit(solution)/shard_map/all_to_all | solution.py:26
  104.1 333.6 %all-reduce.2.cloned.1.call-start = ((), (), s32[]{:S(2)}) async-start(), calls=%async_computation.2 | async-start | bytes 2359296 | tf_op jit(solution)/shard_map/psum | solution.py:37
Sparse Core Ops, SparseCore 0:
  10.1 211.2 all-gather.1
  226.7 210.9 all-reduce.1
where the time goes:
time: 448 us; the launch traced here: 447 us
  waiting for transfers between devices  303 us (68%)
  local copies, waits for them, and re-layouts  55.7 us (12%)
  other arithmetic  50.3 us (11%)
  between operations  14.1 us (3%)
  starting transfers between devices  13.8 us (3%)
  matrix products  10.1 us (2%)
    psum x1, waiting for transfers between devices, shards(): lax.psum(partial_input, 'mp').astype(jnp.float32).astype(jnp.bfloat16)  179 us
    all_gather x1, waiting for transfers between devices, shards(): lax.all_gather(w_up, 'fsdp', axis=0, tiled=True)  117 us
    unnamed x1, other arithmetic  48.9 us
    unnamed x10, local copies, waits for them, and re-layouts  30.9 us
    convert_element_type x1, local copies, waits for them, and re-layouts, shards(): local_sum[None].astype(jnp.bfloat16)  20.4 us
    all_to_all x1, starting transfers between devices, shards(): lax.all_to_all(local_sum[None].astype(jnp.bfloat16), 'fsdp', split_axis=1...  13.7 us
  transfers between devices with their start and end apart: 3, of which 3 were waited for; matrix products, arithmetic and copies ran while one was open for 25% of the time, Pallas kernels for 0%

commit v1 on v0

v1 whole, which is shorter than its diff:
```python
import math

import jax
import jax.numpy as jnp
from jax import lax
from jax.sharding import PartitionSpec as P

Z_LO, Y = 4, 8
X, Z_HI, CORE = 4, 2, 2


def fsdp_index(z, y):
    return z * Y + y


def mp_index(x, h, c):
    return (x * Z_HI + h) * CORE + c


Y_GROUPS = [[fsdp_index(z, y) for y in range(Y)] for z in range(Z_LO)]
Z_GROUPS = [[fsdp_index(z, y) for z in range(Z_LO)] for y in range(Y)]
X_GROUPS = [[mp_index(x, h, c) for x in range(X)] for h in range(Z_HI) for c in range(CORE)]
C_GROUPS = [[mp_index(x, h, c) for c in range(CORE)] for x in range(X) for h in range(Z_HI)]
RING_GROUPS = [
    [fsdp_index(z, y) * (X * Z_HI * CORE) + mp_index(x, h, c) for h in range(Z_HI) for z in range(Z_LO)]
    for y in range(Y)
    for x in range(X)
    for c in range(CORE)
]


def gelu_slope(hidden):
    coeff = math.sqrt(2.0 / math.pi)
    inner = coeff * (hidden + 0.044715 * hidden * hidden * hidden)
    tangent = jnp.tanh(inner)
    return 0.5 * (1.0 + tangent) + 0.5 * hidden * (1.0 - tangent * tangent) * coeff * (
        1.0 + 3.0 * 0.044715 * hidden * hidden
    )


def swap(blocks, axis, groups):
    return lax.all_to_all(blocks, axis, 0, 0, axis_index_groups=groups, tiled=True)


def added(blocks):
    return jnp.sum(blocks.astype(jnp.float32), axis=0).astype(jnp.bfloat16)


def shards(tokens, pre_act, grad_act, w_up):
    rows, width = tokens.shape
    units = pre_act.shape[1]
    quarter = width // Z_LO
    norm_factor = float(rows * Z_LO * Y) ** (-0.5)

    weight = lax.all_gather(w_up, "fsdp", axis=0, axis_index_groups=Y_GROUPS, tiled=True)
    hidden_grad = (grad_act.astype(jnp.float32) * gelu_slope(pre_act.astype(jnp.float32))).astype(
        jnp.bfloat16
    )
    hidden = swap(jnp.broadcast_to(hidden_grad[None], (Z_LO, rows, units)), "fsdp", Z_GROUPS)
    hidden = hidden.reshape(Z_LO * rows, units)
    patches = swap(tokens.reshape(rows, Z_LO, quarter).transpose(1, 0, 2), "fsdp", Z_GROUPS)
    patches = patches.reshape(Z_LO * rows, quarter)

    weight_part = lax.dot_general(
        patches, hidden, (((0,), (0,)), ((), ())), preferred_element_type=jnp.float32
    ).astype(jnp.bfloat16)
    received = swap(weight_part.reshape(Y, quarter // Y, units), "fsdp", Y_GROUPS)
    grad_weight = (jnp.sum(received.astype(jnp.float32), axis=0) * norm_factor).astype(jnp.bfloat16)

    partial = lax.dot_general(
        hidden, weight, (((1,), (1,)), ((), ())), preferred_element_type=jnp.float32
    ).astype(jnp.bfloat16)
    piece = rows // (CORE * X)
    partial = partial.reshape(Z_LO, CORE, X, piece, quarter).transpose(1, 2, 0, 3, 4)
    partial = added(swap(partial, "mp", C_GROUPS).reshape(CORE, X, Z_LO, piece, quarter))
    partial = added(swap(partial, "mp", X_GROUPS))
    both = jnp.broadcast_to(partial[None], (Z_HI, Z_LO, piece, quarter))
    both = swap(both.reshape(Z_HI * Z_LO, piece, quarter), ("fsdp", "mp"), RING_GROUPS)
    mine = added(both.reshape(Z_HI, Z_LO, piece, quarter))
    mine = mine.transpose(1, 0, 2).reshape(piece, width)
    mine = lax.all_gather(mine, "mp", axis=0, axis_index_groups=X_GROUPS, tiled=True)
    half = jnp.broadcast_to(mine[None], (CORE, X * piece, width))
    grad_input = swap(half, "mp", C_GROUPS).reshape(rows, width)
    return (grad_weight, grad_input)


def solution(mesh):
    placed = (P("fsdp", None), P("fsdp", "mp"), P("fsdp", "mp"), P("fsdp", "mp"))
    return jax.shard_map(
        shards,
        mesh=mesh,
        in_specs=placed,
        out_specs=(P("fsdp", "mp"), P("fsdp", None)),
        check_vma=False,
    )
```

time: 448 us -> 195 us (0.44)
  waiting for transfers between devices: 303 us -> 85.5 us
  blocking collectives: 0 us -> 64.6 us
  local copies, waits for them, and re-layouts: 55.7 us -> 4.05 us
  other arithmetic: 50.3 us -> 2.71 us
  matrix products: 10.1 us -> 4.53 us
  starting transfers between devices: 13.8 us -> 18.9 us
    psum x1 -> x0, waiting for transfers between devices: 179 us -> none  [shards(): lax.psum(partial_input, 'mp').astype(jnp.float32).astype(jnp.bfloat16)]
    all_gather x1, waiting for transfers between devices: 117 us -> 7.87 us  [shards(): lax.all_gather(w_up, 'fsdp', axis=0, axis_index_groups=Y_GROUPS, tiled=True)]
    all_to_all x1 -> x4, waiting for transfers between devices: 6.4 us -> 76.9 us  [swap(): lax.all_to_all(blocks, axis, 0, 0, axis_index_groups=groups, tiled=True)]
    all_to_all x0 -> x3, blocking collectives: none -> 53.9 us  [swap(): lax.all_to_all(blocks, axis, 0, 0, axis_index_groups=groups, tiled=True)]
    unnamed x1 -> x0, other arithmetic: 48.9 us -> none
    unnamed x10 -> x7, local copies, waits for them, and re-layouts: 30.9 us -> 1.03 us
    convert_element_type x1 -> x0, local copies, waits for them, and re-layouts: 20.4 us -> none  [shards(): local_sum[None].astype(jnp.bfloat16)]
    all_gather x0 -> x1, blocking collectives: none -> 10.7 us  [shards(): lax.all_gather(mine, 'mp', axis=0, axis_index_groups=X_GROUPS, tiled=True)]
  transfers between devices with their start and end apart: 3 -> 5, of which waited for: 3 -> 5; matrix products, arithmetic and copies ran while one was open for 25% -> 3% of each run, Pallas kernels for 0% -> 0%
where the time goes in v1:
time: 195 us; the launch traced here: 194 us
  waiting for transfers between devices  85.5 us (44%)
  blocking collectives  64.6 us (33%)
  starting transfers between devices  18.9 us (10%)
  between operations  14.1 us (7%)
  matrix products  4.53 us (2%)
  local copies, waits for them, and re-layouts  4.05 us (2%)
  other arithmetic  2.71 us (1%)
    all_to_all x4, waiting for transfers between devices, swap(): lax.all_to_all(blocks, axis, 0, 0, axis_index_groups=groups, tiled=True)  76.9 us
    all_to_all x3, blocking collectives, swap(): lax.all_to_all(blocks, axis, 0, 0, axis_index_groups=groups, tiled=True)  53.9 us
    all_to_all x4, starting transfers between devices, swap(): lax.all_to_all(blocks, axis, 0, 0, axis_index_groups=groups, tiled=True)  18.9 us
    all_gather x1, blocking collectives, shards(): lax.all_gather(mine, 'mp', axis=0, axis_index_groups=X_GROUPS, tiled=True)  10.7 us
    all_gather x1, waiting for transfers between devices, shards(): lax.all_gather(w_up, 'fsdp', axis=0, axis_index_groups=Y_GROUPS, tiled=True)  7.87 us
  transfers between devices with their start and end apart: 5, of which 5 were waited for; matrix products, arithmetic and copies ran while one was open for 3% of the time, Pallas kernels for 0%

profile of v1, /device:TPU:1, one launch (start us, length us, event | category | flops | bytes accessed | tf_op | source)
XLA Modules:
  0.0 194.4 jit_solution(3792913504839872534)
XLA Ops:
  7.2 0.0 all-gather.2.cloned.1.call-start
  7.2 0.7 all-gather.2.cloned.1.call-update
  7.9 1.5 fusion.7
  9.4 0.1 broadcast_in_dim.6
  9.4 35.5 %all_to_all.35 = bf16[4,192,768]{2,1,0:T(8,128)(2,1)S(1)} all-to-all(bf16[4,192,768]{2,1,0:T(8,128)(2,1)S(1)} %broadcast_in_dim.6), channel_id=1, replica_groups={{0,128,256,384},{16,144,272,400},{32,160,288,416},{48,176,304,432},{64,..., dimensions={0} | all-to-all | bytes 2359296 | tf_op jit(solution)/shard_map/all_to_all | solution.py:42
  45.0 0.0 copy-start.1
  45.0 7.9 %all-gather.2.cloned.1.call-done = bf16[768,768]{1,0:T(8,128)(2,1)} async-done(((bf16[96,768]{1,0:T(8,128)(2,1)}), bf16[768,768]{1,0:T(8,128)(2,1)}) %all-gather.2.cloned.1.call-update) | async-done | bytes 1179664 | tf_op jit(solution)/shard_map/all_gather | solution.py:55
  52.8 2.4 %convolution_convert_fusion = bf16[768,768]{1,0:T(8,128)(2,1)S(1)} fusion(bf16[768,768]{1,0:T(8,128)(2,1)S(1)} %bitcast.30, bf16[768,768]{1,0:T(8,128)(2,1)} %all-gather.2.cloned.1.call-done), kind=kOutput, calls=%fused_computation.2 | convolution fusion | flops 906559488 | bytes 3538944 | tf_op jit(solution)/shard_map/dot_general | solution.py:70
  55.2 0.0 copy-done.1
  55.2 0.1 copy.29
  55.3 8.9 %all_to_all.36 = bf16[2,4,4,24,768]{4,3,1,2,0:T(8,128)(2,1)S(1)} all-to-all(bf16[2,4,4,24,768]{4,3,1,2,0:T(8,128)(2,1)S(1)} %bitcast.28), channel_id=1, replica_groups={{0,1},{2,3},{4,5},{6,7},{8,9},{10,11},{12,13},{14,15},{16,17},{18,19},{..., dimensions={0} | all-to-all | bytes 2359296 | tf_op jit(solution)/shard_map/all_to_all | solution.py:42
  64.2 0.2 reduce_sum.46
  64.5 0.0 copy-start
  64.5 0.9 copy.21
  65.4 4.1 %all-to-all-start.4 = ((bf16[4,4,24,768]{3,2,1,0:T(8,128)(2,1)}), bf16[4,4,24,768]{3,2,1,0:T(8,128)(2,1)S(1)}, u32[]{:S(2)}, u32[]{:S(2)}) async-start(bf16[4,4,24,768]{3,2,1,0:T(8,128)(2,1)} %copy.21), calls=%async_computation.4 | async-start | bytes 1179648 | tf_op jit(solution)/shard_map/all_to_all | solution.py:42
  69.5 0.0 copy-done
  69.5 1.1 copy.28
  70.6 8.5 %all-to-all-done.4 = bf16[4,4,24,768]{3,2,1,0:T(8,128)(2,1)S(1)} async-done(((bf16[4,4,24,768]{3,2,1,0:T(8,128)(2,1)}), bf16[4,4,24,768]{3,2,1,0:T(8,128)(2,1)S(1)}, u32[]{:S(2)}, u32[]{:S(2)}) %all-to-all-start.4) | async-done | bytes 589856 | tf_op jit(solution)/shard_map/all_to_all | solution.py:42
  79.1 4.8 %all-to-all-start.1 = ((bf16[4,192,768]{2,1,0:T(8,128)(2,1)}), bf16[4,192,768]{2,1,0:T(8,128)(2,1)S(1)}, u32[]{:S(2)}, u32[]{:S(2)}) async-start(bf16[4,192,768]{2,1,0:T(8,128)(2,1)} %bitcast.25), calls=%async_computation.1 | async-start | bytes 2359296 | tf_op jit(solution)/shard_map/all_to_all | solution.py:42
  83.9 0.0 copy-start.2
  83.9 0.1 reduce_sum.47
  83.9 27.9 %all-to-all-done.1 = bf16[4,192,768]{2,1,0:T(8,128)(2,1)S(1)} async-done(((bf16[4,192,768]{2,1,0:T(8,128)(2,1)}), bf16[4,192,768]{2,1,0:T(8,128)(2,1)S(1)}, u32[]{:S(2)}, u32[]{:S(2)}) %all-to-all-start.1) | async-done | bytes 1179680 | tf_op jit(solution)/shard_map/all_to_all | solution.py:42
  111.9 0.7 broadcast_in_dim.7
  112.6 5.8 %all-to-all-start.5 = ((bf16[8,24,768]{2,1,0:T(8,128)(2,1)}), bf16[8,24,768]{2,1,0:T(8,128)(2,1)S(1)}, u32[]{:S(2)}, u32[]{:S(2)}) async-start(bf16[8,24,768]{2,1,0:T(8,128)(2,1)} %bitcast.7), calls=%async_computation.5 | async-start | bytes 589824 | tf_op jit(solution)/shard_map/all_to_all | solution.py:42
  118.4 0.0 copy-done.2
  118.4 2.1 %bitcast_convert_fusion = bf16[768,768]{0,1:T(8,128)(2,1)} fusion(bf16[4,192,768]{2,1,0:T(8,128)(2,1)S(1)} %copy-done.2, bf16[4,192,768]{2,1,0:T(8,128)(2,1)S(1)} %all-to-all-done.1), kind=kOutput, calls=%fused_computation | convolution fusion | flops 906559488 | bytes 3538944 | tf_op jit(solution)/shard_map/dot_general | solution.py:64
  120.6 8.4 %all-to-all-done.5 = bf16[8,24,768]{2,1,0:T(8,128)(2,1)S(1)} async-done(((bf16[8,24,768]{2,1,0:T(8,128)(2,1)}), bf16[8,24,768]{2,1,0:T(8,128)(2,1)S(1)}, u32[]{:S(2)}, u32[]{:S(2)}) %all-to-all-start.5) | async-done | bytes 294944 | tf_op jit(solution)/shard_map/all_to_all | solution.py:42
  129.0 0.1 reduce_sum.48
  129.1 10.7 %all_gather.7 = bf16[96,3072]{1,0:T(8,128)(2,1)S(1)} all-gather(bf16[24,3072]{1,0:T(8,128)(2,1)S(1)} %bitcast.34), channel_id=1, replica_groups={{0,4,8,12},{1,5,9,13},{2,6,10,14},{3,7,11,15},{16,20,24,28},{17,21,25,2..., dimensions={0}, use_global_device_ids=true | all-gather | bytes 737280 | tf_op jit(solution)/shard_map/all_gather | solution.py:81
  139.8 0.1 broadcast_in_dim.8
  139.9 9.5 %all_to_all.37 = bf16[2,96,3072]{2,1,0:T(8,128)(2,1)S(1)} all-to-all(bf16[2,96,3072]{2,1,0:T(8,128)(2,1)S(1)} %broadcast_in_dim.8), channel_id=1, replica_groups={{0,1},{2,3},{4,5},{6,7},{8,9},{10,11},{12,13},{14,15},{16,17},{18,19},{..., dimensions={0} | all-to-all | bytes 2359296 | tf_op jit(solution)/shard_map/all_to_all | solution.py:42
  149.4 4.2 %all-to-all-start.2 = ((bf16[8,96,768]{2,1,0:T(8,128)(2,1)}), bf16[8,96,768]{2,1,0:T(8,128)(2,1)S(1)}, u32[]{:S(2)}, u32[]{:S(2)}) async-start(bf16[8,96,768]{2,1,0:T(8,128)(2,1)} %bitcast.3), calls=%async_computation.2 | async-start | bytes 2359296 | tf_op jit(solution)/shard_map/all_to_all | solution.py:42
  153.6 32.1 %all-to-all-done.2 = bf16[8,96,768]{2,1,0:T(8,128)(2,1)S(1)} async-done(((bf16[8,96,768]{2,1,0:T(8,128)(2,1)}), bf16[8,96,768]{2,1,0:T(8,128)(2,1)S(1)}, u32[]{:S(2)}, u32[]{:S(2)}) %all-to-all-start.2) | async-done | bytes 1179680 | tf_op jit(solution)/shard_map/all_to_all | solution.py:42
  185.7 0.2 convert_reduce_fusion
  185.9 0.7 multiply_convert_fusion
  186.6 1.0 copy.31
  (1 shorter events, 0.0 us)
Async XLA Ops:
  7.2 45.7 %all-gather.2.cloned.1.call-start = ((), (), s32[]{:S(2)}) async-start(), calls=%async_computation.7 | async-start | bytes 1327104 | tf_op jit(solution)/shard_map/all_gather | solution.py:55
  45.0 10.3 %copy-start.1 = (bf16[4,192,768]{2,1,0:T(8,128)(2,1)}, bf16[4,192,768]{2,1,0:T(8,128)(2,1)S(1)}, u32[]{:S(2)}) copy-start(bf16[4,192,768]{2,1,0:T(8,128)(2,1)S(1)} %all_to_all.35) | copy-start | bytes 3538948
  64.5 5.0 %copy-start = (bf16[192,3072]{1,0:T(8,128)(2,1)S(1)}, bf16[192,3072]{1,0:T(8,128)(2,1)}, u32[]{:S(2)}) copy-start(bf16[192,3072]{1,0:T(8,128)(2,1)} %param.4) | copy-start | bytes 3538948
  65.4 13.7 %all-to-all-start.4 = ((bf16[4,4,24,768]{3,2,1,0:T(8,128)(2,1)}), bf16[4,4,24,768]{3,2,1,0:T(8,128)(2,1)S(1)}, u32[]{:S(2)}, u32[]{:S(2)}) async-start(bf16[4,4,24,768]{3,2,1,0:T(8,128)(2,1)} %copy.21), calls=%async_computation.4 | async-start | bytes 1179648 | tf_op jit(solution)/shard_map/all_to_all | solution.py:42
  79.1 32.8 %all-to-all-start.1 = ((bf16[4,192,768]{2,1,0:T(8,128)(2,1)}), bf16[4,192,768]{2,1,0:T(8,128)(2,1)S(1)}, u32[]{:S(2)}, u32[]{:S(2)}) async-start(bf16[4,192,768]{2,1,0:T(8,128)(2,1)} %bitcast.25), calls=%async_computation.1 | async-start | bytes 2359296 | tf_op jit(solution)/shard_map/all_to_all | solution.py:42
  83.9 34.6 %copy-start.2 = (bf16[4,192,768]{2,1,0:T(8,128)(2,1)S(1)}, bf16[4,192,768]{2,1,0:T(8,128)(2,1)}, u32[]{:S(2)}) copy-start(bf16[4,192,768]{2,1,0:T(8,128)(2,1)} %copy-done.1) | copy-start | bytes 3538948
  112.6 16.4 %all-to-all-start.5 = ((bf16[8,24,768]{2,1,0:T(8,128)(2,1)}), bf16[8,24,768]{2,1,0:T(8,128)(2,1)S(1)}, u32[]{:S(2)}, u32[]{:S(2)}) async-start(bf16[8,24,768]{2,1,0:T(8,128)(2,1)} %bitcast.7), calls=%async_computation.5 | async-start | bytes 589824 | tf_op jit(solution)/shard_map/all_to_all | solution.py:42
  149.4 36.3 %all-to-all-start.2 = ((bf16[8,96,768]{2,1,0:T(8,128)(2,1)}), bf16[8,96,768]{2,1,0:T(8,128)(2,1)S(1)}, u32[]{:S(2)}, u32[]{:S(2)}) async-start(bf16[8,96,768]{2,1,0:T(8,128)(2,1)} %bitcast.3), calls=%async_computation.2 | async-start | bytes 2359296 | tf_op jit(solution)/shard_map/all_to_all | solution.py:42
Sparse Core Ops, SparseCore 0:
  10.1 42.7 all-gather.1

commit v2 on v1

v2 whole, which is shorter than its diff:
```python
import math

import jax
import jax.numpy as jnp
from jax import lax
from jax.sharding import PartitionSpec as P

Z_LO, Y = 4, 8
X, Z_HI, CORE = 4, 2, 2
AXES = ("fsdp", "mp")


def fsdp_index(z, y):
    return z * Y + y


def mp_index(x, h, c):
    return (x * Z_HI + h) * CORE + c


Y_GROUPS = [[fsdp_index(z, y) for y in range(Y)] for z in range(Z_LO)]


def moved(value, target):
    pairs = []
    for z in range(Z_LO):
        for y in range(Y):
            for x in range(X):
                for h in range(Z_HI):
                    for c in range(CORE):
                        z2, y2, x2, h2, c2 = target(z, y, x, h, c)
                        source = fsdp_index(z, y) * X * Z_HI * CORE + mp_index(x, h, c)
                        goal = fsdp_index(z2, y2) * X * Z_HI * CORE + mp_index(x2, h2, c2)
                        pairs.append((source, goal))
    return lax.ppermute(value, AXES, pairs)


def along_z_lo(value, step):
    return moved(value, lambda z, y, x, h, c: ((z + step) % Z_LO, y, x, h, c))


def along_ring(value, step):
    def target(z, y, x, h, c):
        place = (h * Z_LO + z + step) % (Z_HI * Z_LO)
        return place % Z_LO, y, x, place // Z_LO, c

    return moved(value, target)


def along_x(value, step):
    return moved(value, lambda z, y, x, h, c: (z, y, (x + step) % X, h, c))


def to_other_core(value):
    return moved(value, lambda z, y, x, h, c: (z, y, x, h, 1 - c))


def gelu_slope(hidden):
    coeff = math.sqrt(2.0 / math.pi)
    inner = coeff * (hidden + 0.044715 * hidden * hidden * hidden)
    tangent = jnp.tanh(inner)
    return 0.5 * (1.0 + tangent) + 0.5 * hidden * (1.0 - tangent * tangent) * coeff * (
        1.0 + 3.0 * 0.044715 * hidden * hidden
    )


def swap(blocks, axis, groups):
    return lax.all_to_all(blocks, axis, 0, 0, axis_index_groups=groups, tiled=True)


def total(parts):
    result = parts[0].astype(jnp.float32)
    for part in parts[1:]:
        result = result + part.astype(jnp.float32)
    return result.astype(jnp.bfloat16)


def canonical(blocks, shift, axis):
    n = blocks.shape[axis]
    doubled = jnp.concatenate([jnp.flip(blocks, axis)] * 2, axis)
    return lax.dynamic_slice_in_dim(doubled, (n - 1 - shift) % n, n, axis)


def shards(tokens, pre_act, grad_act, w_up):
    rows, width = tokens.shape
    units = pre_act.shape[1]
    quarter = width // Z_LO
    half = quarter // CORE
    norm_factor = float(rows * Z_LO * Y) ** (-0.5)
    z_lo = lax.axis_index("fsdp") // Y
    x = lax.axis_index("mp") // (Z_HI * CORE)
    core = lax.axis_index("mp") % CORE

    weight = swap(jnp.broadcast_to(w_up[None], (Y,) + w_up.shape), "fsdp", Y_GROUPS)
    weight = weight.reshape(quarter, units)
    hidden_grad = (grad_act.astype(jnp.float32) * gelu_slope(pre_act.astype(jnp.float32))).astype(
        jnp.bfloat16
    )
    hidden = jnp.stack([hidden_grad] + [along_z_lo(hidden_grad, k) for k in range(1, Z_LO)])
    mine = lax.dynamic_slice_in_dim(tokens, core * (rows // CORE), rows // CORE, 0)
    mine = [
        lax.dynamic_slice_in_dim(mine, ((z_lo + k) % Z_LO) * quarter, quarter, 1) for k in range(Z_LO)
    ]
    mine = jnp.stack([mine[0]] + [along_z_lo(mine[k], k) for k in range(1, Z_LO)])
    other = to_other_core(mine)
    patches = jnp.where(
        core == 0, jnp.stack([mine, other], axis=1), jnp.stack([other, mine], axis=1)
    ).reshape(Z_LO * rows, quarter)
    hidden = hidden.reshape(Z_LO * rows, units)

    weight_part = lax.dot_general(
        patches, hidden, (((0,), (0,)), ((), ())), preferred_element_type=jnp.float32
    ).astype(jnp.bfloat16)
    received = swap(weight_part.reshape(Y, quarter // Y, units), "fsdp", Y_GROUPS)
    grad_weight = (jnp.sum(received.astype(jnp.float32), axis=0) * norm_factor).astype(jnp.bfloat16)

    def partial_of(which):
        chosen = lax.dynamic_slice_in_dim(weight, which * half, half, 0)
        return lax.dot_general(
            hidden, chosen, (((1,), (1,)), ((), ())), preferred_element_type=jnp.float32
        ).astype(jnp.bfloat16)

    theirs = to_other_core(partial_of(1 - core))
    partial = total([partial_of(core), theirs])
    piece = rows // X
    partial = partial.reshape(Z_LO, X, piece, half)
    pieces = [
        lax.dynamic_slice_in_dim(partial, (x + j) % X, 1, 1).reshape(Z_LO, piece, half) for j in range(X)
    ]
    partial = total([pieces[0]] + [along_x(pieces[j], j) for j in range(1, X)])
    ring = [partial[0]] + [along_ring(partial[-m % Z_LO], m) for m in range(1, Z_HI * Z_LO)]
    ring = jnp.stack([total([ring[m], ring[m + Z_LO]]) for m in range(Z_LO)])
    ring = canonical(ring, z_lo, 0).transpose(1, 0, 2).reshape(piece, Z_LO * half)
    gathered = jnp.stack([ring] + [along_x(ring, j) for j in range(1, X)])
    theirs = to_other_core(gathered)
    gathered = canonical(gathered, x, 0).reshape(rows, Z_LO, half)
    theirs = canonical(theirs, x, 0).reshape(rows, Z_LO, half)
    grad_input = jnp.where(
        core == 0, jnp.stack([gathered, theirs], axis=2), jnp.stack([theirs, gathered], axis=2)
    ).reshape(rows, width)
    return (grad_weight, grad_input)


def solution(mesh):
    placed = (P("fsdp", None), P("fsdp", "mp"), P("fsdp", "mp"), P("fsdp", "mp"))
    return jax.shard_map(
        shards,
        mesh=mesh,
        in_specs=placed,
        out_specs=(P("fsdp", "mp"), P("fsdp", None)),
        check_vma=False,
    )
```

time: 195 us -> 150 us (0.77)
  starting transfers between devices: 18.9 us -> 94.4 us
  blocking collectives: 64.6 us -> 0 us
  waiting for transfers between devices: 85.5 us -> 32.2 us
  between operations: 14.1 us -> 1.42 us
  local copies, waits for them, and re-layouts: 4.05 us -> 8.77 us
  other arithmetic: 2.71 us -> 7.35 us
    ppermute x0 -> x22, starting transfers between devices: none -> 80.1 us  [moved(): return lax.ppermute(value, AXES, pairs)]
    all_to_all x4 -> x2, waiting for transfers between devices: 76.9 us -> 0.01 us  [swap(): lax.all_to_all(blocks, axis, 0, 0, axis_index_groups=groups, tiled=True)]
    all_to_all x3 -> x0, blocking collectives: 53.9 us -> none  [swap(): lax.all_to_all(blocks, axis, 0, 0, axis_index_groups=groups, tiled=True)]
    ppermute x0 -> x22, waiting for transfers between devices: none -> 32.2 us  [moved(): return lax.ppermute(value, AXES, pairs)]
    all_gather x1 -> x0, blocking collectives: 10.7 us -> none  [shards(): lax.all_gather(mine, 'mp', axis=0, axis_index_groups=X_GROUPS, tiled=True)]
    all_gather x1 -> x0, waiting for transfers between devices: 7.87 us -> none  [shards(): lax.all_gather(w_up, 'fsdp', axis=0, axis_index_groups=Y_GROUPS, tiled=True)]
    all_to_all x4 -> x2, starting transfers between devices: 18.9 us -> 14.3 us  [swap(): lax.all_to_all(blocks, axis, 0, 0, axis_index_groups=groups, tiled=True)]
    select_n x0 -> x2, local copies, waits for them, and re-layouts: none -> 3.52 us  [shards(): jnp.where(core == 0, jnp.stack([gathered, theirs], axis=2), jnp.stack([th...]
  transfers between devices with their start and end apart: 5 -> 24, of which waited for: 5 -> 6; matrix products, arithmetic and copies ran while one was open for 3% -> 8% of each run, Pallas kernels for 0% -> 0%
where the time goes in v2:
time: 150 us; the launch traced here: 149 us
  starting transfers between devices  94.4 us (63%)
  waiting for transfers between devices  32.2 us (21%)
  local copies, waits for them, and re-layouts  8.77 us (6%)
  other arithmetic  7.35 us (5%)
  matrix products  4.57 us (3%)
    ppermute x22, starting transfers between devices, moved(): return lax.ppermute(value, AXES, pairs)  80.1 us
    ppermute x22, waiting for transfers between devices, moved(): return lax.ppermute(value, AXES, pairs)  32.2 us
    all_to_all x2, starting transfers between devices, swap(): lax.all_to_all(blocks, axis, 0, 0, axis_index_groups=groups, tiled=True)  14.3 us
    select_n x2, local copies, waits for them, and re-layouts, shards(): jnp.where(core == 0, jnp.stack([gathered, theirs], axis=2), jnp.stack([th...  3.52 us
  transfers between devices with their start and end apart: 24, of which 6 were waited for; matrix products, arithmetic and copies ran while one was open for 8% of the time, Pallas kernels for 0%

profile of v2, /device:TPU:1, one launch (start us, length us, event | category | flops | bytes accessed | tf_op | source)
XLA Modules:
  0.0 148.7 jit_solution(6560255382207585945)
XLA Ops:
  0.6 2.0 %broadcast_in_dim.2 = bf16[8,96,768]{2,1,0:T(8,128)(2,1)} broadcast(bf16[96,768]{1,0:T(8,128)(2,1)} %param.7), dimensions={1,2} | broadcast | bytes 1327104 | tf_op jit(solution)/shard_map/broadcast_in_dim | solution.py:94
  2.6 7.8 %all-to-all-start.1 = ((bf16[8,96,768]{2,1,0:T(8,128)(2,1)}), bf16[8,96,768]{2,1,0:T(8,128)(2,1)S(1)}, u32[]{:S(2)}, u32[]{:S(2)}) async-start(bf16[8,96,768]{2,1,0:T(8,128)(2,1)} %broadcast_in_dim.2), calls=%async_computation.1 | async-start | bytes 2359296 | tf_op jit(solution)/shard_map/all_to_all | solution.py:68
  10.6 1.1 dynamic-slice_bitcast_fusion.3
  11.6 7.6 %collective-permute-start.2 = (bf16[96,768]{1,0:T(8,128)(2,1)S(1)}, bf16[96,768]{1,0:T(8,128)(2,1)S(1)}, u32[]{:S(2)}, u32[]{:S(2)}) collective-permute-start(bf16[96,768]{1,0:T(8,128)(2,1)S(1)} %get-tuple-element.4), channel_id=1, source_target_pairs={{0,384},{1,385},{2,386},{3,387},{4,388},{5,389},{6,390},{7,391},{8... | collective-permute-start | bytes 442376 | tf_op jit(solution)/shard_map/ppermute | solution.py:35
  19.3 0.4 fusion.12
  19.7 1.9 %collective-permute-start.6 = (bf16[192,768]{1,0:T(8,128)(2,1)S(1)}, bf16[192,768]{1,0:T(8,128)(2,1)S(1)}, u32[]{:S(2)}, u32[]{:S(2)}) collective-permute-start(bf16[192,768]{1,0:T(8,128)(2,1)S(1)} %fusion.12), channel_id=1, source_target_pairs={{0,384},{1,385},{2,386},{3,387},{4,388},{5,389},{6,390},{7,391},{8... | collective-permute-start | bytes 884744 | tf_op jit(solution)/shard_map/ppermute | solution.py:35
  21.6 1.9 %collective-permute-start.5 = (bf16[192,768]{1,0:T(8,128)(2,1)S(1)}, bf16[192,768]{1,0:T(8,128)(2,1)S(1)}, u32[]{:S(2)}, u32[]{:S(2)}) collective-permute-start(bf16[192,768]{1,0:T(8,128)(2,1)S(1)} %fusion.12), channel_id=1, source_target_pairs={{0,256},{1,257},{2,258},{3,259},{4,260},{5,261},{6,262},{7,263},{8... | collective-permute-start | bytes 884744 | tf_op jit(solution)/shard_map/ppermute | solution.py:35
  23.5 3.4 %collective-permute-start.4 = (bf16[192,768]{1,0:T(8,128)(2,1)S(1)}, bf16[192,768]{1,0:T(8,128)(2,1)S(1)}, u32[]{:S(2)}, u32[]{:S(2)}) collective-permute-start(bf16[192,768]{1,0:T(8,128)(2,1)S(1)} %fusion.12), channel_id=1, source_target_pairs={{0,128},{1,129},{2,130},{3,131},{4,132},{5,133},{6,134},{7,135},{8... | collective-permute-start | bytes 884744 | tf_op jit(solution)/shard_map/ppermute | solution.py:35
  26.9 4.3 %collective-permute-start.1 = (bf16[96,768]{1,0:T(8,128)(2,1)}, bf16[96,768]{1,0:T(8,128)(2,1)S(1)}, u32[]{:S(2)}, u32[]{:S(2)}) collective-permute-start(bf16[96,768]{1,0:T(8,128)(2,1)} %get-tuple-element.5), channel_id=1, source_target_pairs={{0,256},{1,257},{2,258},{3,259},{4,260},{5,261},{6,262},{7,263},{8... | collective-permute-start | bytes 442376 | tf_op jit(solution)/shard_map/ppermute | solution.py:35
  31.2 1.9 %collective-permute-start = (bf16[96,768]{1,0:T(8,128)(2,1)}, bf16[96,768]{1,0:T(8,128)(2,1)S(1)}, u32[]{:S(2)}, u32[]{:S(2)}) collective-permute-start(bf16[96,768]{1,0:T(8,128)(2,1)} %get-tuple-element.3), channel_id=1, source_target_pairs={{0,128},{1,129},{2,130},{3,131},{4,132},{5,133},{6,134},{7,135},{8... | collective-permute-start | bytes 442376 | tf_op jit(solution)/shard_map/ppermute | solution.py:35
  33.1 22.5 %collective-permute-done.1 = bf16[96,768]{1,0:T(8,128)(2,1)S(1)} collective-permute-done((bf16[96,768]{1,0:T(8,128)(2,1)}, bf16[96,768]{1,0:T(8,128)(2,1)S(1)}, u32[]{:S(2)}, u32[]{:S(2)}) %collective-permute-start.1) | collective-permute-done | bytes 147488 | tf_op jit(solution)/shard_map/ppermute | solution.py:35
  55.6 0.9 fusion.28
  56.5 3.3 %collective-permute-start.3 = (bf16[4,96,768]{2,1,0:T(8,128)(2,1)}, bf16[4,96,768]{2,1,0:T(8,128)(2,1)}, u32[]{:S(2)}, u32[]{:S(2)}) collective-permute-start(bf16[4,96,768]{2,1,0:T(8,128)(2,1)} %get-tuple-element.10), channel_id=1, source_target_pairs={{0,1},{1,0},{2,3},{3,2},{4,5},{5,4},{6,7},{7,6},{8,9},{9,8},{10,11... | collective-permute-start | bytes 1769480 | tf_op jit(solution)/shard_map/ppermute | solution.py:35
  59.9 0.7 copy-done.1
  60.6 1.2 pad_maximum_fusion
  61.9 1.6 %convolution_convert_fusion.1 = bf16[768,384]{1,0:T(8,128)(2,1)} fusion(bf16[768,768]{1,0:T(8,128)(2,1)S(1)} %bitcast.62, bf16[768,768]{1,0:T(8,128)(2,1)S(1)} %bitcast.60, s32[]{:T(128)S(6)} %select_n.157), kind=kOutput, calls=%fused_computation.9 | convolution fusion | flops 453279744 | bytes 2359300 | tf_op jit(solution)/shard_map/dot_general | solution.py:119
  63.5 1.9 %collective-permute-start.7 = (bf16[768,384]{1,0:T(8,128)(2,1)}, bf16[768,384]{1,0:T(8,128)(2,1)S(1)}, u32[]{:S(2)}, u32[]{:S(2)}) collective-permute-start(bf16[768,384]{1,0:T(8,128)(2,1)} %convolution_convert_fusion.1), channel_id=1, source_target_pairs={{0,1},{1,0},{2,3},{3,2},{4,5},{5,4},{6,7},{7,6},{8,9},{9,8},{10,11... | collective-permute-start | bytes 1769480 | tf_op jit(solution)/shard_map/ppermute | solution.py:35
  65.5 1.4 maximum_select_fusion
  66.9 0.7 collective-permute-done.7
  67.6 0.8 fusion.2
  68.4 0.8 copy-done
  69.3 4.4 %collective-permute-start.10 = (bf16[4,48,384]{2,1,0:T(8,128)(2,1)S(1)}, bf16[4,48,384]{2,1,0:T(8,128)(2,1)S(1)}, u32[]{:S(2)}, u32[]{:S(2)}) collective-permute-start(bf16[4,48,384]{2,1,0:T(8,128)(2,1)S(1)} %get-tuple-element.7), channel_id=1, source_target_pairs={{0,12},{1,13},{2,14},{3,15},{4,0},{5,1},{6,2},{7,3},{8,4},{9,5},{1... | collective-permute-start | bytes 442376 | tf_op jit(solution)/shard_map/ppermute | solution.py:35
  73.7 2.4 %collective-permute-start.9 = (bf16[4,48,384]{2,1,0:T(8,128)(2,1)S(1)}, bf16[4,48,384]{2,1,0:T(8,128)(2,1)S(1)}, u32[]{:S(2)}, u32[]{:S(2)}) collective-permute-start(bf16[4,48,384]{2,1,0:T(8,128)(2,1)S(1)} %get-tuple-element.8), channel_id=1, source_target_pairs={{0,8},{1,9},{2,10},{3,11},{4,12},{5,13},{6,14},{7,15},{8,0},{9,1},... | collective-permute-start | bytes 442376 | tf_op jit(solution)/shard_map/ppermute | solution.py:35
  76.1 2.5 %collective-permute-start.8 = (bf16[4,48,384]{2,1,0:T(8,128)(2,1)S(1)}, bf16[4,48,384]{2,1,0:T(8,128)(2,1)S(1)}, u32[]{:S(2)}, u32[]{:S(2)}) collective-permute-start(bf16[4,48,384]{2,1,0:T(8,128)(2,1)S(1)} %get-tuple-element.6), channel_id=1, source_target_pairs={{0,4},{1,5},{2,6},{3,7},{4,8},{5,9},{6,10},{7,11},{8,12},{9,13},{1... | collective-permute-start | bytes 442376 | tf_op jit(solution)/shard_map/ppermute | solution.py:35
  78.6 2.1 %convolution_convert_fusion = bf16[768,768]{1,0:T(8,128)(2,1)} fusion(bf16[768,768]{1,0:T(8,128)(2,1)S(1)} %bitcast.59, bf16[768,768]{1,0:T(8,128)(2,1)S(1)} %bitcast.64), kind=kOutput, calls=%fused_computation.1 | convolution fusion | flops 906559488 | bytes 3538944 | tf_op jit(solution)/shard_map/dot_general | solution.py:111
  80.8 6.5 %all-to-all-start = ((bf16[8,96,768]{2,1,0:T(8,128)(2,1)}), bf16[8,96,768]{2,1,0:T(8,128)(2,1)S(1)}, u32[]{:S(2)}, u32[]{:S(2)}) async-start(bf16[8,96,768]{2,1,0:T(8,128)(2,1)} %bitcast.12), calls=%async_computation | async-start | bytes 2359296 | tf_op jit(solution)/shard_map/all_to_all | solution.py:68
  87.3 1.0 fusion.18
  88.3 9.2 %collective-permute-start.11 = (bf16[48,384]{1,0:T(8,128)(2,1)S(1)}, bf16[48,384]{1,0:T(8,128)(2,1)S(1)}, u32[]{:S(2)}, u32[]{:S(2)}) collective-permute-start(bf16[48,384]{1,0:T(8,128)(2,1)S(1)} %get-tuple-element.13), channel_id=1, source_target_pairs={{0,2},{1,3},{2,0},{3,1},{4,6},{5,7},{6,4},{7,5},{8,10},{9,11},{10,... | collective-permute-start | bytes 110600 | tf_op jit(solution)/shard_map/ppermute | solution.py:35
  97.6 1.9 %collective-permute-start.17 = (bf16[48,384]{1,0:T(8,128)(2,1)S(1)}, bf16[48,384]{1,0:T(8,128)(2,1)S(1)}, u32[]{:S(2)}, u32[]{:S(2)}) collective-permute-start(bf16[48,384]{1,0:T(8,128)(2,1)S(1)} %get-tuple-element.14), channel_id=1, source_target_pairs={{0,386},{1,387},{2,384},{3,385},{4,390},{5,391},{6,388},{7,389},{8... | collective-permute-start | bytes 110600 | tf_op jit(solution)/shard_map/ppermute | solution.py:35
  99.5 6.1 %collective-permute-start.16 = (bf16[48,384]{1,0:T(8,128)(2,1)S(1)}, bf16[48,384]{1,0:T(8,128)(2,1)S(1)}, u32[]{:S(2)}, u32[]{:S(2)}) collective-permute-start(bf16[48,384]{1,0:T(8,128)(2,1)S(1)} %get-tuple-element.14), channel_id=1, source_target_pairs={{0,384},{1,385},{2,386},{3,387},{4,388},{5,389},{6,390},{7,391},{8... | collective-permute-start | bytes 110600 | tf_op jit(solution)/shard_map/ppermute | solution.py:35
  105.6 2.4 %collective-permute-start.15 = (bf16[48,384]{1,0:T(8,128)(2,1)S(1)}, bf16[48,384]{1,0:T(8,128)(2,1)S(1)}, u32[]{:S(2)}, u32[]{:S(2)}) collective-permute-start(bf16[48,384]{1,0:T(8,128)(2,1)S(1)} %get-tuple-element.15), channel_id=1, source_target_pairs={{0,258},{1,259},{2,256},{3,257},{4,262},{5,263},{6,260},{7,261},{8... | collective-permute-start | bytes 110600 | tf_op jit(solution)/shard_map/ppermute | solution.py:35
  108.1 3.7 %collective-permute-start.14 = (bf16[48,384]{1,0:T(8,128)(2,1)S(1)}, bf16[48,384]{1,0:T(8,128)(2,1)S(1)}, u32[]{:S(2)}, u32[]{:S(2)}) collective-permute-start(bf16[48,384]{1,0:T(8,128)(2,1)S(1)} %get-tuple-element.15), channel_id=1, source_target_pairs={{0,256},{1,257},{2,258},{3,259},{4,260},{5,261},{6,262},{7,263},{8... | collective-permute-start | bytes 110600 | tf_op jit(solution)/shard_map/ppermute | solution.py:35
  111.8 2.9 %collective-permute-start.13 = (bf16[48,384]{1,0:T(8,128)(2,1)S(1)}, bf16[48,384]{1,0:T(8,128)(2,1)S(1)}, u32[]{:S(2)}, u32[]{:S(2)}) collective-permute-start(bf16[48,384]{1,0:T(8,128)(2,1)S(1)} %get-tuple-element.16), channel_id=1, source_target_pairs={{0,130},{1,131},{2,128},{3,129},{4,134},{5,135},{6,132},{7,133},{8... | collective-permute-start | bytes 110600 | tf_op jit(solution)/shard_map/ppermute | solution.py:35
  114.7 3.9 %collective-permute-start.12 = (bf16[48,384]{1,0:T(8,128)(2,1)S(1)}, bf16[48,384]{1,0:T(8,128)(2,1)S(1)}, u32[]{:S(2)}, u32[]{:S(2)}) collective-permute-start(bf16[48,384]{1,0:T(8,128)(2,1)S(1)} %get-tuple-element.16), channel_id=1, source_target_pairs={{0,128},{1,129},{2,130},{3,131},{4,132},{5,133},{6,134},{7,135},{8... | collective-permute-start | bytes 110600 | tf_op jit(solution)/shard_map/ppermute | solution.py:35
  118.7 1.9 %collective-permute-done.12 = bf16[48,384]{1,0:T(8,128)(2,1)S(1)} collective-permute-done((bf16[48,384]{1,0:T(8,128)(2,1)S(1)}, bf16[48,384]{1,0:T(8,128)(2,1)S(1)}, u32[]{:S(2)}, u32[]{:S(2)}) %collective-permute-start.12) | collective-permute-done | bytes 36896 | tf_op jit(solution)/shard_map/ppermute | solution.py:35
  120.8 4.0 %collective-permute-start.20 = (bf16[48,1536]{1,0:T(8,128)(2,1)S(1)}, bf16[48,1536]{1,0:T(8,128)(2,1)S(1)}, u32[]{:S(2)}, u32[]{:S(2)}) collective-permute-start(bf16[48,1536]{1,0:T(8,128)(2,1)S(1)} %bitcast.76), channel_id=1, source_target_pairs={{0,12},{1,13},{2,14},{3,15},{4,0},{5,1},{6,2},{7,3},{8,4},{9,5},{1... | collective-permute-start | bytes 442376 | tf_op jit(solution)/shard_map/ppermute | solution.py:35
  124.8 3.2 %collective-permute-start.19 = (bf16[48,1536]{1,0:T(8,128)(2,1)S(1)}, bf16[48,1536]{1,0:T(8,128)(2,1)S(1)}, u32[]{:S(2)}, u32[]{:S(2)}) collective-permute-start(bf16[48,1536]{1,0:T(8,128)(2,1)S(1)} %bitcast.77), channel_id=1, source_target_pairs={{0,8},{1,9},{2,10},{3,11},{4,12},{5,13},{6,14},{7,15},{8,0},{9,1},... | collective-permute-start | bytes 442376 | tf_op jit(solution)/shard_map/ppermute | solution.py:35
  128.0 1.9 %collective-permute-start.18 = (bf16[48,1536]{1,0:T(8,128)(2,1)S(1)}, bf16[48,1536]{1,0:T(8,128)(2,1)S(1)}, u32[]{:S(2)}, u32[]{:S(2)}) collective-permute-start(bf16[48,1536]{1,0:T(8,128)(2,1)S(1)} %bitcast.78), channel_id=1, source_target_pairs={{0,4},{1,5},{2,6},{3,7},{4,8},{5,9},{6,10},{7,11},{8,12},{9,13},{1... | collective-permute-start | bytes 442376 | tf_op jit(solution)/shard_map/ppermute | solution.py:35
  130.1 2.1 %collective-permute-done.19 = bf16[48,1536]{1,0:T(8,128)(2,1)S(1)} collective-permute-done((bf16[48,1536]{1,0:T(8,128)(2,1)S(1)}, bf16[48,1536]{1,0:T(8,128)(2,1)S(1)}, u32[]{:S(2)}, u32[]{:S(2)}) %collective-permute-start.19) | collective-permute-done | bytes 147488 | tf_op jit(solution)/shard_map/ppermute | solution.py:35
  132.2 4.6 %collective-permute-done.18 = bf16[48,1536]{1,0:T(8,128)(2,1)S(1)} collective-permute-done((bf16[48,1536]{1,0:T(8,128)(2,1)S(1)}, bf16[48,1536]{1,0:T(8,128)(2,1)S(1)}, u32[]{:S(2)}, u32[]{:S(2)}) %collective-permute-start.18) | collective-permute-done | bytes 147488 | tf_op jit(solution)/shard_map/ppermute | solution.py:35
  136.9 5.4 %collective-permute-start.21 = (bf16[4,48,1536]{2,1,0:T(8,128)(2,1)S(1)}, bf16[4,48,1536]{2,1,0:T(8,128)(2,1)S(1)}, u32[]{:S(2)}, u32[]{:S(2)}) collective-permute-start(bf16[4,48,1536]{2,1,0:T(8,128)(2,1)S(1)} %pad_maximum_fusion.2), channel_id=1, source_target_pairs={{0,1},{1,0},{2,3},{3,2},{4,5},{5,4},{6,7},{7,6},{8,9},{9,8},{10,11... | collective-permute-start | bytes 1769480 | tf_op jit(solution)/shard_map/ppermute | solution.py:35
  142.5 0.7 multiply_convert_fusion
  143.2 0.2 fusion.4
  143.6 0.3 collective-permute-done.21
  144.0 0.2 fusion.3
  144.3 0.9 maximum_select_fusion.1
  145.2 1.8 %copy.13 = bf16[192,4,2,384]{3,2,1,0:T(2,128)(2,1)S(1)} copy(bf16[192,4,2,384]{3,1,0,2:T(4,128)(2,1)S(1)} %maximum_select_fusion.1) | data formatting | bytes 2359296 | tf_op jit(solution)/shard_map/jit(_where)/select_n | solution.py:138
  147.0 1.7 %select_n.172 = bf16[192,3072]{1,0:T(8,128)(2,1)} reshape(bf16[192,4,2,384]{3,2,1,0:T(2,128)(2,1)S(1)} %copy.13) | data formatting | bytes 2359296 | tf_op jit(solution)/shard_map/jit(_where)/select_n | solution.py:138
  (46 shorter events, 1.1 us)
Async XLA Ops:
  2.6 7.9 %copy-start.5 = (bf16[192,3072]{1,0:T(8,128)(2,1)S(1)}, bf16[192,3072]{1,0:T(8,128)(2,1)}, u32[]{:S(2)}) copy-start(bf16[192,3072]{1,0:T(8,128)(2,1)} %param.4) | copy-start | bytes 3538948
  2.6 59.2 %all-to-all-start.1 = ((bf16[8,96,768]{2,1,0:T(8,128)(2,1)}), bf16[8,96,768]{2,1,0:T(8,128)(2,1)S(1)}, u32[]{:S(2)}, u32[]{:S(2)}) async-start(bf16[8,96,768]{2,1,0:T(8,128)(2,1)} %broadcast_in_dim.2), calls=%async_computation.1 | async-start | bytes 2359296 | tf_op jit(solution)/shard_map/all_to_all | solution.py:68
  10.4 8.8 %copy-start.3 = (bf16[192,768]{1,0:T(8,128)(2,1)S(1)}, bf16[192,768]{1,0:T(8,128)(2,1)}, u32[]{:S(2)}) copy-start(bf16[192,768]{1,0:T(8,128)(2,1)} %param.5) | copy-start | bytes 884740
  10.4 8.8 %copy-start.4 = (bf16[192,768]{1,0:T(8,128)(2,1)S(1)}, bf16[192,768]{1,0:T(8,128)(2,1)}, u32[]{:S(2)}) copy-start(bf16[192,768]{1,0:T(8,128)(2,1)} %param.6) | copy-start | bytes 884740
  11.6 19.6 %collective-permute-start.2 = (bf16[96,768]{1,0:T(8,128)(2,1)S(1)}, bf16[96,768]{1,0:T(8,128)(2,1)S(1)}, u32[]{:S(2)}, u32[]{:S(2)}) collective-permute-start(bf16[96,768]{1,0:T(8,128)(2,1)S(1)} %get-tuple-element.4), channel_id=1, source_target_pairs={{0,384},{1,385},{2,386},{3,387},{4,388},{5,389},{6,390},{7,391},{8... | collective-permute-start | bytes 442376 | tf_op jit(solution)/shard_map/ppermute | solution.py:35
  19.7 40.1 %collective-permute-start.6 = (bf16[192,768]{1,0:T(8,128)(2,1)S(1)}, bf16[192,768]{1,0:T(8,128)(2,1)S(1)}, u32[]{:S(2)}, u32[]{:S(2)}) collective-permute-start(bf16[192,768]{1,0:T(8,128)(2,1)S(1)} %fusion.12), channel_id=1, source_target_pairs={{0,384},{1,385},{2,386},{3,387},{4,388},{5,389},{6,390},{7,391},{8... | collective-permute-start | bytes 884744 | tf_op jit(solution)/shard_map/ppermute | solution.py:35
  21.6 38.2 %collective-permute-start.5 = (bf16[192,768]{1,0:T(8,128)(2,1)S(1)}, bf16[192,768]{1,0:T(8,128)(2,1)S(1)}, u32[]{:S(2)}, u32[]{:S(2)}) collective-permute-start(bf16[192,768]{1,0:T(8,128)(2,1)S(1)} %fusion.12), channel_id=1, source_target_pairs={{0,256},{1,257},{2,258},{3,259},{4,260},{5,261},{6,262},{7,263},{8... | collective-permute-start | bytes 884744 | tf_op jit(solution)/shard_map/ppermute | solution.py:35
  23.5 36.3 %collective-permute-start.4 = (bf16[192,768]{1,0:T(8,128)(2,1)S(1)}, bf16[192,768]{1,0:T(8,128)(2,1)S(1)}, u32[]{:S(2)}, u32[]{:S(2)}) collective-permute-start(bf16[192,768]{1,0:T(8,128)(2,1)S(1)} %fusion.12), channel_id=1, source_target_pairs={{0,128},{1,129},{2,130},{3,131},{4,132},{5,133},{6,134},{7,135},{8... | collective-permute-start | bytes 884744 | tf_op jit(solution)/shard_map/ppermute | solution.py:35
  26.9 28.7 %collective-permute-start.1 = (bf16[96,768]{1,0:T(8,128)(2,1)}, bf16[96,768]{1,0:T(8,128)(2,1)S(1)}, u32[]{:S(2)}, u32[]{:S(2)}) collective-permute-start(bf16[96,768]{1,0:T(8,128)(2,1)} %get-tuple-element.5), channel_id=1, source_target_pairs={{0,256},{1,257},{2,258},{3,259},{4,260},{5,261},{6,262},{7,263},{8... | collective-permute-start | bytes 442376 | tf_op jit(solution)/shard_map/ppermute | solution.py:35
  31.2 24.4 %collective-permute-start = (bf16[96,768]{1,0:T(8,128)(2,1)}, bf16[96,768]{1,0:T(8,128)(2,1)S(1)}, u32[]{:S(2)}, u32[]{:S(2)}) collective-permute-start(bf16[96,768]{1,0:T(8,128)(2,1)} %get-tuple-element.3), channel_id=1, source_target_pairs={{0,128},{1,129},{2,130},{3,131},{4,132},{5,133},{6,134},{7,135},{8... | collective-permute-start | bytes 442376 | tf_op jit(solution)/shard_map/ppermute | solution.py:35
  56.5 8.9 %collective-permute-start.3 = (bf16[4,96,768]{2,1,0:T(8,128)(2,1)}, bf16[4,96,768]{2,1,0:T(8,128)(2,1)}, u32[]{:S(2)}, u32[]{:S(2)}) collective-permute-start(bf16[4,96,768]{2,1,0:T(8,128)(2,1)} %get-tuple-element.10), channel_id=1, source_target_pairs={{0,1},{1,0},{2,3},{3,2},{4,5},{5,4},{6,7},{7,6},{8,9},{9,8},{10,11... | collective-permute-start | bytes 1769480 | tf_op jit(solution)/shard_map/ppermute | solution.py:35
  59.8 0.7 copy-start.1
  59.9 0.8 copy-start.2
  63.5 4.1 %collective-permute-start.7 = (bf16[768,384]{1,0:T(8,128)(2,1)}, bf16[768,384]{1,0:T(8,128)(2,1)S(1)}, u32[]{:S(2)}, u32[]{:S(2)}) collective-permute-start(bf16[768,384]{1,0:T(8,128)(2,1)} %convolution_convert_fusion.1), channel_id=1, source_target_pairs={{0,1},{1,0},{2,3},{3,2},{4,5},{5,4},{6,7},{7,6},{8,9},{9,8},{10,11... | collective-permute-start | bytes 1769480 | tf_op jit(solution)/shard_map/ppermute | solution.py:35
  68.4 0.8 copy-start
  69.3 18.0 %collective-permute-start.10 = (bf16[4,48,384]{2,1,0:T(8,128)(2,1)S(1)}, bf16[4,48,384]{2,1,0:T(8,128)(2,1)S(1)}, u32[]{:S(2)}, u32[]{:S(2)}) collective-permute-start(bf16[4,48,384]{2,1,0:T(8,128)(2,1)S(1)} %get-tuple-element.7), channel_id=1, source_target_pairs={{0,12},{1,13},{2,14},{3,15},{4,0},{5,1},{6,2},{7,3},{8,4},{9,5},{1... | collective-permute-start | bytes 442376 | tf_op jit(solution)/shard_map/ppermute | solution.py:35
  73.7 13.6 %collective-permute-start.9 = (bf16[4,48,384]{2,1,0:T(8,128)(2,1)S(1)}, bf16[4,48,384]{2,1,0:T(8,128)(2,1)S(1)}, u32[]{:S(2)}, u32[]{:S(2)}) collective-permute-start(bf16[4,48,384]{2,1,0:T(8,128)(2,1)S(1)} %get-tuple-element.8), channel_id=1, source_target_pairs={{0,8},{1,9},{2,10},{3,11},{4,12},{5,13},{6,14},{7,15},{8,0},{9,1},... | collective-permute-start | bytes 442376 | tf_op jit(solution)/shard_map/ppermute | solution.py:35
  76.1 11.2 %collective-permute-start.8 = (bf16[4,48,384]{2,1,0:T(8,128)(2,1)S(1)}, bf16[4,48,384]{2,1,0:T(8,128)(2,1)S(1)}, u32[]{:S(2)}, u32[]{:S(2)}) collective-permute-start(bf16[4,48,384]{2,1,0:T(8,128)(2,1)S(1)} %get-tuple-element.6), channel_id=1, source_target_pairs={{0,4},{1,5},{2,6},{3,7},{4,8},{5,9},{6,10},{7,11},{8,12},{9,13},{1... | collective-permute-start | bytes 442376 | tf_op jit(solution)/shard_map/ppermute | solution.py:35
  80.8 61.6 %all-to-all-start = ((bf16[8,96,768]{2,1,0:T(8,128)(2,1)}), bf16[8,96,768]{2,1,0:T(8,128)(2,1)S(1)}, u32[]{:S(2)}, u32[]{:S(2)}) async-start(bf16[8,96,768]{2,1,0:T(8,128)(2,1)} %bitcast.12), calls=%async_computation | async-start | bytes 2359296 | tf_op jit(solution)/shard_map/all_to_all | solution.py:68
  88.3 23.5 %collective-permute-start.11 = (bf16[48,384]{1,0:T(8,128)(2,1)S(1)}, bf16[48,384]{1,0:T(8,128)(2,1)S(1)}, u32[]{:S(2)}, u32[]{:S(2)}) collective-permute-start(bf16[48,384]{1,0:T(8,128)(2,1)S(1)} %get-tuple-element.13), channel_id=1, source_target_pairs={{0,2},{1,3},{2,0},{3,1},{4,6},{5,7},{6,4},{7,5},{8,10},{9,11},{10,... | collective-permute-start | bytes 110600 | tf_op jit(solution)/shard_map/ppermute | solution.py:35
  97.6 17.1 %collective-permute-start.17 = (bf16[48,384]{1,0:T(8,128)(2,1)S(1)}, bf16[48,384]{1,0:T(8,128)(2,1)S(1)}, u32[]{:S(2)}, u32[]{:S(2)}) collective-permute-start(bf16[48,384]{1,0:T(8,128)(2,1)S(1)} %get-tuple-element.14), channel_id=1, source_target_pairs={{0,386},{1,387},{2,384},{3,385},{4,390},{5,391},{6,388},{7,389},{8... | collective-permute-start | bytes 110600 | tf_op jit(solution)/shard_map/ppermute | solution.py:35
  99.5 19.1 %collective-permute-start.16 = (bf16[48,384]{1,0:T(8,128)(2,1)S(1)}, bf16[48,384]{1,0:T(8,128)(2,1)S(1)}, u32[]{:S(2)}, u32[]{:S(2)}) collective-permute-start(bf16[48,384]{1,0:T(8,128)(2,1)S(1)} %get-tuple-element.14), channel_id=1, source_target_pairs={{0,384},{1,385},{2,386},{3,387},{4,388},{5,389},{6,390},{7,391},{8... | collective-permute-start | bytes 110600 | tf_op jit(solution)/shard_map/ppermute | solution.py:35
  105.6 13.0 %collective-permute-start.15 = (bf16[48,384]{1,0:T(8,128)(2,1)S(1)}, bf16[48,384]{1,0:T(8,128)(2,1)S(1)}, u32[]{:S(2)}, u32[]{:S(2)}) collective-permute-start(bf16[48,384]{1,0:T(8,128)(2,1)S(1)} %get-tuple-element.15), channel_id=1, source_target_pairs={{0,258},{1,259},{2,256},{3,257},{4,262},{5,263},{6,260},{7,261},{8... | collective-permute-start | bytes 110600 | tf_op jit(solution)/shard_map/ppermute | solution.py:35
  108.1 10.6 %collective-permute-start.14 = (bf16[48,384]{1,0:T(8,128)(2,1)S(1)}, bf16[48,384]{1,0:T(8,128)(2,1)S(1)}, u32[]{:S(2)}, u32[]{:S(2)}) collective-permute-start(bf16[48,384]{1,0:T(8,128)(2,1)S(1)} %get-tuple-element.15), channel_id=1, source_target_pairs={{0,256},{1,257},{2,258},{3,259},{4,260},{5,261},{6,262},{7,263},{8... | collective-permute-start | bytes 110600 | tf_op jit(solution)/shard_map/ppermute | solution.py:35
  111.8 6.9 %collective-permute-start.13 = (bf16[48,384]{1,0:T(8,128)(2,1)S(1)}, bf16[48,384]{1,0:T(8,128)(2,1)S(1)}, u32[]{:S(2)}, u32[]{:S(2)}) collective-permute-start(bf16[48,384]{1,0:T(8,128)(2,1)S(1)} %get-tuple-element.16), channel_id=1, source_target_pairs={{0,130},{1,131},{2,128},{3,129},{4,134},{5,135},{6,132},{7,133},{8... | collective-permute-start | bytes 110600 | tf_op jit(solution)/shard_map/ppermute | solution.py:35
  114.7 5.9 %collective-permute-start.12 = (bf16[48,384]{1,0:T(8,128)(2,1)S(1)}, bf16[48,384]{1,0:T(8,128)(2,1)S(1)}, u32[]{:S(2)}, u32[]{:S(2)}) collective-permute-start(bf16[48,384]{1,0:T(8,128)(2,1)S(1)} %get-tuple-element.16), channel_id=1, source_target_pairs={{0,128},{1,129},{2,130},{3,131},{4,132},{5,133},{6,134},{7,135},{8... | collective-permute-start | bytes 110600 | tf_op jit(solution)/shard_map/ppermute | solution.py:35
  120.8 9.2 %collective-permute-start.20 = (bf16[48,1536]{1,0:T(8,128)(2,1)S(1)}, bf16[48,1536]{1,0:T(8,128)(2,1)S(1)}, u32[]{:S(2)}, u32[]{:S(2)}) collective-permute-start(bf16[48,1536]{1,0:T(8,128)(2,1)S(1)} %bitcast.76), channel_id=1, source_target_pairs={{0,12},{1,13},{2,14},{3,15},{4,0},{5,1},{6,2},{7,3},{8,4},{9,5},{1... | collective-permute-start | bytes 442376 | tf_op jit(solution)/shard_map/ppermute | solution.py:35
  124.8 7.4 %collective-permute-start.19 = (bf16[48,1536]{1,0:T(8,128)(2,1)S(1)}, bf16[48,1536]{1,0:T(8,128)(2,1)S(1)}, u32[]{:S(2)}, u32[]{:S(2)}) collective-permute-start(bf16[48,1536]{1,0:T(8,128)(2,1)S(1)} %bitcast.77), channel_id=1, source_target_pairs={{0,8},{1,9},{2,10},{3,11},{4,12},{5,13},{6,14},{7,15},{8,0},{9,1},... | collective-permute-start | bytes 442376 | tf_op jit(solution)/shard_map/ppermute | solution.py:35
  128.0 8.9 %collective-permute-start.18 = (bf16[48,1536]{1,0:T(8,128)(2,1)S(1)}, bf16[48,1536]{1,0:T(8,128)(2,1)S(1)}, u32[]{:S(2)}, u32[]{:S(2)}) collective-permute-start(bf16[48,1536]{1,0:T(8,128)(2,1)S(1)} %bitcast.78), channel_id=1, source_target_pairs={{0,4},{1,5},{2,6},{3,7},{4,8},{5,9},{6,10},{7,11},{8,12},{9,13},{1... | collective-permute-start | bytes 442376 | tf_op jit(solution)/shard_map/ppermute | solution.py:35
  136.9 7.0 %collective-permute-start.21 = (bf16[4,48,1536]{2,1,0:T(8,128)(2,1)S(1)}, bf16[4,48,1536]{2,1,0:T(8,128)(2,1)S(1)}, u32[]{:S(2)}, u32[]{:S(2)}) collective-permute-start(bf16[4,48,1536]{2,1,0:T(8,128)(2,1)S(1)} %pad_maximum_fusion.2), channel_id=1, source_target_pairs={{0,1},{1,0},{2,3},{3,2},{4,5},{5,4},{6,7},{7,6},{8,9},{9,8},{10,11... | collective-permute-start | bytes 1769480 | tf_op jit(solution)/shard_map/ppermute | solution.py:35

commit v3 on v2

--- a/solution.py
+++ b/solution.py
@@ -19,6 +19,13 @@
 
 
 Y_GROUPS = [[fsdp_index(z, y) for y in range(Y)] for z in range(Z_LO)]
+X_GROUPS = [[mp_index(x, h, c) for x in range(X)] for h in range(Z_HI) for c in range(CORE)]
+RING_GROUPS = [
+    [fsdp_index(z, y) * (X * Z_HI * CORE) + mp_index(x, h, c) for h in range(Z_HI) for z in range(Z_LO)]
+    for y in range(Y)
+    for x in range(X)
+    for c in range(CORE)
+]
 
 
 def moved(value, target):
@@ -85,59 +92,64 @@
     rows, width = tokens.shape
     units = pre_act.shape[1]
     quarter = width // Z_LO
-    half = quarter // CORE
     norm_factor = float(rows * Z_LO * Y) ** (-0.5)
     z_lo = lax.axis_index("fsdp") // Y
     x = lax.axis_index("mp") // (Z_HI * CORE)
     core = lax.axis_index("mp") % CORE
 
-    weight = swap(jnp.broadcast_to(w_up[None], (Y,) + w_up.shape), "fsdp", Y_GROUPS)
-    weight = weight.reshape(quarter, units)
+    weight = lax.all_gather(w_up, "fsdp", axis=0, axis_index_groups=Y_GROUPS, tiled=True)
     hidden_grad = (grad_act.astype(jnp.float32) * gelu_slope(pre_act.astype(jnp.float32))).astype(
         jnp.bfloat16
     )
-    hidden = jnp.stack([hidden_grad] + [along_z_lo(hidden_grad, k) for k in range(1, Z_LO)])
-    mine = lax.dynamic_slice_in_dim(tokens, core * (rows // CORE), rows // CORE, 0)
+    hidden = [hidden_grad] + [along_z_lo(hidden_grad, k) for k in range(1, Z_LO)]
+    hidden = jnp.stack(hidden).reshape(Z_LO * rows, units)
+    part = rows // (CORE * X)
+    mine = lax.dynamic_slice_in_dim(tokens, (core * X + x) * part, part, 0)
     mine = [
         lax.dynamic_slice_in_dim(mine, ((z_lo + k) % Z_LO) * quarter, quarter, 1) for k in range(Z_LO)
     ]
     mine = jnp.stack([mine[0]] + [along_z_lo(mine[k], k) for k in range(1, Z_LO)])
+    mine = lax.all_gather(mine, "mp", axis=1, axis_index_groups=X_GROUPS, tiled=True)
     other = to_other_core(mine)
     patches = jnp.where(
         core == 0, jnp.stack([mine, other], axis=1), jnp.stack([other, mine], axis=1)
     ).reshape(Z_LO * rows, quarter)
-    hidden = hidden.reshape(Z_LO * rows, units)
 
     weight_part = lax.dot_general(
         patches, hidden, (((0,), (0,)), ((), ())), preferred_element_type=jnp.float32
     ).astype(jnp.bfloat16)
-    received = swap(weight_part.reshape(Y, quarter // Y, units), "fsdp", Y_GROUPS)
-    grad_weight = (jnp.sum(received.astype(jnp.float32), axis=0) * norm_factor).astype(jnp.bfloat16)
+    received = lax.psum_scatter(
+        weight_part, "fsdp", scatter_dimension=0, axis_index_groups=Y_GROUPS, tiled=True
+    )
+    grad_weight = (received.astype(jnp.float32) * norm_factor).astype(jnp.bfloat16)
+
+    share = rows // CORE
+    piece = share // X
+    by_core = hidden.reshape(Z_LO, CORE, X, piece, units)
 
     def partial_of(which):
-        chosen = lax.dynamic_slice_in_dim(weight, which * half, half, 0)
+        chosen = lax.dynamic_slice_in_dim(by_core, which, 1, 1).transpose(1, 2, 0, 3, 4)
         return lax.dot_general(
-            hidden, chosen, (((1,), (1,)), ((), ())), preferred_element_type=jnp.float32
-        ).astype(jnp.bfloat16)
+            chosen.reshape(Z_LO * share, units),
+            weight,
+            (((1,), (1,)), ((), ())),
+            preferred_element_type=jnp.float32,
+        )
 
-    theirs = to_other_core(partial_of(1 - core))
-    partial = total([partial_of(core), theirs])
-    piece = rows // X
-    partial = partial.reshape(Z_LO, X, piece, half)
-    pieces = [
-        lax.dynamic_slice_in_dim(partial, (x + j) % X, 1, 1).reshape(Z_LO, piece, half) for j in range(X)
-    ]
-    partial = total([pieces[0]] + [along_x(pieces[j], j) for j in range(1, X)])
-    ring = [partial[0]] + [along_ring(partial[-m % Z_LO], m) for m in range(1, Z_HI * Z_LO)]
-    ring = jnp.stack([total([ring[m], ring[m + Z_LO]]) for m in range(Z_LO)])
-    ring = canonical(ring, z_lo, 0).transpose(1, 0, 2).reshape(piece, Z_LO * half)
-    gathered = jnp.stack([ring] + [along_x(ring, j) for j in range(1, X)])
-    theirs = to_other_core(gathered)
-    gathered = canonical(gathered, x, 0).reshape(rows, Z_LO, half)
-    theirs = canonical(theirs, x, 0).reshape(rows, Z_LO, half)
+    theirs = to_other_core(partial_of(1 - core).astype(jnp.bfloat16))
+    partial = (partial_of(core) + theirs.astype(jnp.float32)).astype(jnp.bfloat16)
+    partial = swap(partial.reshape(X, Z_LO, piece, quarter), "mp", X_GROUPS)
+    partial = total([partial[j] for j in range(X)])
+    partial = canonical(partial, z_lo, 0)
+    both = jnp.concatenate([partial, partial], 0)
+    both = swap(both, AXES, RING_GROUPS).reshape(Z_HI, Z_LO, piece, quarter)
+    ring = total([both[0], both[1]])
+    ring = ring.transpose(1, 0, 2).reshape(piece, width)
+    mine = lax.all_gather(ring, "mp", axis=0, axis_index_groups=X_GROUPS, tiled=True)
+    theirs = to_other_core(mine)
     grad_input = jnp.where(
-        core == 0, jnp.stack([gathered, theirs], axis=2), jnp.stack([theirs, gathered], axis=2)
-    ).reshape(rows, width)
+        core == 0, jnp.concatenate([mine, theirs], 0), jnp.concatenate([theirs, mine], 0)
+    )
     return (grad_weight, grad_input)
 
 

time: 150 us -> 127 us (0.85)
  starting transfers between devices: 94.4 us -> 47.1 us
  blocking collectives: 0 us -> 40.5 us
  waiting for transfers between devices: 32.2 us -> 10.8 us
  between operations: 1.42 us -> 14.4 us
  local copies, waits for them, and re-layouts: 8.77 us -> 2.4 us
  other arithmetic: 7.35 us -> 4.96 us
  matrix products: 4.57 us -> 6.39 us
    ppermute x22 -> x9, starting transfers between devices: 80.1 us -> 43 us  [moved(): return lax.ppermute(value, AXES, pairs)]
    ppermute x22 -> x9, waiting for transfers between devices: 32.2 us -> 0.02 us  [moved(): return lax.ppermute(value, AXES, pairs)]
    all_gather x0 -> x2, blocking collectives: none -> 23.2 us  [the longest x1 12 us: shards(): lax.all_gather(mine, 'mp', axis=1, axis_index_groups=X_GROUPS, tiled=True)]
    all_to_all x0 -> x1, blocking collectives: none -> 17.3 us  [swap(): lax.all_to_all(blocks, axis, 0, 0, axis_index_groups=groups, tiled=True)]
    all_to_all x2 -> x1, starting transfers between devices: 14.3 us -> 3.97 us  [swap(): lax.all_to_all(blocks, axis, 0, 0, axis_index_groups=groups, tiled=True)]
    all_to_all x2 -> x1, waiting for transfers between devices: 0.01 us -> 10 us  [swap(): lax.all_to_all(blocks, axis, 0, 0, axis_index_groups=groups, tiled=True)]
    select_n x2 -> x0, local copies, waits for them, and re-layouts: 3.52 us -> none  [shards(): jnp.where(core == 0, jnp.stack([gathered, theirs], axis=2), jnp.stack([th...]
    broadcast_in_dim x1 -> x0, local copies, waits for them, and re-layouts: 2 us -> none  [shards(): jnp.broadcast_to(w_up[None], (Y,) + w_up.shape)]
  transfers between devices with their start and end apart: 24 -> 12, of which waited for: 6 -> 1; matrix products, arithmetic and copies ran while one was open for 8% -> 9% of each run, Pallas kernels for 0% -> 0%
where the time goes in v3:
time: 127 us
  starting transfers between devices  47.1 us (37%)
  blocking collectives  40.5 us (32%)
  between operations  14.4 us (11%)
  waiting for transfers between devices  10.8 us (9%)
  matrix products  6.39 us (5%)
  other arithmetic  4.96 us (4%)
  local copies, waits for them, and re-layouts  2.4 us (2%)
    ppermute x9, starting transfers between devices, moved(): return lax.ppermute(value, AXES, pairs)  43 us
    all_to_all x1, blocking collectives, swap(): lax.all_to_all(blocks, axis, 0, 0, axis_index_groups=groups, tiled=True)  17.3 us
    all_gather x1, blocking collectives, shards(): lax.all_gather(mine, 'mp', axis=1, axis_index_groups=X_GROUPS, tiled=True)  12 us
    all_gather x1, blocking collectives, shards(): lax.all_gather(ring, 'mp', axis=0, axis_index_groups=X_GROUPS, tiled=True)  11.2 us
    all_to_all x1, waiting for transfers between devices, swap(): lax.all_to_all(blocks, axis, 0, 0, axis_index_groups=groups, tiled=True)  10 us
    dot_general x2, matrix products, partial_of(): lax.dot_general(chosen.reshape(Z_LO * share, units), weight, (((1,), (1,)...  4.25 us
    all_to_all x1, starting transfers between devices, swap(): lax.all_to_all(blocks, axis, 0, 0, axis_index_groups=groups, tiled=True)  3.97 us
  transfers between devices with their start and end apart: 12, of which 1 were waited for; matrix products, arithmetic and copies ran while one was open for 9% of the time, Pallas kernels for 0%

profile of v3, /device:TPU:1, one launch (start us, length us, event | category | flops | bytes accessed | tf_op | source)
XLA Modules:
  0.0 126.5 jit_solution(9922839548355947298)
XLA Ops:
  7.2 0.0 all-gather.2.cloned.1.call-start
  7.2 0.7 all-gather.2.cloned.1.call-update
  7.9 0.0 reduce-scatter.2.cloned.1.call-start
  8.1 1.1 dynamic-slice_bitcast_fusion
  9.1 4.8 %collective-permute-start = (bf16[24,768]{1,0:T(8,128)(2,1)S(1)}, bf16[24,768]{1,0:T(8,128)(2,1)S(1)}, u32[]{:S(2)}, u32[]{:S(2)}) collective-permute-start(bf16[24,768]{1,0:T(8,128)(2,1)S(1)} %get-tuple-element.5), channel_id=1, source_target_pairs={{0,128},{1,129},{2,130},{3,131},{4,132},{5,133},{6,134},{7,135},{8... | collective-permute-start | bytes 110600 | tf_op jit(solution)/shard_map/ppermute | solution.py:42
  14.0 5.8 %collective-permute-start.1 = (bf16[24,768]{1,0:T(8,128)(2,1)S(1)}, bf16[24,768]{1,0:T(8,128)(2,1)S(1)}, u32[]{:S(2)}, u32[]{:S(2)}) collective-permute-start(bf16[24,768]{1,0:T(8,128)(2,1)S(1)} %get-tuple-element.7), channel_id=1, source_target_pairs={{0,256},{1,257},{2,258},{3,259},{4,260},{5,261},{6,262},{7,263},{8... | collective-permute-start | bytes 110600 | tf_op jit(solution)/shard_map/ppermute | solution.py:42
  19.8 2.2 %collective-permute-start.2 = (bf16[24,768]{1,0:T(8,128)(2,1)S(1)}, bf16[24,768]{1,0:T(8,128)(2,1)S(1)}, u32[]{:S(2)}, u32[]{:S(2)}) collective-permute-start(bf16[24,768]{1,0:T(8,128)(2,1)S(1)} %get-tuple-element.6), channel_id=1, source_target_pairs={{0,384},{1,385},{2,386},{3,387},{4,388},{5,389},{6,390},{7,391},{8... | collective-permute-start | bytes 110600 | tf_op jit(solution)/shard_map/ppermute | solution.py:42
  22.0 1.5 %fusion.7 = bf16[192,768]{1,0:T(8,128)(2,1)S(1)} fusion(bf16[192,768]{1,0:T(8,128)(2,1)} %param.5, bf16[192,768]{1,0:T(8,128)(2,1)} %param.6), kind=kLoop, calls=%fused_computation.21 | loop fusion | flops 3096576 | bytes 884736 | tf_op jit(solution)/shard_map/convert_element_type | solution.py:101
  23.4 3.1 %collective-permute-start.4 = (bf16[192,768]{1,0:T(8,128)(2,1)S(1)}, bf16[192,768]{1,0:T(8,128)(2,1)S(1)}, u32[]{:S(2)}, u32[]{:S(2)}) collective-permute-start(bf16[192,768]{1,0:T(8,128)(2,1)S(1)} %fusion.7), channel_id=1, source_target_pairs={{0,128},{1,129},{2,130},{3,131},{4,132},{5,133},{6,134},{7,135},{8... | collective-permute-start | bytes 884744 | tf_op jit(solution)/shard_map/ppermute | solution.py:42
  26.6 1.9 %collective-permute-start.5 = (bf16[192,768]{1,0:T(8,128)(2,1)S(1)}, bf16[192,768]{1,0:T(8,128)(2,1)S(1)}, u32[]{:S(2)}, u32[]{:S(2)}) collective-permute-start(bf16[192,768]{1,0:T(8,128)(2,1)S(1)} %fusion.7), channel_id=1, source_target_pairs={{0,256},{1,257},{2,258},{3,259},{4,260},{5,261},{6,262},{7,263},{8... | collective-permute-start | bytes 884744 | tf_op jit(solution)/shard_map/ppermute | solution.py:42
  28.5 0.0 collective-permute-done
  28.5 4.0 %collective-permute-start.6 = (bf16[192,768]{1,0:T(8,128)(2,1)S(1)}, bf16[192,768]{1,0:T(8,128)(2,1)S(1)}, u32[]{:S(2)}, u32[]{:S(2)}) collective-permute-start(bf16[192,768]{1,0:T(8,128)(2,1)S(1)} %fusion.7), channel_id=1, source_target_pairs={{0,384},{1,385},{2,386},{3,387},{4,388},{5,389},{6,390},{7,391},{8... | collective-permute-start | bytes 884744 | tf_op jit(solution)/shard_map/ppermute | solution.py:42
  32.5 0.0 collective-permute-done.1
  32.5 0.0 collective-permute-done.2
  32.6 12.0 %all_gather.9 = bf16[4,96,768]{2,1,0:T(8,128)(2,1)S(1)} all-gather(bf16[4,24,768]{2,1,0:T(8,128)(2,1)S(1)} %pad_maximum_fusion.3), channel_id=1, replica_groups={{0,4,8,12},{1,5,9,13},{2,6,10,14},{3,7,11,15},{16,20,24,28},{17,21,25,2..., dimensions={1}, use_global_device_ids=true | all-gather | bytes 737280 | tf_op jit(solution)/shard_map/all_gather | solution.py:112
  44.5 8.9 %collective-permute-start.3 = (bf16[4,96,768]{2,1,0:T(8,128)(2,1)S(1)}, bf16[4,96,768]{2,1,0:T(8,128)(2,1)S(1)}, u32[]{:S(2)}, u32[]{:S(2)}) collective-permute-start(bf16[4,96,768]{2,1,0:T(8,128)(2,1)S(1)} %all_gather.9), channel_id=1, source_target_pairs={{0,1},{1,0},{2,3},{3,2},{4,5},{5,4},{6,7},{7,6},{8,9},{9,8},{10,11... | collective-permute-start | bytes 1769480 | tf_op jit(solution)/shard_map/ppermute | solution.py:42
  53.4 0.0 collective-permute-done.4
  53.4 0.0 collective-permute-done.5
  53.4 0.0 collective-permute-done.6
  53.5 0.1 pad_maximum_fusion.1
  53.6 0.1 constant_dynamic-slice_fusion
  53.7 0.0 all-gather.2.cloned.1.call-done
  53.7 2.8 %convolution_convert_fusion.1 = bf16[384,768]{1,0:T(8,128)(2,1)} fusion(bf16[384,768]{1,0:T(8,128)(2,1)S(1)} %bitcast.50, bf16[768,768]{1,0:T(8,128)(2,1)} %all-gather.2.cloned.1.call-done), kind=kOutput, calls=%fused_computation.8 | convolution fusion | flops 453279744 | bytes 2359296 | tf_op jit(solution)/shard_map/dot_general | solution.py:132
  56.5 5.6 %collective-permute-start.7 = (bf16[384,768]{1,0:T(8,128)(2,1)}, bf16[384,768]{1,0:T(8,128)(2,1)S(1)}, u32[]{:S(2)}, u32[]{:S(2)}) collective-permute-start(bf16[384,768]{1,0:T(8,128)(2,1)} %convolution_convert_fusion.1), channel_id=1, source_target_pairs={{0,1},{1,0},{2,3},{3,2},{4,5},{5,4},{6,7},{7,6},{8,9},{9,8},{10,11... | collective-permute-start | bytes 1769480 | tf_op jit(solution)/shard_map/ppermute | solution.py:42
  62.1 0.2 pad_maximum_fusion
  62.3 0.0 collective-permute-done.3
  62.3 0.1 maximum_select_fusion
  62.4 2.1 %convolution_convert_fusion = bf16[768,768]{1,0:T(8,128)(2,1)} fusion(bf16[768,768]{1,0:T(8,128)(2,1)S(1)} %bitcast.45, bf16[768,768]{1,0:T(8,128)(2,1)S(1)} %bitcast.46), kind=kOutput, calls=%fused_computation | convolution fusion | flops 906559488 | bytes 3538944 | tf_op jit(solution)/shard_map/dot_general | solution.py:118
  64.5 0.0 copy-start
  64.5 0.0 reduce-scatter.2.cloned.1.call-update
  64.6 0.0 collective-permute-done.7
  64.6 1.2 copy-done
  65.8 1.5 %add_convert_fusion = bf16[384,768]{1,0:T(8,128)(2,1)} fusion(bf16[384,768]{1,0:T(8,128)(2,1)S(1)} %collective-permute-done.7, bf16[384,768]{1,0:T(8,128)(2,1)S(1)} %bitcast.49, bf16[768,768]{1,0:T(8,128)(2,1)S(1)} %copy-done), kind=kOutput, calls=%fused_computation.13 | convolution fusion | flops 453869568 | bytes 2949120 | tf_op jit(solution)/shard_map/dot_general | solution.py:132
  67.3 4.0 %all-to-all-start = ((bf16[4,4,24,768]{3,2,1,0:T(8,128)(2,1)}), bf16[4,4,24,768]{3,2,1,0:T(8,128)(2,1)S(1)}, u32[]{:S(2)}, u32[]{:S(2)}) async-start(bf16[4,4,24,768]{3,2,1,0:T(8,128)(2,1)} %bitcast.20), calls=%async_computation.1 | async-start | bytes 1179648 | tf_op jit(solution)/shard_map/all_to_all | solution.py:75
  71.3 10.0 %all-to-all-done = bf16[4,4,24,768]{3,2,1,0:T(8,128)(2,1)S(1)} async-done(((bf16[4,4,24,768]{3,2,1,0:T(8,128)(2,1)}), bf16[4,4,24,768]{3,2,1,0:T(8,128)(2,1)S(1)}, u32[]{:S(2)}, u32[]{:S(2)}) %all-to-all-start) | async-done | bytes 589856 | tf_op jit(solution)/shard_map/all_to_all | solution.py:75
  81.3 0.1 fusion.9
  81.4 0.1 fusion.11
  81.5 17.3 %all_to_all.10 = bf16[8,24,768]{2,1,0:T(8,128)(2,1)S(1)} all-to-all(bf16[8,24,768]{2,1,0:T(8,128)(2,1)S(1)} %pad_maximum_fusion.2), channel_id=1, replica_groups={{0,128,256,384,2,130,258,386},{1,129,257,385,3,131,259,387},{4,132,260,..., dimensions={0} | all-to-all | bytes 589824 | tf_op jit(solution)/shard_map/all_to_all | solution.py:75
  98.9 11.2 %all_gather.11 = bf16[96,3072]{1,0:T(8,128)(2,1)S(1)} all-gather(bf16[24,3072]{1,0:T(8,128)(2,1)S(1)} %bitcast.48), channel_id=1, replica_groups={{0,4,8,12},{1,5,9,13},{2,6,10,14},{3,7,11,15},{16,20,24,28},{17,21,25,2..., dimensions={0}, use_global_device_ids=true | all-gather | bytes 737280 | tf_op jit(solution)/shard_map/all_gather | solution.py:148
  110.1 6.7 %collective-permute-start.8 = (bf16[96,3072]{1,0:T(8,128)(2,1)S(1)}, bf16[96,3072]{1,0:T(8,128)(2,1)S(1)}, u32[]{:S(2)}, u32[]{:S(2)}) collective-permute-start(bf16[96,3072]{1,0:T(8,128)(2,1)S(1)} %all_gather.11), channel_id=1, source_target_pairs={{0,1},{1,0},{2,3},{3,2},{4,5},{5,4},{6,7},{7,6},{8,9},{9,8},{10,11... | collective-permute-start | bytes 1769480 | tf_op jit(solution)/shard_map/ppermute | solution.py:42
  116.8 0.0 reduce-scatter.2.cloned.1.call-done
  116.8 1.6 %multiply_convert_fusion = bf16[96,768]{1,0:T(8,128)(2,1)} fusion(bf16[96,768]{1,0:T(8,128)(2,1)} %reduce-scatter.2.cloned.1.call-done), kind=kLoop, calls=%fused_computation.28 | loop fusion | flops 221184 | bytes 294912 | tf_op jit(solution)/shard_map/convert_element_type | solution.py:124
  118.4 0.0 collective-permute-done.8
  118.4 1.3 maximum_select_fusion.1
  (5 shorter events, 0.1 us)
Async XLA Ops:
  7.2 46.6 %all-gather.2.cloned.1.call-start = ((), (), s32[]{:S(2)}) async-start(), calls=%async_computation.4 | async-start | bytes 1327104 | tf_op jit(solution)/shard_map/all_gather | solution.py:100
  7.9 108.9 %reduce-scatter.2.cloned.1.call-start = ((), (), s32[]{:S(2)}) async-start(), calls=%async_computation.3 | async-start | bytes 1327104 | tf_op jit(solution)/shard_map/reduce_scatter | solution.py:121
  9.1 19.4 %collective-permute-start = (bf16[24,768]{1,0:T(8,128)(2,1)S(1)}, bf16[24,768]{1,0:T(8,128)(2,1)S(1)}, u32[]{:S(2)}, u32[]{:S(2)}) collective-permute-start(bf16[24,768]{1,0:T(8,128)(2,1)S(1)} %get-tuple-element.5), channel_id=1, source_target_pairs={{0,128},{1,129},{2,130},{3,131},{4,132},{5,133},{6,134},{7,135},{8... | collective-permute-start | bytes 110600 | tf_op jit(solution)/shard_map/ppermute | solution.py:42
  14.0 18.6 %collective-permute-start.1 = (bf16[24,768]{1,0:T(8,128)(2,1)S(1)}, bf16[24,768]{1,0:T(8,128)(2,1)S(1)}, u32[]{:S(2)}, u32[]{:S(2)}) collective-permute-start(bf16[24,768]{1,0:T(8,128)(2,1)S(1)} %get-tuple-element.7), channel_id=1, source_target_pairs={{0,256},{1,257},{2,258},{3,259},{4,260},{5,261},{6,262},{7,263},{8... | collective-permute-start | bytes 110600 | tf_op jit(solution)/shard_map/ppermute | solution.py:42
  19.8 12.7 %collective-permute-start.2 = (bf16[24,768]{1,0:T(8,128)(2,1)S(1)}, bf16[24,768]{1,0:T(8,128)(2,1)S(1)}, u32[]{:S(2)}, u32[]{:S(2)}) collective-permute-start(bf16[24,768]{1,0:T(8,128)(2,1)S(1)} %get-tuple-element.6), channel_id=1, source_target_pairs={{0,384},{1,385},{2,386},{3,387},{4,388},{5,389},{6,390},{7,391},{8... | collective-permute-start | bytes 110600 | tf_op jit(solution)/shard_map/ppermute | solution.py:42
  23.4 30.0 %collective-permute-start.4 = (bf16[192,768]{1,0:T(8,128)(2,1)S(1)}, bf16[192,768]{1,0:T(8,128)(2,1)S(1)}, u32[]{:S(2)}, u32[]{:S(2)}) collective-permute-start(bf16[192,768]{1,0:T(8,128)(2,1)S(1)} %fusion.7), channel_id=1, source_target_pairs={{0,128},{1,129},{2,130},{3,131},{4,132},{5,133},{6,134},{7,135},{8... | collective-permute-start | bytes 884744 | tf_op jit(solution)/shard_map/ppermute | solution.py:42
  26.6 26.9 %collective-permute-start.5 = (bf16[192,768]{1,0:T(8,128)(2,1)S(1)}, bf16[192,768]{1,0:T(8,128)(2,1)S(1)}, u32[]{:S(2)}, u32[]{:S(2)}) collective-permute-start(bf16[192,768]{1,0:T(8,128)(2,1)S(1)} %fusion.7), channel_id=1, source_target_pairs={{0,256},{1,257},{2,258},{3,259},{4,260},{5,261},{6,262},{7,263},{8... | collective-permute-start | bytes 884744 | tf_op jit(solution)/shard_map/ppermute | solution.py:42
  28.5 24.9 %collective-permute-start.6 = (bf16[192,768]{1,0:T(8,128)(2,1)S(1)}, bf16[192,768]{1,0:T(8,128)(2,1)S(1)}, u32[]{:S(2)}, u32[]{:S(2)}) collective-permute-start(bf16[192,768]{1,0:T(8,128)(2,1)S(1)} %fusion.7), channel_id=1, source_target_pairs={{0,384},{1,385},{2,386},{3,387},{4,388},{5,389},{6,390},{7,391},{8... | collective-permute-start | bytes 884744 | tf_op jit(solution)/shard_map/ppermute | solution.py:42
  44.5 17.8 %collective-permute-start.3 = (bf16[4,96,768]{2,1,0:T(8,128)(2,1)S(1)}, bf16[4,96,768]{2,1,0:T(8,128)(2,1)S(1)}, u32[]{:S(2)}, u32[]{:S(2)}) collective-permute-start(bf16[4,96,768]{2,1,0:T(8,128)(2,1)S(1)} %all_gather.9), channel_id=1, source_target_pairs={{0,1},{1,0},{2,3},{3,2},{4,5},{5,4},{6,7},{7,6},{8,9},{9,8},{10,11... | collective-permute-start | bytes 1769480 | tf_op jit(solution)/shard_map/ppermute | solution.py:42
  56.5 8.1 %collective-permute-start.7 = (bf16[384,768]{1,0:T(8,128)(2,1)}, bf16[384,768]{1,0:T(8,128)(2,1)S(1)}, u32[]{:S(2)}, u32[]{:S(2)}) collective-permute-start(bf16[384,768]{1,0:T(8,128)(2,1)} %convolution_convert_fusion.1), channel_id=1, source_target_pairs={{0,1},{1,0},{2,3},{3,2},{4,5},{5,4},{6,7},{7,6},{8,9},{9,8},{10,11... | collective-permute-start | bytes 1769480 | tf_op jit(solution)/shard_map/ppermute | solution.py:42
  64.5 1.3 %copy-start = (bf16[768,768]{1,0:T(8,128)(2,1)S(1)}, bf16[768,768]{1,0:T(8,128)(2,1)}, u32[]{:S(2)}) copy-start(bf16[768,768]{1,0:T(8,128)(2,1)} %all-gather.2.cloned.1.call-done) | copy-start | bytes 3538948
  67.3 14.0 %all-to-all-start = ((bf16[4,4,24,768]{3,2,1,0:T(8,128)(2,1)}), bf16[4,4,24,768]{3,2,1,0:T(8,128)(2,1)S(1)}, u32[]{:S(2)}, u32[]{:S(2)}) async-start(bf16[4,4,24,768]{3,2,1,0:T(8,128)(2,1)} %bitcast.20), calls=%async_computation.1 | async-start | bytes 1179648 | tf_op jit(solution)/shard_map/all_to_all | solution.py:75
  110.1 8.3 %collective-permute-start.8 = (bf16[96,3072]{1,0:T(8,128)(2,1)S(1)}, bf16[96,3072]{1,0:T(8,128)(2,1)S(1)}, u32[]{:S(2)}, u32[]{:S(2)}) collective-permute-start(bf16[96,3072]{1,0:T(8,128)(2,1)S(1)} %all_gather.11), channel_id=1, source_target_pairs={{0,1},{1,0},{2,3},{3,2},{4,5},{5,4},{6,7},{7,6},{8,9},{9,8},{10,11... | collective-permute-start | bytes 1769480 | tf_op jit(solution)/shard_map/ppermute | solution.py:42
Sparse Core Ops, SparseCore 0:
  10.1 42.9 all-gather.1
  64.7 36.7 reduce-scatter.1

commit v4 on v3

v4 whole, which is shorter than its diff:
```python
import math

import jax
import jax.numpy as jnp
from jax import lax
from jax.experimental import pallas as pl
from jax.experimental.pallas import tpu as pltpu
from jax.sharding import PartitionSpec as P

Z_LO, Y = 4, 8
X, Z_HI, CORE = 4, 2, 2
AXES = ("fsdp", "mp")


def fsdp_index(z, y):
    return z * Y + y


def mp_index(x, h, c):
    return (x * Z_HI + h) * CORE + c


Y_GROUPS = [[fsdp_index(z, y) for y in range(Y)] for z in range(Z_LO)]
X_GROUPS = [[mp_index(x, h, c) for x in range(X)] for h in range(Z_HI) for c in range(CORE)]
RING_GROUPS = [
    [fsdp_index(z, y) * (X * Z_HI * CORE) + mp_index(x, h, c) for h in range(Z_HI) for z in range(Z_LO)]
    for y in range(Y)
    for x in range(X)
    for c in range(CORE)
]


def moved(value, target):
    pairs = []
    for z in range(Z_LO):
        for y in range(Y):
            for x in range(X):
                for h in range(Z_HI):
                    for c in range(CORE):
                        z2, y2, x2, h2, c2 = target(z, y, x, h, c)
                        source = fsdp_index(z, y) * X * Z_HI * CORE + mp_index(x, h, c)
                        goal = fsdp_index(z2, y2) * X * Z_HI * CORE + mp_index(x2, h2, c2)
                        pairs.append((source, goal))
    return lax.ppermute(value, AXES, pairs)


def along_z_lo(value, step):
    return moved(value, lambda z, y, x, h, c: ((z + step) % Z_LO, y, x, h, c))


def to_other_core(value):
    return moved(value, lambda z, y, x, h, c: (z, y, x, h, 1 - c))


def gelu_slope(hidden):
    coeff = math.sqrt(2.0 / math.pi)
    inner = coeff * (hidden + 0.044715 * hidden * hidden * hidden)
    tangent = jnp.tanh(inner)
    return 0.5 * (1.0 + tangent) + 0.5 * hidden * (1.0 - tangent * tangent) * coeff * (
        1.0 + 3.0 * 0.044715 * hidden * hidden
    )


def swap(blocks, axis, groups):
    return lax.all_to_all(blocks, axis, 0, 0, axis_index_groups=groups, tiled=True)


def input_parts_kernel(place, *refs):
    blocks, weight, outs = refs[:Z_LO], refs[Z_LO], refs[Z_LO + 1 :]
    rows = blocks[0].shape[0]
    piece = rows // X
    half = weight.shape[0] // CORE
    lhs = jnp.concatenate([block[...] for block in blocks], axis=0)
    for out, which in zip(outs, (1 - place[1], place[1])):
        result = lax.dot_general(
            lhs,
            weight[pl.ds(pl.multiple_of(which * half, half), half), :],
            (((1,), (1,)), ((), ())),
            preferred_element_type=jnp.float32,
        )
        for k in range(Z_LO):
            owner = jnp.bitwise_and(place[0] + (Z_LO - k), Z_LO - 1)
            for x in range(X):
                start = k * rows + x * piece
                out[x, owner] = result[start : start + piece].astype(out.dtype)


def input_parts(place, blocks, weight):
    rows, units = blocks[0].shape
    half = weight.shape[0] // CORE
    out = jax.ShapeDtypeStruct((X, Z_LO, rows // X, half), jnp.bfloat16)
    return pl.pallas_call(
        input_parts_kernel,
        in_specs=[pl.BlockSpec(memory_space=pltpu.SMEM)]
        + [pl.BlockSpec(memory_space=pltpu.VMEM)] * (Z_LO + 1),
        out_specs=[pl.BlockSpec(memory_space=pltpu.VMEM)] * 2,
        out_shape=[out, out],
        compiler_params=pltpu.CompilerParams(vmem_limit_bytes=32 * 1024 * 1024),
        cost_estimate=pl.CostEstimate(
            flops=4 * Z_LO * rows * units * half,
            bytes_accessed=2 * (Z_LO * rows * units + 2 * half * units + 2 * Z_LO * rows * half),
            transcendentals=0,
        ),
    )(place, *blocks, weight)


def joined_kernel(core, mine, theirs, out):
    blocks, quarters, piece, half = mine.shape
    for own in range(CORE):

        @pl.when(core[0] == own)
        def _():
            for x in range(blocks):
                for z in range(quarters):
                    for c in range(CORE):
                        start = (z * CORE + c) * half
                        out[x * piece : (x + 1) * piece, start : start + half] = (
                            mine if c == own else theirs
                        )[x, z]


def joined(core, mine, theirs):
    x, z, piece, half = mine.shape
    return pl.pallas_call(
        joined_kernel,
        in_specs=[
            pl.BlockSpec(memory_space=pltpu.SMEM),
            pl.BlockSpec(memory_space=pltpu.VMEM),
            pl.BlockSpec(memory_space=pltpu.VMEM),
        ],
        out_specs=pl.BlockSpec(memory_space=pltpu.VMEM),
        out_shape=jax.ShapeDtypeStruct((x * piece, z * CORE * half), mine.dtype),
        compiler_params=pltpu.CompilerParams(vmem_limit_bytes=32 * 1024 * 1024),
        cost_estimate=pl.CostEstimate(
            flops=0, bytes_accessed=4 * CORE * mine.size, transcendentals=0
        ),
    )(core, mine, theirs)


def total(blocks):
    return jnp.sum(blocks.astype(jnp.float32), axis=0).astype(jnp.bfloat16)


def shards(tokens, pre_act, grad_act, w_up):
    rows, width = tokens.shape
    units = pre_act.shape[1]
    quarter = width // Z_LO
    half = quarter // CORE
    piece = rows // X
    norm_factor = float(rows * Z_LO * Y) ** (-0.5)
    z_lo = lax.shift_right_logical(lax.axis_index("fsdp"), 3)
    x = lax.shift_right_logical(lax.axis_index("mp"), 2)
    core = jnp.bitwise_and(lax.axis_index("mp"), 1)
    own_place = jnp.stack([z_lo, core])

    weight = lax.all_gather(w_up, "fsdp", axis=0, axis_index_groups=Y_GROUPS, tiled=True)
    hidden_grad = (grad_act.astype(jnp.float32) * gelu_slope(pre_act.astype(jnp.float32))).astype(
        jnp.bfloat16
    )
    hidden = [hidden_grad] + [along_z_lo(hidden_grad, k) for k in range(1, Z_LO)]
    part = rows // (CORE * X)
    mine = lax.dynamic_slice_in_dim(tokens, (core * X + x) * part, part, 0)
    mine = [
        lax.dynamic_slice_in_dim(mine, jnp.bitwise_and(z_lo + k, Z_LO - 1) * quarter, quarter, 1)
        for k in range(Z_LO)
    ]
    mine = jnp.stack([mine[0]] + [along_z_lo(mine[k], k) for k in range(1, Z_LO)])
    mine = lax.all_gather(mine, "mp", axis=1, axis_index_groups=X_GROUPS, tiled=True)
    mine, hidden = lax.optimization_barrier((mine, hidden))
    other = to_other_core(mine)
    patches = jnp.where(
        core == 0, jnp.stack([mine, other], axis=1), jnp.stack([other, mine], axis=1)
    ).reshape(Z_LO * rows, quarter)

    weight_part = lax.dot_general(
        patches,
        jnp.concatenate(hidden, 0),
        (((0,), (0,)), ((), ())),
        preferred_element_type=jnp.float32,
    ).astype(jnp.bfloat16)
    received = lax.psum_scatter(
        weight_part, "fsdp", scatter_dimension=0, axis_index_groups=Y_GROUPS, tiled=True
    )
    grad_weight = (received.astype(jnp.float32) * norm_factor).astype(jnp.bfloat16)

    for_other, for_own = input_parts(own_place, hidden, weight)
    theirs = to_other_core(for_other)
    partial = (for_own.astype(jnp.float32) + theirs.astype(jnp.float32)).astype(jnp.bfloat16)
    partial = total(swap(partial, "mp", X_GROUPS))
    both = jnp.broadcast_to(partial[None], (Z_HI, Z_LO, piece, half))
    both = swap(both.reshape(Z_HI * Z_LO, piece, half), AXES, RING_GROUPS)
    mine = total(both.reshape(Z_HI, Z_LO, piece, half))
    mine = swap(jnp.broadcast_to(mine[None], (X, Z_LO, piece, half)), "mp", X_GROUPS)
    grad_input = joined(core.reshape(1), mine, to_other_core(mine))
    return (grad_weight, grad_input)


def solution(mesh):
    placed = (P("fsdp", None), P("fsdp", "mp"), P("fsdp", "mp"), P("fsdp", "mp"))
    return jax.shard_map(
        shards,
        mesh=mesh,
        in_specs=placed,
        out_specs=(P("fsdp", "mp"), P("fsdp", None)),
        check_vma=False,
    )
```

time: 127 us -> 124 us (0.976)
  blocking collectives: 40.5 us -> 52.9 us
  starting transfers between devices: 47.1 us -> 38.5 us
  waiting for transfers between devices: 10.8 us -> 5.78 us
  matrix products: 6.39 us -> 2.13 us
  Pallas kernels: 0 us -> 3.05 us
    all_to_all x1 -> x3, blocking collectives: 17.3 us -> 41.3 us  [swap(): lax.all_to_all(blocks, axis, 0, 0, axis_index_groups=groups, tiled=True)]
    all_gather x1 -> x0, blocking collectives: 11.2 us -> none  [shards(): lax.all_gather(ring, 'mp', axis=0, axis_index_groups=X_GROUPS, tiled=True)]
    all_to_all x1 -> x0, waiting for transfers between devices: 10 us -> none  [swap(): lax.all_to_all(blocks, axis, 0, 0, axis_index_groups=groups, tiled=True)]
    ppermute x9, waiting for transfers between devices: 0.02 us -> 5.04 us  [moved(): return lax.ppermute(value, AXES, pairs)]
    ppermute x9, starting transfers between devices: 43 us -> 38.4 us  [moved(): return lax.ppermute(value, AXES, pairs)]
    dot_general x3 -> x1, matrix products: 6.39 us -> 2.13 us  [shards(): lax.dot_general(patches, jnp.concatenate(hidden, 0), (((0,), (0,)), ((),...]
    all_to_all x1 -> x0, starting transfers between devices: 3.97 us -> none  [swap(): lax.all_to_all(blocks, axis, 0, 0, axis_index_groups=groups, tiled=True)]
    pallas_call x0 -> x2, Pallas kernels: none -> 3.05 us  [the longest x1 1.93 us: input_parts(): pl.pallas_call(input_parts_kernel, in_specs=[pl.BlockSpec(memory_space=pl...]
  transfers between devices with their start and end apart: 12 -> 11, of which waited for: 1 -> 2; matrix products, arithmetic and copies ran while one was open for 9% -> 6% of each run, Pallas kernels for 0% -> 0%
where the time goes in v4:
time: 124 us
  blocking collectives  52.9 us (43%)
  starting transfers between devices  38.5 us (31%)
  between operations  14.2 us (11%)
  waiting for transfers between devices  5.78 us (5%)
  other arithmetic  4.63 us (4%)
  Pallas kernels  3.05 us (2%)
  local copies, waits for them, and re-layouts  2.4 us (2%)
  matrix products  2.13 us (2%)
    all_to_all x3, blocking collectives, swap(): lax.all_to_all(blocks, axis, 0, 0, axis_index_groups=groups, tiled=True)  41.3 us
    ppermute x9, starting transfers between devices, moved(): return lax.ppermute(value, AXES, pairs)  38.4 us
    all_gather x1, blocking collectives, shards(): lax.all_gather(mine, 'mp', axis=1, axis_index_groups=X_GROUPS, tiled=True)  11.7 us
    ppermute x9, waiting for transfers between devices, moved(): return lax.ppermute(value, AXES, pairs)  5.04 us
  transfers between devices with their start and end apart: 11, of which 2 were waited for; matrix products, arithmetic and copies ran while one was open for 6% of the time, Pallas kernels for 0%

profile of v4, /device:TPU:1, one launch (start us, length us, event | category | flops | bytes accessed | tf_op | source)
XLA Modules:
  0.0 123.7 jit_solution(5440641968660906579)
XLA Ops:
  7.2 0.0 all-gather.2.cloned.1.call-start
  7.2 0.7 all-gather.2.cloned.1.call-update
  7.9 0.0 reduce-scatter.2.cloned.1.call-start
  8.0 1.1 dynamic-slice_bitcast_fusion
  9.0 8.4 %collective-permute-start.2 = (bf16[24,768]{1,0:T(8,128)(2,1)S(1)}, bf16[24,768]{1,0:T(8,128)(2,1)S(1)}, u32[]{:S(2)}, u32[]{:S(2)}) collective-permute-start(bf16[24,768]{1,0:T(8,128)(2,1)S(1)} %get-tuple-element.18), channel_id=1, source_target_pairs={{0,384},{1,385},{2,386},{3,387},{4,388},{5,389},{6,390},{7,391},{8... | collective-permute-start | bytes 110600 | tf_op jit(solution)/shard_map/ppermute | solution.py:44
  17.5 1.9 %collective-permute-start.1 = (bf16[24,768]{1,0:T(8,128)(2,1)S(1)}, bf16[24,768]{1,0:T(8,128)(2,1)S(1)}, u32[]{:S(2)}, u32[]{:S(2)}) collective-permute-start(bf16[24,768]{1,0:T(8,128)(2,1)S(1)} %get-tuple-element.19), channel_id=1, source_target_pairs={{0,256},{1,257},{2,258},{3,259},{4,260},{5,261},{6,262},{7,263},{8... | collective-permute-start | bytes 110600 | tf_op jit(solution)/shard_map/ppermute | solution.py:44
  19.4 2.2 %collective-permute-start = (bf16[24,768]{1,0:T(8,128)(2,1)S(1)}, bf16[24,768]{1,0:T(8,128)(2,1)S(1)}, u32[]{:S(2)}, u32[]{:S(2)}) collective-permute-start(bf16[24,768]{1,0:T(8,128)(2,1)S(1)} %get-tuple-element.17), channel_id=1, source_target_pairs={{0,128},{1,129},{2,130},{3,131},{4,132},{5,133},{6,134},{7,135},{8... | collective-permute-start | bytes 110600 | tf_op jit(solution)/shard_map/ppermute | solution.py:44
  21.6 1.5 %fusion.14.refs_0_ = bf16[192,768]{1,0:T(8,128)(2,1)S(1)} fusion(bf16[192,768]{1,0:T(8,128)(2,1)} %param.5, bf16[192,768]{1,0:T(8,128)(2,1)} %param.6), kind=kLoop, calls=%fused_computation.24 | loop fusion | flops 3096576 | bytes 884736 | tf_op jit(solution)/shard_map/convert_element_type | solution.py:157
  23.1 4.3 %collective-permute-start.3 = (bf16[192,768]{1,0:T(8,128)(2,1)S(1)}, bf16[192,768]{1,0:T(8,128)(2,1)S(1)}, u32[]{:S(2)}, u32[]{:S(2)}) collective-permute-start(bf16[192,768]{1,0:T(8,128)(2,1)S(1)} %fusion.14.refs_0_), channel_id=1, source_target_pairs={{0,128},{1,129},{2,130},{3,131},{4,132},{5,133},{6,134},{7,135},{8... | collective-permute-start | bytes 884744 | tf_op jit(solution)/shard_map/ppermute | solution.py:44
  27.3 2.8 %collective-permute-start.4 = (bf16[192,768]{1,0:T(8,128)(2,1)S(1)}, bf16[192,768]{1,0:T(8,128)(2,1)S(1)}, u32[]{:S(2)}, u32[]{:S(2)}) collective-permute-start(bf16[192,768]{1,0:T(8,128)(2,1)S(1)} %fusion.14.refs_0_), channel_id=1, source_target_pairs={{0,256},{1,257},{2,258},{3,259},{4,260},{5,261},{6,262},{7,263},{8... | collective-permute-start | bytes 884744 | tf_op jit(solution)/shard_map/ppermute | solution.py:44
  30.2 0.0 collective-permute-done.2
  30.2 3.1 %collective-permute-start.5 = (bf16[192,768]{1,0:T(8,128)(2,1)S(1)}, bf16[192,768]{1,0:T(8,128)(2,1)S(1)}, u32[]{:S(2)}, u32[]{:S(2)}) collective-permute-start(bf16[192,768]{1,0:T(8,128)(2,1)S(1)} %fusion.14.refs_0_), channel_id=1, source_target_pairs={{0,384},{1,385},{2,386},{3,387},{4,388},{5,389},{6,390},{7,391},{8... | collective-permute-start | bytes 884744 | tf_op jit(solution)/shard_map/ppermute | solution.py:44
  33.3 0.0 collective-permute-done.1
  33.3 0.0 collective-permute-done
  33.3 11.7 %all_gather.6 = bf16[4,96,768]{2,1,0:T(8,128)(2,1)S(1)} all-gather(bf16[4,24,768]{2,1,0:T(8,128)(2,1)S(1)} %pad_maximum_fusion), channel_id=1, replica_groups={{0,4,8,12},{1,5,9,13},{2,6,10,14},{3,7,11,15},{16,20,24,28},{17,21,25,2..., dimensions={1}, use_global_device_ids=true | all-gather | bytes 737280 | tf_op jit(solution)/shard_map/all_gather | solution.py:168
  45.0 0.0 collective-permute-done.3.refs_1_
  45.0 3.5 %collective-permute-done.4.refs_2_ = bf16[192,768]{1,0:T(8,128)(2,1)S(1)} collective-permute-done((bf16[192,768]{1,0:T(8,128)(2,1)S(1)}, bf16[192,768]{1,0:T(8,128)(2,1)S(1)}, u32[]{:S(2)}, u32[]{:S(2)}) %collective-permute-start.4) | collective-permute-done | bytes 294944 | tf_op jit(solution)/shard_map/ppermute | solution.py:44
  48.5 0.0 collective-permute-done.5.refs_3_
  48.5 3.9 %collective-permute-start.6 = (bf16[4,96,768]{2,1,0:T(8,128)(2,1)S(1)}, bf16[4,96,768]{2,1,0:T(8,128)(2,1)S(1)}, u32[]{:S(2)}, u32[]{:S(2)}) collective-permute-start(bf16[4,96,768]{2,1,0:T(8,128)(2,1)S(1)} %all_gather.6), channel_id=1, source_target_pairs={{0,1},{1,0},{2,3},{3,2},{4,5},{5,4},{6,7},{7,6},{8,9},{9,8},{10,11... | collective-permute-start | bytes 1769480 | tf_op jit(solution)/shard_map/ppermute | solution.py:44
  52.4 0.1 pad_add_fusion.place
  52.5 1.5 %collective-permute-done.6 = bf16[4,96,768]{2,1,0:T(8,128)(2,1)S(1)} collective-permute-done((bf16[4,96,768]{2,1,0:T(8,128)(2,1)S(1)}, bf16[4,96,768]{2,1,0:T(8,128)(2,1)S(1)}, u32[]{:S(2)}, u32[]{:S(2)}) %collective-permute-start.6) | collective-permute-done | bytes 589856 | tf_op jit(solution)/shard_map/ppermute | solution.py:44
  54.0 0.1 maximum_select_fusion
  54.1 0.0 all-gather.2.cloned.1.call-done.refs_4_
  54.1 0.0 copy-start
  54.1 1.3 %copy-done = bf16[768,768]{1,0:T(8,128)(2,1)S(1)} copy-done((bf16[768,768]{1,0:T(8,128)(2,1)S(1)}, bf16[768,768]{1,0:T(8,128)(2,1)}, u32[]{:S(2)}) %copy-start) | copy-done | bytes 1179672
  55.4 1.9 %shard_map.59 = (bf16[4,4,48,384]{3,2,1,0:T(8,128)(2,1)S(1)}, bf16[4,4,48,384]{3,2,1,0:T(8,128)(2,1)S(1)}) custom-call(s32[2]{0:T(128)S(1)} %pad_add_fusion.place, bf16[192,768]{1,0:T(8,128)(2,1)S(1)} %fusion.14.refs_0_, bf16[192,768]{1,0:T(8,128)(2,1)S(1)} %collective-permute-done.3.refs_1_, bf16[192,768]{1,0:T(8,128)(2,1)S(1)} %collective-permute-done.4.refs_2_, ...), custom_call_target="tpu_custom_call" | custom-call | flops 905969664 | bytes 3538944 | tf_op jit(solution)/shard_map/pallas_call | solution.py:92
  57.3 5.2 %collective-permute-start.7 = (bf16[4,4,48,384]{3,2,1,0:T(8,128)(2,1)S(1)}, bf16[4,4,48,384]{3,2,1,0:T(8,128)(2,1)}, u32[]{:S(2)}, u32[]{:S(2)}) collective-permute-start(bf16[4,4,48,384]{3,2,1,0:T(8,128)(2,1)S(1)} %get-tuple-element.15), channel_id=1, source_target_pairs={{0,1},{1,0},{2,3},{3,2},{4,5},{5,4},{6,7},{7,6},{8,9},{9,8},{10,11... | collective-permute-start | bytes 1769480 | tf_op jit(solution)/shard_map/ppermute | solution.py:44
  62.6 2.1 %convolution_convert_fusion = bf16[768,768]{1,0:T(8,128)(2,1)} fusion(bf16[768,768]{1,0:T(8,128)(2,1)S(1)} %bitcast.14, bf16[192,768]{1,0:T(8,128)(2,1)S(1)} %collective-permute-done.5.refs_3_, bf16[192,768]{1,0:T(8,128)(2,1)S(1)} %collective-permute-done.4.refs_2_, bf16[192,768]{1,0:T(8,128)(2,1)S(1)} %collective-permute-done.3.refs_1_, ...), kind=kOutput, calls=%fused_computation | convolution fusion | flops 911278080 | bytes 3538944 | tf_op jit(solution)/shard_map/dot_general | solution.py:175
  64.7 0.0 reduce-scatter.2.cloned.1.call-update
  64.7 0.0 collective-permute-done.7
  64.7 1.2 add_convert_fusion
  65.9 13.5 %all_to_all.15 = bf16[4,4,48,384]{3,2,1,0:T(8,128)(2,1)S(1)} all-to-all(bf16[4,4,48,384]{3,2,1,0:T(8,128)(2,1)S(1)} %add_convert_fusion), channel_id=1, replica_groups={{0,4,8,12},{1,5,9,13},{2,6,10,14},{3,7,11,15},{16,20,24,28},{17,21,25,2..., dimensions={0} | all-to-all | bytes 1179648 | tf_op jit(solution)/shard_map/all_to_all | solution.py:65
  79.4 0.1 reduce_sum.24
  79.6 18.1 %all_to_all.16 = bf16[8,48,384]{2,1,0:T(8,128)(2,1)S(1)} all-to-all(bf16[8,48,384]{2,1,0:T(8,128)(2,1)S(1)} %bitcast.16), channel_id=1, replica_groups={{0,128,256,384,2,130,258,386},{1,129,257,385,3,131,259,387},{4,132,260,..., dimensions={0} | all-to-all | bytes 589824 | tf_op jit(solution)/shard_map/all_to_all | solution.py:65
  97.7 0.1 reduce_sum.25
  97.7 0.1 broadcast_in_dim.5
  97.8 9.7 %all_to_all.17.mine = bf16[4,4,48,384]{3,2,1,0:T(8,128)(2,1)S(1)} all-to-all(bf16[4,4,48,384]{3,2,1,0:T(8,128)(2,1)S(1)} %broadcast_in_dim.5), channel_id=1, replica_groups={{0,4,8,12},{1,5,9,13},{2,6,10,14},{3,7,11,15},{16,20,24,28},{17,21,25,2..., dimensions={0} | all-to-all | bytes 1179648 | tf_op jit(solution)/shard_map/all_to_all | solution.py:65
  107.5 6.6 %collective-permute-start.8 = (bf16[4,4,48,384]{3,2,1,0:T(8,128)(2,1)S(1)}, bf16[4,4,48,384]{3,2,1,0:T(8,128)(2,1)S(1)}, u32[]{:S(2)}, u32[]{:S(2)}) collective-permute-start(bf16[4,4,48,384]{3,2,1,0:T(8,128)(2,1)S(1)} %all_to_all.17.mine), channel_id=1, source_target_pairs={{0,1},{1,0},{2,3},{3,2},{4,5},{5,4},{6,7},{7,6},{8,9},{9,8},{10,11... | collective-permute-start | bytes 1769480 | tf_op jit(solution)/shard_map/ppermute | solution.py:44
  114.1 0.0 reduce-scatter.2.cloned.1.call-done
  114.1 1.6 %multiply_convert_fusion = bf16[96,768]{1,0:T(8,128)(2,1)} fusion(bf16[96,768]{1,0:T(8,128)(2,1)} %reduce-scatter.2.cloned.1.call-done), kind=kLoop, calls=%fused_computation.26 | loop fusion | flops 221184 | bytes 294912 | tf_op jit(solution)/shard_map/convert_element_type | solution.py:184
  115.7 0.0 collective-permute-done.8.theirs
  115.7 1.1 shard_map.60
  (2 shorter events, 0.0 us)
Async XLA Ops:
  7.2 47.0 %all-gather.2.cloned.1.call-start = ((), (), s32[]{:S(2)}) async-start(), calls=%async_computation.5 | async-start | bytes 1327104 | tf_op jit(solution)/shard_map/all_gather | solution.py:156
  7.9 106.2 %reduce-scatter.2.cloned.1.call-start = ((), (), s32[]{:S(2)}) async-start(), calls=%async_computation.4 | async-start | bytes 1327104 | tf_op jit(solution)/shard_map/reduce_scatter | solution.py:181
  9.0 21.2 %collective-permute-start.2 = (bf16[24,768]{1,0:T(8,128)(2,1)S(1)}, bf16[24,768]{1,0:T(8,128)(2,1)S(1)}, u32[]{:S(2)}, u32[]{:S(2)}) collective-permute-start(bf16[24,768]{1,0:T(8,128)(2,1)S(1)} %get-tuple-element.18), channel_id=1, source_target_pairs={{0,384},{1,385},{2,386},{3,387},{4,388},{5,389},{6,390},{7,391},{8... | collective-permute-start | bytes 110600 | tf_op jit(solution)/shard_map/ppermute | solution.py:44
  17.5 15.8 %collective-permute-start.1 = (bf16[24,768]{1,0:T(8,128)(2,1)S(1)}, bf16[24,768]{1,0:T(8,128)(2,1)S(1)}, u32[]{:S(2)}, u32[]{:S(2)}) collective-permute-start(bf16[24,768]{1,0:T(8,128)(2,1)S(1)} %get-tuple-element.19), channel_id=1, source_target_pairs={{0,256},{1,257},{2,258},{3,259},{4,260},{5,261},{6,262},{7,263},{8... | collective-permute-start | bytes 110600 | tf_op jit(solution)/shard_map/ppermute | solution.py:44
  19.4 13.9 %collective-permute-start = (bf16[24,768]{1,0:T(8,128)(2,1)S(1)}, bf16[24,768]{1,0:T(8,128)(2,1)S(1)}, u32[]{:S(2)}, u32[]{:S(2)}) collective-permute-start(bf16[24,768]{1,0:T(8,128)(2,1)S(1)} %get-tuple-element.17), channel_id=1, source_target_pairs={{0,128},{1,129},{2,130},{3,131},{4,132},{5,133},{6,134},{7,135},{8... | collective-permute-start | bytes 110600 | tf_op jit(solution)/shard_map/ppermute | solution.py:44
  23.1 21.9 %collective-permute-start.3 = (bf16[192,768]{1,0:T(8,128)(2,1)S(1)}, bf16[192,768]{1,0:T(8,128)(2,1)S(1)}, u32[]{:S(2)}, u32[]{:S(2)}) collective-permute-start(bf16[192,768]{1,0:T(8,128)(2,1)S(1)} %fusion.14.refs_0_), channel_id=1, source_target_pairs={{0,128},{1,129},{2,130},{3,131},{4,132},{5,133},{6,134},{7,135},{8... | collective-permute-start | bytes 884744 | tf_op jit(solution)/shard_map/ppermute | solution.py:44
  27.3 21.1 %collective-permute-start.4 = (bf16[192,768]{1,0:T(8,128)(2,1)S(1)}, bf16[192,768]{1,0:T(8,128)(2,1)S(1)}, u32[]{:S(2)}, u32[]{:S(2)}) collective-permute-start(bf16[192,768]{1,0:T(8,128)(2,1)S(1)} %fusion.14.refs_0_), channel_id=1, source_target_pairs={{0,256},{1,257},{2,258},{3,259},{4,260},{5,261},{6,262},{7,263},{8... | collective-permute-start | bytes 884744 | tf_op jit(solution)/shard_map/ppermute | solution.py:44
  30.2 18.3 %collective-permute-start.5 = (bf16[192,768]{1,0:T(8,128)(2,1)S(1)}, bf16[192,768]{1,0:T(8,128)(2,1)S(1)}, u32[]{:S(2)}, u32[]{:S(2)}) collective-permute-start(bf16[192,768]{1,0:T(8,128)(2,1)S(1)} %fusion.14.refs_0_), channel_id=1, source_target_pairs={{0,384},{1,385},{2,386},{3,387},{4,388},{5,389},{6,390},{7,391},{8... | collective-permute-start | bytes 884744 | tf_op jit(solution)/shard_map/ppermute | solution.py:44
  48.5 5.5 %collective-permute-start.6 = (bf16[4,96,768]{2,1,0:T(8,128)(2,1)S(1)}, bf16[4,96,768]{2,1,0:T(8,128)(2,1)S(1)}, u32[]{:S(2)}, u32[]{:S(2)}) collective-permute-start(bf16[4,96,768]{2,1,0:T(8,128)(2,1)S(1)} %all_gather.6), channel_id=1, source_target_pairs={{0,1},{1,0},{2,3},{3,2},{4,5},{5,4},{6,7},{7,6},{8,9},{9,8},{10,11... | collective-permute-start | bytes 1769480 | tf_op jit(solution)/shard_map/ppermute | solution.py:44
  54.1 1.3 %copy-start = (bf16[768,768]{1,0:T(8,128)(2,1)S(1)}, bf16[768,768]{1,0:T(8,128)(2,1)}, u32[]{:S(2)}) copy-start(bf16[768,768]{1,0:T(8,128)(2,1)} %all-gather.2.cloned.1.call-done.refs_4_) | copy-start | bytes 3538948
  57.3 7.4 %collective-permute-start.7 = (bf16[4,4,48,384]{3,2,1,0:T(8,128)(2,1)S(1)}, bf16[4,4,48,384]{3,2,1,0:T(8,128)(2,1)}, u32[]{:S(2)}, u32[]{:S(2)}) collective-permute-start(bf16[4,4,48,384]{3,2,1,0:T(8,128)(2,1)S(1)} %get-tuple-element.15), channel_id=1, source_target_pairs={{0,1},{1,0},{2,3},{3,2},{4,5},{5,4},{6,7},{7,6},{8,9},{9,8},{10,11... | collective-permute-start | bytes 1769480 | tf_op jit(solution)/shard_map/ppermute | solution.py:44
  107.5 8.3 %collective-permute-start.8 = (bf16[4,4,48,384]{3,2,1,0:T(8,128)(2,1)S(1)}, bf16[4,4,48,384]{3,2,1,0:T(8,128)(2,1)S(1)}, u32[]{:S(2)}, u32[]{:S(2)}) collective-permute-start(bf16[4,4,48,384]{3,2,1,0:T(8,128)(2,1)S(1)} %all_to_all.17.mine), channel_id=1, source_target_pairs={{0,1},{1,0},{2,3},{3,2},{4,5},{5,4},{6,7},{7,6},{8,9},{9,8},{10,11... | collective-permute-start | bytes 1769480 | tf_op jit(solution)/shard_map/ppermute | solution.py:44
Sparse Core Ops, SparseCore 0:
  10.1 42.9 all-gather.1
  64.8 39.5 reduce-scatter.1

commit v5 on v4

--- a/solution.py
+++ b/solution.py
@@ -21,6 +21,7 @@
 
 
 Y_GROUPS = [[fsdp_index(z, y) for y in range(Y)] for z in range(Z_LO)]
+C_GROUPS = [[mp_index(x, h, c) for c in range(CORE)] for x in range(X) for h in range(Z_HI)]
 X_GROUPS = [[mp_index(x, h, c) for x in range(X)] for h in range(Z_HI) for c in range(CORE)]
 RING_GROUPS = [
     [fsdp_index(z, y) * (X * Z_HI * CORE) + mp_index(x, h, c) for h in range(Z_HI) for z in range(Z_LO)]
@@ -157,20 +158,23 @@
     hidden_grad = (grad_act.astype(jnp.float32) * gelu_slope(pre_act.astype(jnp.float32))).astype(
         jnp.bfloat16
     )
-    hidden = [hidden_grad] + [along_z_lo(hidden_grad, k) for k in range(1, Z_LO)]
     part = rows // (CORE * X)
     mine = lax.dynamic_slice_in_dim(tokens, (core * X + x) * part, part, 0)
     mine = [
         lax.dynamic_slice_in_dim(mine, jnp.bitwise_and(z_lo + k, Z_LO - 1) * quarter, quarter, 1)
         for k in range(Z_LO)
     ]
-    mine = jnp.stack([mine[0]] + [along_z_lo(mine[k], k) for k in range(1, Z_LO)])
+    mine = [mine[0]] + [along_z_lo(mine[k], k) for k in range(1, Z_LO)]
+    mine, hidden_grad = lax.optimization_barrier((mine, hidden_grad))
+    hidden = [hidden_grad] + [along_z_lo(hidden_grad, k) for k in range(1, Z_LO)]
+    mine = jnp.stack(mine)
     mine = lax.all_gather(mine, "mp", axis=1, axis_index_groups=X_GROUPS, tiled=True)
-    mine, hidden = lax.optimization_barrier((mine, hidden))
-    other = to_other_core(mine)
-    patches = jnp.where(
-        core == 0, jnp.stack([mine, other], axis=1), jnp.stack([other, mine], axis=1)
-    ).reshape(Z_LO * rows, quarter)
+    patches = [
+        lax.all_gather(mine[k : k + 2], "mp", axis=1, axis_index_groups=C_GROUPS, tiled=True)
+        for k in range(0, Z_LO, 2)
+    ]
+    patches, hidden = lax.optimization_barrier((patches, hidden))
+    patches = jnp.concatenate(patches, 0).reshape(Z_LO * rows, quarter)
 
     weight_part = lax.dot_general(
         patches,
@@ -178,6 +182,7 @@
         (((0,), (0,)), ((), ())),
         preferred_element_type=jnp.float32,
     ).astype(jnp.bfloat16)
+    weight_part, hidden = lax.optimization_barrier((weight_part, hidden))
     received = lax.psum_scatter(
         weight_part, "fsdp", scatter_dimension=0, axis_index_groups=Y_GROUPS, tiled=True
     )

time: 124 us -> 122 us (0.984)
  blocking collectives: 52.9 us -> 62 us
  starting transfers between devices: 38.5 us -> 30.7 us
  waiting for transfers between devices: 5.78 us -> 3.33 us
    all_gather x0 -> x2, blocking collectives: none -> 10.5 us  [shards(): lax.all_gather(mine[k:k + 2], 'mp', axis=1, axis_index_groups=C_GROUPS, t...]
    ppermute x9 -> x8, starting transfers between devices: 38.4 us -> 30.6 us  [moved(): return lax.ppermute(value, AXES, pairs)]
    ppermute x9 -> x8, waiting for transfers between devices: 5.04 us -> 2.61 us  [moved(): return lax.ppermute(value, AXES, pairs)]
  transfers between devices with their start and end apart: 11 -> 10, of which waited for: 2 -> 2; matrix products, arithmetic and copies ran while one was open for 6% -> 6% of each run, Pallas kernels for 0% -> 0%
where the time goes in v5:
time: 122 us; the launch traced here: 121 us
  blocking collectives  62 us (51%)
  starting transfers between devices  30.7 us (25%)
  between operations  14.2 us (12%)
  other arithmetic  3.57 us (3%)
  waiting for transfers between devices  3.33 us (3%)
  Pallas kernels  3.05 us (2%)
  local copies, waits for them, and re-layouts  2.44 us (2%)
  matrix products  2.14 us (2%)
    all_to_all x3, blocking collectives, swap(): lax.all_to_all(blocks, axis, 0, 0, axis_index_groups=groups, tiled=True)  40.1 us
    ppermute x8, starting transfers between devices, moved(): return lax.ppermute(value, AXES, pairs)  30.6 us
    all_gather x1, blocking collectives, shards(): lax.all_gather(mine, 'mp', axis=1, axis_index_groups=X_GROUPS, tiled=True)  11.4 us
    all_gather x2, blocking collectives, shards(): lax.all_gather(mine[k:k + 2], 'mp', axis=1, axis_index_groups=C_GROUPS, t...  10.5 us
    ppermute x8, waiting for transfers between devices, moved(): return lax.ppermute(value, AXES, pairs)  2.61 us
  transfers between devices with their start and end apart: 10, of which 2 were waited for; matrix products, arithmetic and copies ran while one was open for 6% of the time, Pallas kernels for 0%

profile of v5, /device:TPU:1, one launch (start us, length us, event | category | flops | bytes accessed | tf_op | source)
XLA Modules:
  0.0 121.3 jit_solution(14543689136330611193)
XLA Ops:
  7.2 0.0 all-gather.2.cloned.1.call-start
  7.2 0.7 all-gather.2.cloned.1.call-update
  7.9 0.0 reduce-scatter.2.cloned.1.call-start
  8.0 1.1 fusion.17
  9.0 4.8 %collective-permute-start = (bf16[24,768]{1,0:T(8,128)(2,1)S(1)}, bf16[24,768]{1,0:T(8,128)(2,1)S(1)}, u32[]{:S(2)}, u32[]{:S(2)}) collective-permute-start(bf16[24,768]{1,0:T(8,128)(2,1)S(1)} %get-tuple-element.39), channel_id=1, source_target_pairs={{0,128},{1,129},{2,130},{3,131},{4,132},{5,133},{6,134},{7,135},{8... | collective-permute-start | bytes 110600 | tf_op jit(solution)/shard_map/ppermute | solution.py:45
  13.9 5.8 %collective-permute-start.1 = (bf16[24,768]{1,0:T(8,128)(2,1)S(1)}, bf16[24,768]{1,0:T(8,128)(2,1)S(1)}, u32[]{:S(2)}, u32[]{:S(2)}) collective-permute-start(bf16[24,768]{1,0:T(8,128)(2,1)S(1)} %get-tuple-element.41), channel_id=1, source_target_pairs={{0,256},{1,257},{2,258},{3,259},{4,260},{5,261},{6,262},{7,263},{8... | collective-permute-start | bytes 110600 | tf_op jit(solution)/shard_map/ppermute | solution.py:45
  19.7 2.2 %collective-permute-start.2 = (bf16[24,768]{1,0:T(8,128)(2,1)S(1)}, bf16[24,768]{1,0:T(8,128)(2,1)S(1)}, u32[]{:S(2)}, u32[]{:S(2)}) collective-permute-start(bf16[24,768]{1,0:T(8,128)(2,1)S(1)} %get-tuple-element.38), channel_id=1, source_target_pairs={{0,384},{1,385},{2,386},{3,387},{4,388},{5,389},{6,390},{7,391},{8... | collective-permute-start | bytes 110600 | tf_op jit(solution)/shard_map/ppermute | solution.py:45
  21.9 1.5 %fusion.14.refs_0_ = bf16[192,768]{1,0:T(8,128)(2,1)S(1)} fusion(bf16[192,768]{1,0:T(8,128)(2,1)} %param.5, bf16[192,768]{1,0:T(8,128)(2,1)} %param.6), kind=kLoop, calls=%fused_computation.24 | loop fusion | flops 3096576 | bytes 884736 | tf_op jit(solution)/shard_map/convert_element_type | solution.py:158
  23.3 0.1 pad_add_fusion.place
  23.4 0.0 collective-permute-done
  23.4 0.0 collective-permute-done.1
  23.4 1.0 collective-permute-done.2
  24.4 2.1 %collective-permute-start.3 = (bf16[192,768]{1,0:T(8,128)(2,1)S(1)}, bf16[192,768]{1,0:T(8,128)(2,1)S(1)}, u32[]{:S(2)}, u32[]{:S(2)}) collective-permute-start(bf16[192,768]{1,0:T(8,128)(2,1)S(1)} %fusion.14.refs_0_), channel_id=1, source_target_pairs={{0,128},{1,129},{2,130},{3,131},{4,132},{5,133},{6,134},{7,135},{8... | collective-permute-start | bytes 884744 | tf_op jit(solution)/shard_map/ppermute | solution.py:45
  26.5 4.0 %collective-permute-start.4 = (bf16[192,768]{1,0:T(8,128)(2,1)S(1)}, bf16[192,768]{1,0:T(8,128)(2,1)S(1)}, u32[]{:S(2)}, u32[]{:S(2)}) collective-permute-start(bf16[192,768]{1,0:T(8,128)(2,1)S(1)} %fusion.14.refs_0_), channel_id=1, source_target_pairs={{0,256},{1,257},{2,258},{3,259},{4,260},{5,261},{6,262},{7,263},{8... | collective-permute-start | bytes 884744 | tf_op jit(solution)/shard_map/ppermute | solution.py:45
  30.6 2.9 %collective-permute-start.5 = (bf16[192,768]{1,0:T(8,128)(2,1)S(1)}, bf16[192,768]{1,0:T(8,128)(2,1)S(1)}, u32[]{:S(2)}, u32[]{:S(2)}) collective-permute-start(bf16[192,768]{1,0:T(8,128)(2,1)S(1)} %fusion.14.refs_0_), channel_id=1, source_target_pairs={{0,384},{1,385},{2,386},{3,387},{4,388},{5,389},{6,390},{7,391},{8... | collective-permute-start | bytes 884744 | tf_op jit(solution)/shard_map/ppermute | solution.py:45
  33.5 11.4 %all_gather.12 = bf16[4,96,768]{2,1,0:T(8,128)(2,1)S(1)} all-gather(bf16[4,24,768]{2,1,0:T(8,128)(2,1)S(1)} %pad_maximum_fusion.1), channel_id=1, replica_groups={{0,4,8,12},{1,5,9,13},{2,6,10,14},{3,7,11,15},{16,20,24,28},{17,21,25,2..., dimensions={1}, use_global_device_ids=true | all-gather | bytes 737280 | tf_op jit(solution)/shard_map/all_gather | solution.py:171
  44.9 8.2 %all_gather.13 = bf16[2,192,768]{2,1,0:T(8,128)(2,1)S(1)} all-gather(bf16[2,96,768]{2,1,0:T(8,128)(2,1)S(1)} %get-tuple-element.43), channel_id=1, replica_groups={{0,1},{2,3},{4,5},{6,7},{8,9},{10,11},{12,13},{14,15},{16,17},{18,19},{..., dimensions={1}, use_global_device_ids=true | all-gather | bytes 884736 | tf_op jit(solution)/shard_map/all_gather | solution.py:173
  53.2 2.2 %all_gather.14 = bf16[2,192,768]{2,1,0:T(8,128)(2,1)S(1)} all-gather(bf16[2,96,768]{2,1,0:T(8,128)(2,1)S(1)} %get-tuple-element.42), channel_id=1, replica_groups={{0,1},{2,3},{4,5},{6,7},{8,9},{10,11},{12,13},{14,15},{16,17},{18,19},{..., dimensions={1}, use_global_device_ids=true | all-gather | bytes 884736 | tf_op jit(solution)/shard_map/all_gather | solution.py:173
  55.4 0.0 collective-permute-done.3.refs_1_
  55.4 0.0 collective-permute-done.4.refs_2_
  55.4 0.0 collective-permute-done.5.refs_3_
  55.4 0.1 pad_maximum_fusion
  55.5 2.1 %convolution_convert_fusion = bf16[768,768]{1,0:T(8,128)(2,1)} fusion(bf16[768,768]{1,0:T(8,128)(2,1)S(1)} %bitcast.10, bf16[192,768]{1,0:T(8,128)(2,1)S(1)} %collective-permute-done.5.refs_3_, bf16[192,768]{1,0:T(8,128)(2,1)S(1)} %collective-permute-done.4.refs_2_, bf16[192,768]{1,0:T(8,128)(2,1)S(1)} %collective-permute-done.3.refs_1_, ...), kind=kOutput, calls=%fused_computation | convolution fusion | flops 911278080 | bytes 3538944 | tf_op jit(solution)/shard_map/dot_general | solution.py:179
  57.7 0.0 all-gather.2.cloned.1.call-done.refs_4_
  57.7 0.0 copy-start
  57.7 1.3 %copy-done = bf16[768,768]{1,0:T(8,128)(2,1)S(1)} copy-done((bf16[768,768]{1,0:T(8,128)(2,1)S(1)}, bf16[768,768]{1,0:T(8,128)(2,1)}, u32[]{:S(2)}) %copy-start) | copy-done | bytes 1179672
  58.9 1.9 %shard_map.59 = (bf16[4,4,48,384]{3,2,1,0:T(8,128)(2,1)S(1)}, bf16[4,4,48,384]{3,2,1,0:T(8,128)(2,1)S(1)}) custom-call(s32[2]{0:T(128)S(1)} %pad_add_fusion.place, bf16[192,768]{1,0:T(8,128)(2,1)S(1)} %fusion.14.refs_0_, bf16[192,768]{1,0:T(8,128)(2,1)S(1)} %collective-permute-done.3.refs_1_, bf16[192,768]{1,0:T(8,128)(2,1)S(1)} %collective-permute-done.4.refs_2_, ...), custom_call_target="tpu_custom_call" | custom-call | flops 905969664 | bytes 3538944 | tf_op jit(solution)/shard_map/pallas_call | solution.py:93
  60.9 2.3 %collective-permute-start.6 = (bf16[4,4,48,384]{3,2,1,0:T(8,128)(2,1)S(1)}, bf16[4,4,48,384]{3,2,1,0:T(8,128)(2,1)S(1)}, u32[]{:S(2)}, u32[]{:S(2)}) collective-permute-start(bf16[4,4,48,384]{3,2,1,0:T(8,128)(2,1)S(1)} %get-tuple-element.37), channel_id=1, source_target_pairs={{0,1},{1,0},{2,3},{3,2},{4,5},{5,4},{6,7},{7,6},{8,9},{9,8},{10,11... | collective-permute-start | bytes 1769480 | tf_op jit(solution)/shard_map/ppermute | solution.py:45
  63.2 0.0 reduce-scatter.2.cloned.1.call-update
  63.2 1.6 %collective-permute-done.6 = bf16[4,4,48,384]{3,2,1,0:T(8,128)(2,1)S(1)} collective-permute-done((bf16[4,4,48,384]{3,2,1,0:T(8,128)(2,1)S(1)}, bf16[4,4,48,384]{3,2,1,0:T(8,128)(2,1)S(1)}, u32[]{:S(2)}, u32[]{:S(2)}) %collective-permute-start.6) | collective-permute-done | bytes 589856 | tf_op jit(solution)/shard_map/ppermute | solution.py:45
  64.8 0.2 add_convert_fusion
  64.9 12.8 %all_to_all.15 = bf16[4,4,48,384]{3,2,1,0:T(8,128)(2,1)S(1)} all-to-all(bf16[4,4,48,384]{3,2,1,0:T(8,128)(2,1)S(1)} %add_convert_fusion), channel_id=1, replica_groups={{0,4,8,12},{1,5,9,13},{2,6,10,14},{3,7,11,15},{16,20,24,28},{17,21,25,2..., dimensions={0} | all-to-all | bytes 1179648 | tf_op jit(solution)/shard_map/all_to_all | solution.py:66
  77.7 0.1 reduce_sum.24
  77.8 17.6 %all_to_all.16 = bf16[8,48,384]{2,1,0:T(8,128)(2,1)S(1)} all-to-all(bf16[8,48,384]{2,1,0:T(8,128)(2,1)S(1)} %bitcast.12), channel_id=1, replica_groups={{0,128,256,384,2,130,258,386},{1,129,257,385,3,131,259,387},{4,132,260,..., dimensions={0} | all-to-all | bytes 589824 | tf_op jit(solution)/shard_map/all_to_all | solution.py:66
  95.5 0.1 reduce_sum.25
  95.5 0.1 broadcast_in_dim.5
  95.6 9.7 %all_to_all.17.mine = bf16[4,4,48,384]{3,2,1,0:T(8,128)(2,1)S(1)} all-to-all(bf16[4,4,48,384]{3,2,1,0:T(8,128)(2,1)S(1)} %broadcast_in_dim.5), channel_id=1, replica_groups={{0,4,8,12},{1,5,9,13},{2,6,10,14},{3,7,11,15},{16,20,24,28},{17,21,25,2..., dimensions={0} | all-to-all | bytes 1179648 | tf_op jit(solution)/shard_map/all_to_all | solution.py:66
  105.3 6.5 %collective-permute-start.7 = (bf16[4,4,48,384]{3,2,1,0:T(8,128)(2,1)S(1)}, bf16[4,4,48,384]{3,2,1,0:T(8,128)(2,1)S(1)}, u32[]{:S(2)}, u32[]{:S(2)}) collective-permute-start(bf16[4,4,48,384]{3,2,1,0:T(8,128)(2,1)S(1)} %all_to_all.17.mine), channel_id=1, source_target_pairs={{0,1},{1,0},{2,3},{3,2},{4,5},{5,4},{6,7},{7,6},{8,9},{9,8},{10,11... | collective-permute-start | bytes 1769480 | tf_op jit(solution)/shard_map/ppermute | solution.py:45
  111.8 0.0 reduce-scatter.2.cloned.1.call-done
  111.8 1.6 %multiply_convert_fusion = bf16[96,768]{1,0:T(8,128)(2,1)} fusion(bf16[96,768]{1,0:T(8,128)(2,1)} %reduce-scatter.2.cloned.1.call-done), kind=kLoop, calls=%fused_computation.26 | loop fusion | flops 221184 | bytes 294912 | tf_op jit(solution)/shard_map/convert_element_type | solution.py:189
  113.4 0.0 collective-permute-done.7.theirs
  113.4 1.1 shard_map.60
  (3 shorter events, 0.1 us)
Async XLA Ops:
  7.2 50.5 %all-gather.2.cloned.1.call-start = ((), (), s32[]{:S(2)}) async-start(), calls=%async_computation.5 | async-start | bytes 1327104 | tf_op jit(solution)/shard_map/all_gather | solution.py:157
  7.9 103.9 %reduce-scatter.2.cloned.1.call-start = ((), (), s32[]{:S(2)}) async-start(), calls=%async_computation.4 | async-start | bytes 1327104 | tf_op jit(solution)/shard_map/reduce_scatter | solution.py:186
  9.0 14.4 %collective-permute-start = (bf16[24,768]{1,0:T(8,128)(2,1)S(1)}, bf16[24,768]{1,0:T(8,128)(2,1)S(1)}, u32[]{:S(2)}, u32[]{:S(2)}) collective-permute-start(bf16[24,768]{1,0:T(8,128)(2,1)S(1)} %get-tuple-element.39), channel_id=1, source_target_pairs={{0,128},{1,129},{2,130},{3,131},{4,132},{5,133},{6,134},{7,135},{8... | collective-permute-start | bytes 110600 | tf_op jit(solution)/shard_map/ppermute | solution.py:45
  13.9 9.6 %collective-permute-start.1 = (bf16[24,768]{1,0:T(8,128)(2,1)S(1)}, bf16[24,768]{1,0:T(8,128)(2,1)S(1)}, u32[]{:S(2)}, u32[]{:S(2)}) collective-permute-start(bf16[24,768]{1,0:T(8,128)(2,1)S(1)} %get-tuple-element.41), channel_id=1, source_target_pairs={{0,256},{1,257},{2,258},{3,259},{4,260},{5,261},{6,262},{7,263},{8... | collective-permute-start | bytes 110600 | tf_op jit(solution)/shard_map/ppermute | solution.py:45
  19.7 4.7 %collective-permute-start.2 = (bf16[24,768]{1,0:T(8,128)(2,1)S(1)}, bf16[24,768]{1,0:T(8,128)(2,1)S(1)}, u32[]{:S(2)}, u32[]{:S(2)}) collective-permute-start(bf16[24,768]{1,0:T(8,128)(2,1)S(1)} %get-tuple-element.38), channel_id=1, source_target_pairs={{0,384},{1,385},{2,386},{3,387},{4,388},{5,389},{6,390},{7,391},{8... | collective-permute-start | bytes 110600 | tf_op jit(solution)/shard_map/ppermute | solution.py:45
  24.4 31.0 %collective-permute-start.3 = (bf16[192,768]{1,0:T(8,128)(2,1)S(1)}, bf16[192,768]{1,0:T(8,128)(2,1)S(1)}, u32[]{:S(2)}, u32[]{:S(2)}) collective-permute-start(bf16[192,768]{1,0:T(8,128)(2,1)S(1)} %fusion.14.refs_0_), channel_id=1, source_target_pairs={{0,128},{1,129},{2,130},{3,131},{4,132},{5,133},{6,134},{7,135},{8... | collective-permute-start | bytes 884744 | tf_op jit(solution)/shard_map/ppermute | solution.py:45
  26.5 28.9 %collective-permute-start.4 = (bf16[192,768]{1,0:T(8,128)(2,1)S(1)}, bf16[192,768]{1,0:T(8,128)(2,1)S(1)}, u32[]{:S(2)}, u32[]{:S(2)}) collective-permute-start(bf16[192,768]{1,0:T(8,128)(2,1)S(1)} %fusion.14.refs_0_), channel_id=1, source_target_pairs={{0,256},{1,257},{2,258},{3,259},{4,260},{5,261},{6,262},{7,263},{8... | collective-permute-start | bytes 884744 | tf_op jit(solution)/shard_map/ppermute | solution.py:45
  30.6 24.9 %collective-permute-start.5 = (bf16[192,768]{1,0:T(8,128)(2,1)S(1)}, bf16[192,768]{1,0:T(8,128)(2,1)S(1)}, u32[]{:S(2)}, u32[]{:S(2)}) collective-permute-start(bf16[192,768]{1,0:T(8,128)(2,1)S(1)} %fusion.14.refs_0_), channel_id=1, source_target_pairs={{0,384},{1,385},{2,386},{3,387},{4,388},{5,389},{6,390},{7,391},{8... | collective-permute-start | bytes 884744 | tf_op jit(solution)/shard_map/ppermute | solution.py:45
  57.7 1.3 %copy-start = (bf16[768,768]{1,0:T(8,128)(2,1)S(1)}, bf16[768,768]{1,0:T(8,128)(2,1)}, u32[]{:S(2)}) copy-start(bf16[768,768]{1,0:T(8,128)(2,1)} %all-gather.2.cloned.1.call-done.refs_4_) | copy-start | bytes 3538948
  60.9 3.9 %collective-permute-start.6 = (bf16[4,4,48,384]{3,2,1,0:T(8,128)(2,1)S(1)}, bf16[4,4,48,384]{3,2,1,0:T(8,128)(2,1)S(1)}, u32[]{:S(2)}, u32[]{:S(2)}) collective-permute-start(bf16[4,4,48,384]{3,2,1,0:T(8,128)(2,1)S(1)} %get-tuple-element.37), channel_id=1, source_target_pairs={{0,1},{1,0},{2,3},{3,2},{4,5},{5,4},{6,7},{7,6},{8,9},{9,8},{10,11... | collective-permute-start | bytes 1769480 | tf_op jit(solution)/shard_map/ppermute | solution.py:45
  105.3 8.1 %collective-permute-start.7 = (bf16[4,4,48,384]{3,2,1,0:T(8,128)(2,1)S(1)}, bf16[4,4,48,384]{3,2,1,0:T(8,128)(2,1)S(1)}, u32[]{:S(2)}, u32[]{:S(2)}) collective-permute-start(bf16[4,4,48,384]{3,2,1,0:T(8,128)(2,1)S(1)} %all_to_all.17.mine), channel_id=1, source_target_pairs={{0,1},{1,0},{2,3},{3,2},{4,5},{5,4},{6,7},{7,6},{8,9},{9,8},{10,11... | collective-permute-start | bytes 1769480 | tf_op jit(solution)/shard_map/ppermute | solution.py:45
Sparse Core Ops, SparseCore 0:
  10.1 42.9 all-gather.1
  63.3 38.2 reduce-scatter.1

commit v6 on v5

--- a/solution.py
+++ b/solution.py
@@ -20,6 +20,7 @@
     return (x * Z_HI + h) * CORE + c
 
 
+Z_GROUPS = [[fsdp_index(z, y) for z in range(Z_LO)] for y in range(Y)]
 Y_GROUPS = [[fsdp_index(z, y) for y in range(Y)] for z in range(Z_LO)]
 C_GROUPS = [[mp_index(x, h, c) for c in range(CORE)] for x in range(X) for h in range(Z_HI)]
 X_GROUPS = [[mp_index(x, h, c) for x in range(X)] for h in range(Z_HI) for c in range(CORE)]
@@ -64,6 +65,21 @@
 
 def swap(blocks, axis, groups):
     return lax.all_to_all(blocks, axis, 0, 0, axis_index_groups=groups, tiled=True)
+
+
+def by_distance_kernel(place, blocks, out):
+    for k in range(Z_LO):
+        out[k] = blocks[jnp.bitwise_and(place[0] + (Z_LO - k), Z_LO - 1)]
+
+
+def by_distance(place, blocks):
+    return pl.pallas_call(
+        by_distance_kernel,
+        in_specs=[pl.BlockSpec(memory_space=pltpu.SMEM), pl.BlockSpec(memory_space=pltpu.VMEM)],
+        out_specs=pl.BlockSpec(memory_space=pltpu.VMEM),
+        out_shape=jax.ShapeDtypeStruct(blocks.shape, blocks.dtype),
+        cost_estimate=pl.CostEstimate(flops=0, bytes_accessed=4 * blocks.size, transcendentals=0),
+    )(place, blocks)
 
 
 def input_parts_kernel(place, *refs):
@@ -160,14 +176,10 @@
     )
     part = rows // (CORE * X)
     mine = lax.dynamic_slice_in_dim(tokens, (core * X + x) * part, part, 0)
-    mine = [
-        lax.dynamic_slice_in_dim(mine, jnp.bitwise_and(z_lo + k, Z_LO - 1) * quarter, quarter, 1)
-        for k in range(Z_LO)
-    ]
-    mine = [mine[0]] + [along_z_lo(mine[k], k) for k in range(1, Z_LO)]
+    mine = swap(mine.reshape(part, Z_LO, quarter).transpose(1, 0, 2), "fsdp", Z_GROUPS)
     mine, hidden_grad = lax.optimization_barrier((mine, hidden_grad))
     hidden = [hidden_grad] + [along_z_lo(hidden_grad, k) for k in range(1, Z_LO)]
-    mine = jnp.stack(mine)
+    mine = by_distance(z_lo.reshape(1), mine)
     mine = lax.all_gather(mine, "mp", axis=1, axis_index_groups=X_GROUPS, tiled=True)
     patches = [
         lax.all_gather(mine[k : k + 2], "mp", axis=1, axis_index_groups=C_GROUPS, tiled=True)

time: 122 us -> 121 us (level)
  starting transfers between devices: 30.7 us -> 26.4 us
  waiting for transfers between devices: 3.33 us -> 6.63 us
  Pallas kernels: 3.05 us -> 4.63 us
    ppermute x8 -> x5, starting transfers between devices: 30.6 us -> 18.6 us  [moved(): return lax.ppermute(value, AXES, pairs)]
    all_to_all x0 -> x1, starting transfers between devices: none -> 7.81 us  [swap(): lax.all_to_all(blocks, axis, 0, 0, axis_index_groups=groups, tiled=True)]
    all_to_all x0 -> x1, waiting for transfers between devices: none -> 4.31 us  [swap(): lax.all_to_all(blocks, axis, 0, 0, axis_index_groups=groups, tiled=True)]
    pallas_call x0 -> x1, Pallas kernels: none -> 1.59 us  [by_distance(): pl.pallas_call(by_distance_kernel, in_specs=[pl.BlockSpec(memory_space=pl...]
    ppermute x8 -> x5, waiting for transfers between devices: 2.61 us -> 1.59 us  [moved(): return lax.ppermute(value, AXES, pairs)]
  transfers between devices with their start and end apart: 10 -> 8, of which waited for: 2 -> 2; matrix products, arithmetic and copies ran while one was open for 6% -> 5% of each run, Pallas kernels for 0% -> 1%
where the time goes in v6:
time: 121 us
  blocking collectives  61.6 us (51%)
  starting transfers between devices  26.4 us (22%)
  between operations  14.2 us (12%)
  waiting for transfers between devices  6.63 us (5%)
  Pallas kernels  4.63 us (4%)
  local copies, waits for them, and re-layouts  2.59 us (2%)
  other arithmetic  2.5 us (2%)
  matrix products  2.14 us (2%)
    all_to_all x3, blocking collectives, swap(): lax.all_to_all(blocks, axis, 0, 0, axis_index_groups=groups, tiled=True)  40 us
    ppermute x5, starting transfers between devices, moved(): return lax.ppermute(value, AXES, pairs)  18.6 us
    all_gather x1, blocking collectives, shards(): lax.all_gather(mine, 'mp', axis=1, axis_index_groups=X_GROUPS, tiled=True)  11.3 us
    all_gather x2, blocking collectives, shards(): lax.all_gather(mine[k:k + 2], 'mp', axis=1, axis_index_groups=C_GROUPS, t...  10.3 us
    all_to_all x1, starting transfers between devices, swap(): lax.all_to_all(blocks, axis, 0, 0, axis_index_groups=groups, tiled=True)  7.81 us
    all_to_all x1, waiting for transfers between devices, swap(): lax.all_to_all(blocks, axis, 0, 0, axis_index_groups=groups, tiled=True)  4.31 us
  transfers between devices with their start and end apart: 8, of which 2 were waited for; matrix products, arithmetic and copies ran while one was open for 5% of the time, Pallas kernels for 1%

profile of v6, /device:TPU:1, one launch (start us, length us, event | category | flops | bytes accessed | tf_op | source)
XLA Modules:
  0.0 120.7 jit_solution(1081206654728342728)
XLA Ops:
  7.2 0.0 copy-start
  7.2 0.0 copy-start.3
  7.2 0.0 copy-start.4
  7.2 0.0 all-gather.2.cloned.1.call-start
  7.2 0.7 all-gather.2.cloned.1.call-update
  7.9 0.5 copy-done
  8.5 0.7 copy.10
  9.1 7.8 %all-to-all-start = ((bf16[4,24,768]{2,1,0:T(8,128)(2,1)}), bf16[4,24,768]{2,1,0:T(8,128)(2,1)S(1)}, u32[]{:S(2)}, u32[]{:S(2)}) async-start(bf16[4,24,768]{2,1,0:T(8,128)(2,1)} %bitcast.12), calls=%async_computation | async-start | bytes 294912 | tf_op jit(solution)/shard_map/all_to_all | solution.py:67
  16.9 0.0 reduce-scatter.2.cloned.1.call-start
  16.9 0.1 pad_add_fusion.place
  17.0 0.0 copy-done.3
  17.0 0.0 copy-done.4
  17.0 0.4 fusion.14.refs_0_
  17.4 4.3 %all-to-all-done.blocks = bf16[4,24,768]{2,1,0:T(8,128)(2,1)S(1)} async-done(((bf16[4,24,768]{2,1,0:T(8,128)(2,1)}), bf16[4,24,768]{2,1,0:T(8,128)(2,1)S(1)}, u32[]{:S(2)}, u32[]{:S(2)}) %all-to-all-start) | async-done | bytes 147488 | tf_op jit(solution)/shard_map/all_to_all | solution.py:67
  21.7 0.0 copy-start.2
  21.8 3.0 %collective-permute-start = (bf16[192,768]{1,0:T(8,128)(2,1)S(1)}, bf16[192,768]{1,0:T(8,128)(2,1)S(1)}, u32[]{:S(2)}, u32[]{:S(2)}) collective-permute-start(bf16[192,768]{1,0:T(8,128)(2,1)S(1)} %fusion.14.refs_0_), channel_id=1, source_target_pairs={{0,128},{1,129},{2,130},{3,131},{4,132},{5,133},{6,134},{7,135},{8... | collective-permute-start | bytes 884744 | tf_op jit(solution)/shard_map/ppermute | solution.py:46
  24.7 2.6 %collective-permute-start.1 = (bf16[192,768]{1,0:T(8,128)(2,1)S(1)}, bf16[192,768]{1,0:T(8,128)(2,1)S(1)}, u32[]{:S(2)}, u32[]{:S(2)}) collective-permute-start(bf16[192,768]{1,0:T(8,128)(2,1)S(1)} %fusion.14.refs_0_), channel_id=1, source_target_pairs={{0,256},{1,257},{2,258},{3,259},{4,260},{5,261},{6,262},{7,263},{8... | collective-permute-start | bytes 884744 | tf_op jit(solution)/shard_map/ppermute | solution.py:46
  27.3 3.4 %collective-permute-start.2 = (bf16[192,768]{1,0:T(8,128)(2,1)S(1)}, bf16[192,768]{1,0:T(8,128)(2,1)S(1)}, u32[]{:S(2)}, u32[]{:S(2)}) collective-permute-start(bf16[192,768]{1,0:T(8,128)(2,1)S(1)} %fusion.14.refs_0_), channel_id=1, source_target_pairs={{0,384},{1,385},{2,386},{3,387},{4,388},{5,389},{6,390},{7,391},{8... | collective-permute-start | bytes 884744 | tf_op jit(solution)/shard_map/ppermute | solution.py:46
  30.8 0.0 copy-done.2
  30.8 1.6 %shard_map.59 = bf16[4,24,768]{2,1,0:T(8,128)(2,1)} custom-call(s32[1]{0:T(128)} %bitcast.place, bf16[4,24,768]{2,1,0:T(8,128)(2,1)} %copy-done.2), custom_call_target="tpu_custom_call" | custom-call | bytes 294912 | tf_op jit(solution)/shard_map/pallas_call | solution.py:76
  32.4 11.3 %all_gather.12 = bf16[4,96,768]{2,1,0:T(8,128)(2,1)S(1)} all-gather(bf16[4,24,768]{2,1,0:T(8,128)(2,1)} %shard_map.59), channel_id=1, replica_groups={{0,4,8,12},{1,5,9,13},{2,6,10,14},{3,7,11,15},{16,20,24,28},{17,21,25,2..., dimensions={1}, use_global_device_ids=true | all-gather | bytes 737280 | tf_op jit(solution)/shard_map/all_gather | solution.py:183
  43.7 8.1 %all_gather.13 = bf16[2,192,768]{2,1,0:T(8,128)(2,1)S(1)} all-gather(bf16[2,96,768]{2,1,0:T(8,128)(2,1)S(1)} %get-tuple-element.33), channel_id=1, replica_groups={{0,1},{2,3},{4,5},{6,7},{8,9},{10,11},{12,13},{14,15},{16,17},{18,19},{..., dimensions={1}, use_global_device_ids=true | all-gather | bytes 884736 | tf_op jit(solution)/shard_map/all_gather | solution.py:185
  51.8 2.2 %all_gather.14 = bf16[2,192,768]{2,1,0:T(8,128)(2,1)S(1)} all-gather(bf16[2,96,768]{2,1,0:T(8,128)(2,1)S(1)} %get-tuple-element.32), channel_id=1, replica_groups={{0,1},{2,3},{4,5},{6,7},{8,9},{10,11},{12,13},{14,15},{16,17},{18,19},{..., dimensions={1}, use_global_device_ids=true | all-gather | bytes 884736 | tf_op jit(solution)/shard_map/all_gather | solution.py:185
  54.0 0.0 collective-permute-done.refs_1_
  54.0 0.0 collective-permute-done.1.refs_2_
  54.0 0.0 collective-permute-done.2.refs_3_
  54.0 0.1 pad_maximum_fusion
  54.1 2.1 %convolution_convert_fusion = bf16[768,768]{1,0:T(8,128)(2,1)} fusion(bf16[768,768]{1,0:T(8,128)(2,1)S(1)} %bitcast.13, bf16[192,768]{1,0:T(8,128)(2,1)S(1)} %collective-permute-done.2.refs_3_, bf16[192,768]{1,0:T(8,128)(2,1)S(1)} %collective-permute-done.1.refs_2_, bf16[192,768]{1,0:T(8,128)(2,1)S(1)} %collective-permute-done.refs_1_, ...), kind=kOutput, calls=%fused_computation | convolution fusion | flops 911278080 | bytes 3538944 | tf_op jit(solution)/shard_map/dot_general | solution.py:191
  56.3 0.0 all-gather.2.cloned.1.call-done.refs_4_
  56.3 0.0 copy-start.1
  56.3 1.3 %copy-done.1 = bf16[768,768]{1,0:T(8,128)(2,1)S(1)} copy-done((bf16[768,768]{1,0:T(8,128)(2,1)S(1)}, bf16[768,768]{1,0:T(8,128)(2,1)}, u32[]{:S(2)}) %copy-start.1) | copy-done | bytes 1179672
  57.5 1.9 %shard_map.60 = (bf16[4,4,48,384]{3,2,1,0:T(8,128)(2,1)S(1)}, bf16[4,4,48,384]{3,2,1,0:T(8,128)(2,1)S(1)}) custom-call(s32[2]{0:T(128)S(1)} %pad_add_fusion.place, bf16[192,768]{1,0:T(8,128)(2,1)S(1)} %fusion.14.refs_0_, bf16[192,768]{1,0:T(8,128)(2,1)S(1)} %collective-permute-done.refs_1_, bf16[192,768]{1,0:T(8,128)(2,1)S(1)} %collective-permute-done.1.refs_2_, ...), custom_call_target="tpu_custom_call" | custom-call | flops 905969664 | bytes 3538944 | tf_op jit(solution)/shard_map/pallas_call | solution.py:109
  59.5 3.1 %collective-permute-start.3 = (bf16[4,4,48,384]{3,2,1,0:T(8,128)(2,1)S(1)}, bf16[4,4,48,384]{3,2,1,0:T(8,128)(2,1)S(1)}, u32[]{:S(2)}, u32[]{:S(2)}) collective-permute-start(bf16[4,4,48,384]{3,2,1,0:T(8,128)(2,1)S(1)} %get-tuple-element.31), channel_id=1, source_target_pairs={{0,1},{1,0},{2,3},{3,2},{4,5},{5,4},{6,7},{7,6},{8,9},{9,8},{10,11... | collective-permute-start | bytes 1769480 | tf_op jit(solution)/shard_map/ppermute | solution.py:46
  62.6 0.0 reduce-scatter.2.cloned.1.call-update
  62.6 1.6 %collective-permute-done.3 = bf16[4,4,48,384]{3,2,1,0:T(8,128)(2,1)S(1)} collective-permute-done((bf16[4,4,48,384]{3,2,1,0:T(8,128)(2,1)S(1)}, bf16[4,4,48,384]{3,2,1,0:T(8,128)(2,1)S(1)}, u32[]{:S(2)}, u32[]{:S(2)}) %collective-permute-start.3) | collective-permute-done | bytes 589856 | tf_op jit(solution)/shard_map/ppermute | solution.py:46
  64.2 0.2 add_convert_fusion
  64.4 13.4 %all_to_all.20 = bf16[4,4,48,384]{3,2,1,0:T(8,128)(2,1)S(1)} all-to-all(bf16[4,4,48,384]{3,2,1,0:T(8,128)(2,1)S(1)} %add_convert_fusion), channel_id=1, replica_groups={{0,4,8,12},{1,5,9,13},{2,6,10,14},{3,7,11,15},{16,20,24,28},{17,21,25,2..., dimensions={0} | all-to-all | bytes 1179648 | tf_op jit(solution)/shard_map/all_to_all | solution.py:67
  77.7 0.1 reduce_sum.24
  77.9 17.0 %all_to_all.21 = bf16[8,48,384]{2,1,0:T(8,128)(2,1)S(1)} all-to-all(bf16[8,48,384]{2,1,0:T(8,128)(2,1)S(1)} %bitcast.15), channel_id=1, replica_groups={{0,128,256,384,2,130,258,386},{1,129,257,385,3,131,259,387},{4,132,260,..., dimensions={0} | all-to-all | bytes 589824 | tf_op jit(solution)/shard_map/all_to_all | solution.py:67
  94.9 0.1 reduce_sum.25
  94.9 0.1 broadcast_in_dim.5
  95.0 9.7 %all_to_all.22.mine = bf16[4,4,48,384]{3,2,1,0:T(8,128)(2,1)S(1)} all-to-all(bf16[4,4,48,384]{3,2,1,0:T(8,128)(2,1)S(1)} %broadcast_in_dim.5), channel_id=1, replica_groups={{0,4,8,12},{1,5,9,13},{2,6,10,14},{3,7,11,15},{16,20,24,28},{17,21,25,2..., dimensions={0} | all-to-all | bytes 1179648 | tf_op jit(solution)/shard_map/all_to_all | solution.py:67
  104.6 6.5 %collective-permute-start.4 = (bf16[4,4,48,384]{3,2,1,0:T(8,128)(2,1)S(1)}, bf16[4,4,48,384]{3,2,1,0:T(8,128)(2,1)S(1)}, u32[]{:S(2)}, u32[]{:S(2)}) collective-permute-start(bf16[4,4,48,384]{3,2,1,0:T(8,128)(2,1)S(1)} %all_to_all.22.mine), channel_id=1, source_target_pairs={{0,1},{1,0},{2,3},{3,2},{4,5},{5,4},{6,7},{7,6},{8,9},{9,8},{10,11... | collective-permute-start | bytes 1769480 | tf_op jit(solution)/shard_map/ppermute | solution.py:46
  111.1 0.0 reduce-scatter.2.cloned.1.call-done
  111.2 1.6 %multiply_convert_fusion = bf16[96,768]{1,0:T(8,128)(2,1)} fusion(bf16[96,768]{1,0:T(8,128)(2,1)} %reduce-scatter.2.cloned.1.call-done), kind=kLoop, calls=%fused_computation.26 | loop fusion | flops 221184 | bytes 294912 | tf_op jit(solution)/shard_map/convert_element_type | solution.py:201
  112.8 0.0 collective-permute-done.4.theirs
  112.8 1.1 shard_map.61
  (3 shorter events, 0.1 us)
Async XLA Ops:
  7.2 1.3 %copy-start = (bf16[192,3072]{1,0:T(8,128)(2,1)S(1)}, bf16[192,3072]{1,0:T(8,128)(2,1)}, u32[]{:S(2)}) copy-start(bf16[192,3072]{1,0:T(8,128)(2,1)} %param.4) | copy-start | bytes 3538948
  7.2 9.8 %copy-start.3 = (bf16[192,768]{1,0:T(8,128)(2,1)S(1)}, bf16[192,768]{1,0:T(8,128)(2,1)}, u32[]{:S(2)}) copy-start(bf16[192,768]{1,0:T(8,128)(2,1)} %param.5) | copy-start | bytes 884740
  7.2 9.8 %copy-start.4 = (bf16[192,768]{1,0:T(8,128)(2,1)S(1)}, bf16[192,768]{1,0:T(8,128)(2,1)}, u32[]{:S(2)}) copy-start(bf16[192,768]{1,0:T(8,128)(2,1)} %param.6) | copy-start | bytes 884740
  7.2 49.1 %all-gather.2.cloned.1.call-start = ((), (), s32[]{:S(2)}) async-start(), calls=%async_computation.6 | async-start | bytes 1327104 | tf_op jit(solution)/shard_map/all_gather | solution.py:173
  9.1 12.6 %all-to-all-start = ((bf16[4,24,768]{2,1,0:T(8,128)(2,1)}), bf16[4,24,768]{2,1,0:T(8,128)(2,1)S(1)}, u32[]{:S(2)}, u32[]{:S(2)}) async-start(bf16[4,24,768]{2,1,0:T(8,128)(2,1)} %bitcast.12), calls=%async_computation | async-start | bytes 294912 | tf_op jit(solution)/shard_map/all_to_all | solution.py:67
  16.9 94.2 %reduce-scatter.2.cloned.1.call-start = ((), (), s32[]{:S(2)}) async-start(), calls=%async_computation.5 | async-start | bytes 1327104 | tf_op jit(solution)/shard_map/reduce_scatter | solution.py:198
  21.7 9.0 %copy-start.2 = (bf16[4,24,768]{2,1,0:T(8,128)(2,1)}, bf16[4,24,768]{2,1,0:T(8,128)(2,1)S(1)}, u32[]{:S(2)}) copy-start(bf16[4,24,768]{2,1,0:T(8,128)(2,1)S(1)} %all-to-all-done.blocks) | copy-start | bytes 442372
  21.8 32.3 %collective-permute-start = (bf16[192,768]{1,0:T(8,128)(2,1)S(1)}, bf16[192,768]{1,0:T(8,128)(2,1)S(1)}, u32[]{:S(2)}, u32[]{:S(2)}) collective-permute-start(bf16[192,768]{1,0:T(8,128)(2,1)S(1)} %fusion.14.refs_0_), channel_id=1, source_target_pairs={{0,128},{1,129},{2,130},{3,131},{4,132},{5,133},{6,134},{7,135},{8... | collective-permute-start | bytes 884744 | tf_op jit(solution)/shard_map/ppermute | solution.py:46
  24.7 29.3 %collective-permute-start.1 = (bf16[192,768]{1,0:T(8,128)(2,1)S(1)}, bf16[192,768]{1,0:T(8,128)(2,1)S(1)}, u32[]{:S(2)}, u32[]{:S(2)}) collective-permute-start(bf16[192,768]{1,0:T(8,128)(2,1)S(1)} %fusion.14.refs_0_), channel_id=1, source_target_pairs={{0,256},{1,257},{2,258},{3,259},{4,260},{5,261},{6,262},{7,263},{8... | collective-permute-start | bytes 884744 | tf_op jit(solution)/shard_map/ppermute | solution.py:46
  27.3 26.7 %collective-permute-start.2 = (bf16[192,768]{1,0:T(8,128)(2,1)S(1)}, bf16[192,768]{1,0:T(8,128)(2,1)S(1)}, u32[]{:S(2)}, u32[]{:S(2)}) collective-permute-start(bf16[192,768]{1,0:T(8,128)(2,1)S(1)} %fusion.14.refs_0_), channel_id=1, source_target_pairs={{0,384},{1,385},{2,386},{3,387},{4,388},{5,389},{6,390},{7,391},{8... | collective-permute-start | bytes 884744 | tf_op jit(solution)/shard_map/ppermute | solution.py:46
  56.3 1.3 %copy-start.1 = (bf16[768,768]{1,0:T(8,128)(2,1)S(1)}, bf16[768,768]{1,0:T(8,128)(2,1)}, u32[]{:S(2)}) copy-start(bf16[768,768]{1,0:T(8,128)(2,1)} %all-gather.2.cloned.1.call-done.refs_4_) | copy-start | bytes 3538948
  59.5 4.7 %collective-permute-start.3 = (bf16[4,4,48,384]{3,2,1,0:T(8,128)(2,1)S(1)}, bf16[4,4,48,384]{3,2,1,0:T(8,128)(2,1)S(1)}, u32[]{:S(2)}, u32[]{:S(2)}) collective-permute-start(bf16[4,4,48,384]{3,2,1,0:T(8,128)(2,1)S(1)} %get-tuple-element.31), channel_id=1, source_target_pairs={{0,1},{1,0},{2,3},{3,2},{4,5},{5,4},{6,7},{7,6},{8,9},{9,8},{10,11... | collective-permute-start | bytes 1769480 | tf_op jit(solution)/shard_map/ppermute | solution.py:46
  104.6 8.1 %collective-permute-start.4 = (bf16[4,4,48,384]{3,2,1,0:T(8,128)(2,1)S(1)}, bf16[4,4,48,384]{3,2,1,0:T(8,128)(2,1)S(1)}, u32[]{:S(2)}, u32[]{:S(2)}) collective-permute-start(bf16[4,4,48,384]{3,2,1,0:T(8,128)(2,1)S(1)} %all_to_all.22.mine), channel_id=1, source_target_pairs={{0,1},{1,0},{2,3},{3,2},{4,5},{5,4},{6,7},{7,6},{8,9},{9,8},{10,11... | collective-permute-start | bytes 1769480 | tf_op jit(solution)/shard_map/ppermute | solution.py:46
Sparse Core Ops, SparseCore 0:
  10.1 42.9 all-gather.1
  62.7 36.1 reduce-scatter.1

commit v7 on v6

--- a/solution.py
+++ b/solution.py
@@ -82,43 +82,45 @@
     )(place, blocks)
 
 
-def input_parts_kernel(place, *refs):
-    blocks, weight, outs = refs[:Z_LO], refs[Z_LO], refs[Z_LO + 1 :]
+def input_part_kernel(place, *refs):
+    blocks, weight, out, chosen, arrived = refs[:Z_LO], refs[Z_LO], refs[-3], refs[-2], refs[-1]
     rows = blocks[0].shape[0]
     piece = rows // X
-    half = weight.shape[0] // CORE
+    half = chosen.shape[0]
+    copy = pltpu.make_async_copy(
+        weight.at[pl.ds(pl.multiple_of(place[1] * half, half), half)], chosen, arrived
+    )
+    copy.start()
     lhs = jnp.concatenate([block[...] for block in blocks], axis=0)
-    for out, which in zip(outs, (1 - place[1], place[1])):
-        result = lax.dot_general(
-            lhs,
-            weight[pl.ds(pl.multiple_of(which * half, half), half), :],
-            (((1,), (1,)), ((), ())),
-            preferred_element_type=jnp.float32,
-        )
-        for k in range(Z_LO):
-            owner = jnp.bitwise_and(place[0] + (Z_LO - k), Z_LO - 1)
-            for x in range(X):
-                start = k * rows + x * piece
-                out[x, owner] = result[start : start + piece].astype(out.dtype)
-
-
-def input_parts(place, blocks, weight):
+    copy.wait()
+    result = lax.dot_general(
+        lhs, chosen[...], (((1,), (1,)), ((), ())), preferred_element_type=jnp.float32
+    )
+    for k in range(Z_LO):
+        owner = jnp.bitwise_and(place[0] + (Z_LO - k), Z_LO - 1)
+        for x in range(X):
+            start = k * rows + x * piece
+            out[x, owner] = result[start : start + piece].astype(out.dtype)
+
+
+def input_part(place, blocks, weight):
     rows, units = blocks[0].shape
     half = weight.shape[0] // CORE
-    out = jax.ShapeDtypeStruct((X, Z_LO, rows // X, half), jnp.bfloat16)
     return pl.pallas_call(
-        input_parts_kernel,
+        input_part_kernel,
         in_specs=[pl.BlockSpec(memory_space=pltpu.SMEM)]
-        + [pl.BlockSpec(memory_space=pltpu.VMEM)] * (Z_LO + 1),
-        out_specs=[pl.BlockSpec(memory_space=pltpu.VMEM)] * 2,
-        out_shape=[out, out],
+        + [pl.BlockSpec(memory_space=pltpu.VMEM)] * Z_LO
+        + [pl.BlockSpec(memory_space=pltpu.HBM)],
+        out_specs=pl.BlockSpec(memory_space=pltpu.VMEM),
+        out_shape=jax.ShapeDtypeStruct((X, Z_LO, rows // X, half), jnp.bfloat16),
+        scratch_shapes=[pltpu.VMEM((half, units), jnp.bfloat16), pltpu.SemaphoreType.DMA],
         compiler_params=pltpu.CompilerParams(vmem_limit_bytes=32 * 1024 * 1024),
         cost_estimate=pl.CostEstimate(
-            flops=4 * Z_LO * rows * units * half,
-            bytes_accessed=2 * (Z_LO * rows * units + 2 * half * units + 2 * Z_LO * rows * half),
+            flops=2 * Z_LO * rows * units * half,
+            bytes_accessed=2 * (Z_LO * rows * units + half * units + Z_LO * rows * half),
             transcendentals=0,
         ),
-    )(place, *blocks, weight)
+    )(place, *blocks, pltpu.with_memory_space_constraint(weight, pltpu.HBM))
 
 
 def joined_kernel(core, mine, theirs, out):
@@ -168,6 +170,7 @@
     z_lo = lax.shift_right_logical(lax.axis_index("fsdp"), 3)
     x = lax.shift_right_logical(lax.axis_index("mp"), 2)
     core = jnp.bitwise_and(lax.axis_index("mp"), 1)
+    theirs_place = jnp.stack([z_lo, 1 - core])
     own_place = jnp.stack([z_lo, core])
 
     weight = lax.all_gather(w_up, "fsdp", axis=0, axis_index_groups=Y_GROUPS, tiled=True)
@@ -200,9 +203,9 @@
     )
     grad_weight = (received.astype(jnp.float32) * norm_factor).astype(jnp.bfloat16)
 
-    for_other, for_own = input_parts(own_place, hidden, weight)
-    theirs = to_other_core(for_other)
-    partial = (for_own.astype(jnp.float32) + theirs.astype(jnp.float32)).astype(jnp.bfloat16)
+    theirs = to_other_core(input_part(theirs_place, hidden, weight))
+    partial = input_part(own_place, hidden, weight)
+    partial = (partial.astype(jnp.float32) + theirs.astype(jnp.float32)).astype(jnp.bfloat16)
     partial = total(swap(partial, "mp", X_GROUPS))
     both = jnp.broadcast_to(partial[None], (Z_HI, Z_LO, piece, half))
     both = swap(both.reshape(Z_HI * Z_LO, piece, half), AXES, RING_GROUPS)

time: 121 us -> 122 us (level)
  Pallas kernels: 4.63 us -> 7.53 us
  waiting for transfers between devices: 6.63 us -> 5.05 us
  local copies, waits for them, and re-layouts: 2.59 us -> 1.32 us
    pallas_call x1 -> x2, Pallas kernels: 1.93 us -> 4.83 us  [input_part(): pl.pallas_call(input_part_kernel, in_specs=[pl.BlockSpec(memory_space=plt...]
    ppermute x5, waiting for transfers between devices: 1.59 us -> 0.01 us  [moved(): return lax.ppermute(value, AXES, pairs)]
    unnamed x10 -> x8, local copies, waits for them, and re-layouts: 1.79 us -> 0.52 us
  transfers between devices with their start and end apart: 8 -> 8, of which waited for: 2 -> 1; matrix products, arithmetic and copies ran while one was open for 5% -> 5% of each run, Pallas kernels for 1% -> 3%
where the time goes in v7:
time: 122 us; the launch traced here: 121 us
  blocking collectives  62 us (51%)
  starting transfers between devices  26.1 us (21%)
  between operations  14.2 us (12%)
  Pallas kernels  7.53 us (6%)
  waiting for transfers between devices  5.05 us (4%)
  other arithmetic  2.58 us (2%)
  matrix products  2.14 us (2%)
  local copies, waits for them, and re-layouts  1.32 us (1%)
    all_to_all x3, blocking collectives, swap(): lax.all_to_all(blocks, axis, 0, 0, axis_index_groups=groups, tiled=True)  40.4 us
    ppermute x5, starting transfers between devices, moved(): return lax.ppermute(value, AXES, pairs)  18.3 us
    all_gather x1, blocking collectives, shards(): lax.all_gather(mine, 'mp', axis=1, axis_index_groups=X_GROUPS, tiled=True)  11.3 us
    all_gather x2, blocking collectives, shards(): lax.all_gather(mine[k:k + 2], 'mp', axis=1, axis_index_groups=C_GROUPS, t...  10.3 us
    all_to_all x1, starting transfers between devices, swap(): lax.all_to_all(blocks, axis, 0, 0, axis_index_groups=groups, tiled=True)  7.81 us
    pallas_call x2, Pallas kernels, input_part(): pl.pallas_call(input_part_kernel, in_specs=[pl.BlockSpec(memory_space=plt...  4.83 us
    all_to_all x1, waiting for transfers between devices, swap(): lax.all_to_all(blocks, axis, 0, 0, axis_index_groups=groups, tiled=True)  4.31 us
  transfers between devices with their start and end apart: 8, of which 1 were waited for; matrix products, arithmetic and copies ran while one was open for 5% of the time, Pallas kernels for 3%

profile of v7, /device:TPU:1, one launch (start us, length us, event | category | flops | bytes accessed | tf_op | source)
XLA Modules:
  0.0 121.0 jit_solution(13626202406144422805)
XLA Ops:
  7.2 0.0 copy-start
  7.2 0.0 copy-start.2
  7.2 0.0 copy-start.3
  7.2 0.0 all-gather.2.cloned.1.call-start
  7.2 0.7 all-gather.2.cloned.1.call-update
  7.9 0.5 copy-done
  8.5 0.7 copy.10
  9.1 7.8 %all-to-all-start = ((bf16[4,24,768]{2,1,0:T(8,128)(2,1)}), bf16[4,24,768]{2,1,0:T(8,128)(2,1)S(1)}, u32[]{:S(2)}, u32[]{:S(2)}) async-start(bf16[4,24,768]{2,1,0:T(8,128)(2,1)} %bitcast.13), calls=%async_computation | async-start | bytes 294912 | tf_op jit(solution)/shard_map/all_to_all | solution.py:67
  16.9 0.0 reduce-scatter.2.cloned.1.call-start
  16.9 0.1 pad_add_fusion.1.place
  17.0 0.0 copy-done.2
  17.0 0.0 copy-done.3
  17.0 0.4 fusion.14.refs_0_
  17.4 4.3 %all-to-all-done.blocks = bf16[4,24,768]{2,1,0:T(8,128)(2,1)S(1)} async-done(((bf16[4,24,768]{2,1,0:T(8,128)(2,1)}), bf16[4,24,768]{2,1,0:T(8,128)(2,1)S(1)}, u32[]{:S(2)}, u32[]{:S(2)}) %all-to-all-start) | async-done | bytes 147488 | tf_op jit(solution)/shard_map/all_to_all | solution.py:67
  21.7 0.0 copy-start.1
  21.8 3.0 %collective-permute-start = (bf16[192,768]{1,0:T(8,128)(2,1)S(1)}, bf16[192,768]{1,0:T(8,128)(2,1)S(1)}, u32[]{:S(2)}, u32[]{:S(2)}) collective-permute-start(bf16[192,768]{1,0:T(8,128)(2,1)S(1)} %fusion.14.refs_0_), channel_id=1, source_target_pairs={{0,128},{1,129},{2,130},{3,131},{4,132},{5,133},{6,134},{7,135},{8... | collective-permute-start | bytes 884744 | tf_op jit(solution)/shard_map/ppermute | solution.py:46
  24.7 2.6 %collective-permute-start.1 = (bf16[192,768]{1,0:T(8,128)(2,1)S(1)}, bf16[192,768]{1,0:T(8,128)(2,1)S(1)}, u32[]{:S(2)}, u32[]{:S(2)}) collective-permute-start(bf16[192,768]{1,0:T(8,128)(2,1)S(1)} %fusion.14.refs_0_), channel_id=1, source_target_pairs={{0,256},{1,257},{2,258},{3,259},{4,260},{5,261},{6,262},{7,263},{8... | collective-permute-start | bytes 884744 | tf_op jit(solution)/shard_map/ppermute | solution.py:46
  27.3 3.4 %collective-permute-start.2 = (bf16[192,768]{1,0:T(8,128)(2,1)S(1)}, bf16[192,768]{1,0:T(8,128)(2,1)S(1)}, u32[]{:S(2)}, u32[]{:S(2)}) collective-permute-start(bf16[192,768]{1,0:T(8,128)(2,1)S(1)} %fusion.14.refs_0_), channel_id=1, source_target_pairs={{0,384},{1,385},{2,386},{3,387},{4,388},{5,389},{6,390},{7,391},{8... | collective-permute-start | bytes 884744 | tf_op jit(solution)/shard_map/ppermute | solution.py:46
  30.8 0.0 copy-done.1
  30.8 1.6 %shard_map.59 = bf16[4,24,768]{2,1,0:T(8,128)(2,1)} custom-call(s32[1]{0:T(128)} %bitcast.place, bf16[4,24,768]{2,1,0:T(8,128)(2,1)} %copy-done.1), custom_call_target="tpu_custom_call" | custom-call | bytes 294912 | tf_op jit(solution)/shard_map/pallas_call | solution.py:76
  32.4 11.3 %all_gather.12 = bf16[4,96,768]{2,1,0:T(8,128)(2,1)S(1)} all-gather(bf16[4,24,768]{2,1,0:T(8,128)(2,1)} %shard_map.59), channel_id=1, replica_groups={{0,4,8,12},{1,5,9,13},{2,6,10,14},{3,7,11,15},{16,20,24,28},{17,21,25,2..., dimensions={1}, use_global_device_ids=true | all-gather | bytes 737280 | tf_op jit(solution)/shard_map/all_gather | solution.py:186
  43.7 8.1 %all_gather.13 = bf16[2,192,768]{2,1,0:T(8,128)(2,1)S(1)} all-gather(bf16[2,96,768]{2,1,0:T(8,128)(2,1)S(1)} %get-tuple-element.29), channel_id=1, replica_groups={{0,1},{2,3},{4,5},{6,7},{8,9},{10,11},{12,13},{14,15},{16,17},{18,19},{..., dimensions={1}, use_global_device_ids=true | all-gather | bytes 884736 | tf_op jit(solution)/shard_map/all_gather | solution.py:188
  51.8 2.2 %all_gather.14 = bf16[2,192,768]{2,1,0:T(8,128)(2,1)S(1)} all-gather(bf16[2,96,768]{2,1,0:T(8,128)(2,1)S(1)} %get-tuple-element.28), channel_id=1, replica_groups={{0,1},{2,3},{4,5},{6,7},{8,9},{10,11},{12,13},{14,15},{16,17},{18,19},{..., dimensions={1}, use_global_device_ids=true | all-gather | bytes 884736 | tf_op jit(solution)/shard_map/all_gather | solution.py:188
  54.0 0.0 collective-permute-done.refs_1_
  54.0 0.0 collective-permute-done.1.refs_2_
  54.0 0.0 collective-permute-done.2.refs_3_
  54.0 0.1 pad_maximum_fusion
  54.1 2.1 %convolution_convert_fusion = bf16[768,768]{1,0:T(8,128)(2,1)} fusion(bf16[768,768]{1,0:T(8,128)(2,1)S(1)} %bitcast.14, bf16[192,768]{1,0:T(8,128)(2,1)S(1)} %collective-permute-done.2.refs_3_, bf16[192,768]{1,0:T(8,128)(2,1)S(1)} %collective-permute-done.1.refs_2_, bf16[192,768]{1,0:T(8,128)(2,1)S(1)} %collective-permute-done.refs_1_, ...), kind=kOutput, calls=%fused_computation | convolution fusion | flops 911278080 | bytes 3538944 | tf_op jit(solution)/shard_map/dot_general | solution.py:194
  56.3 0.0 all-gather.2.cloned.1.call-done.refs_4_
  56.3 2.4 %shard_map.61 = bf16[4,4,48,384]{3,2,1,0:T(8,128)(2,1)S(1)} custom-call(s32[2]{0:T(128)S(1)} %pad_add_fusion.1.place, bf16[192,768]{1,0:T(8,128)(2,1)S(1)} %fusion.14.refs_0_, bf16[192,768]{1,0:T(8,128)(2,1)S(1)} %collective-permute-done.refs_1_, bf16[192,768]{1,0:T(8,128)(2,1)S(1)} %collective-permute-done.1.refs_2_, ...), custom_call_target="tpu_custom_call" | custom-call | flops 452984832 | bytes 2359296 | tf_op jit(solution)/shard_map/pallas_call | solution.py:109
  58.7 3.1 %collective-permute-start.3 = (bf16[4,4,48,384]{3,2,1,0:T(8,128)(2,1)S(1)}, bf16[4,4,48,384]{3,2,1,0:T(8,128)(2,1)S(1)}, u32[]{:S(2)}, u32[]{:S(2)}) collective-permute-start(bf16[4,4,48,384]{3,2,1,0:T(8,128)(2,1)S(1)} %shard_map.61), channel_id=1, source_target_pairs={{0,1},{1,0},{2,3},{3,2},{4,5},{5,4},{6,7},{7,6},{8,9},{9,8},{10,11... | collective-permute-start | bytes 1769480 | tf_op jit(solution)/shard_map/ppermute | solution.py:46
  61.8 0.0 reduce-scatter.2.cloned.1.call-update
  61.8 0.1 pad_add_fusion.place
  61.9 2.4 %shard_map.60 = bf16[4,4,48,384]{3,2,1,0:T(8,128)(2,1)S(1)} custom-call(s32[2]{0:T(128)S(1)} %pad_add_fusion.place, bf16[192,768]{1,0:T(8,128)(2,1)S(1)} %fusion.14.refs_0_, bf16[192,768]{1,0:T(8,128)(2,1)S(1)} %collective-permute-done.refs_1_, bf16[192,768]{1,0:T(8,128)(2,1)S(1)} %collective-permute-done.1.refs_2_, ...), custom_call_target="tpu_custom_call" | custom-call | flops 452984832 | bytes 2359296 | tf_op jit(solution)/shard_map/pallas_call | solution.py:109
  64.3 0.0 collective-permute-done.3
  64.3 0.2 add_convert_fusion
  64.5 13.5 %all_to_all.20 = bf16[4,4,48,384]{3,2,1,0:T(8,128)(2,1)S(1)} all-to-all(bf16[4,4,48,384]{3,2,1,0:T(8,128)(2,1)S(1)} %add_convert_fusion), channel_id=1, replica_groups={{0,4,8,12},{1,5,9,13},{2,6,10,14},{3,7,11,15},{16,20,24,28},{17,21,25,2..., dimensions={0} | all-to-all | bytes 1179648 | tf_op jit(solution)/shard_map/all_to_all | solution.py:67
  78.0 0.1 reduce_sum.24
  78.1 17.3 %all_to_all.21 = bf16[8,48,384]{2,1,0:T(8,128)(2,1)S(1)} all-to-all(bf16[8,48,384]{2,1,0:T(8,128)(2,1)S(1)} %bitcast.16), channel_id=1, replica_groups={{0,128,256,384,2,130,258,386},{1,129,257,385,3,131,259,387},{4,132,260,..., dimensions={0} | all-to-all | bytes 589824 | tf_op jit(solution)/shard_map/all_to_all | solution.py:67
  95.4 0.1 reduce_sum.25
  95.4 0.1 broadcast_in_dim.5
  95.5 9.7 %all_to_all.22.mine = bf16[4,4,48,384]{3,2,1,0:T(8,128)(2,1)S(1)} all-to-all(bf16[4,4,48,384]{3,2,1,0:T(8,128)(2,1)S(1)} %broadcast_in_dim.5), channel_id=1, replica_groups={{0,4,8,12},{1,5,9,13},{2,6,10,14},{3,7,11,15},{16,20,24,28},{17,21,25,2..., dimensions={0} | all-to-all | bytes 1179648 | tf_op jit(solution)/shard_map/all_to_all | solution.py:67
  105.2 6.2 %collective-permute-start.4 = (bf16[4,4,48,384]{3,2,1,0:T(8,128)(2,1)S(1)}, bf16[4,4,48,384]{3,2,1,0:T(8,128)(2,1)S(1)}, u32[]{:S(2)}, u32[]{:S(2)}) collective-permute-start(bf16[4,4,48,384]{3,2,1,0:T(8,128)(2,1)S(1)} %all_to_all.22.mine), channel_id=1, source_target_pairs={{0,1},{1,0},{2,3},{3,2},{4,5},{5,4},{6,7},{7,6},{8,9},{9,8},{10,11... | collective-permute-start | bytes 1769480 | tf_op jit(solution)/shard_map/ppermute | solution.py:46
  111.4 0.0 reduce-scatter.2.cloned.1.call-done
  111.4 1.6 %multiply_convert_fusion = bf16[96,768]{1,0:T(8,128)(2,1)} fusion(bf16[96,768]{1,0:T(8,128)(2,1)} %reduce-scatter.2.cloned.1.call-done), kind=kLoop, calls=%fused_computation.26 | loop fusion | flops 221184 | bytes 294912 | tf_op jit(solution)/shard_map/convert_element_type | solution.py:204
  113.0 0.0 collective-permute-done.4.theirs
  113.0 1.1 shard_map.62
  (3 shorter events, 0.1 us)
Async XLA Ops:
  7.2 1.3 %copy-start = (bf16[192,3072]{1,0:T(8,128)(2,1)S(1)}, bf16[192,3072]{1,0:T(8,128)(2,1)}, u32[]{:S(2)}) copy-start(bf16[192,3072]{1,0:T(8,128)(2,1)} %param.4) | copy-start | bytes 3538948
  7.2 9.8 %copy-start.2 = (bf16[192,768]{1,0:T(8,128)(2,1)S(1)}, bf16[192,768]{1,0:T(8,128)(2,1)}, u32[]{:S(2)}) copy-start(bf16[192,768]{1,0:T(8,128)(2,1)} %param.5) | copy-start | bytes 884740
  7.2 9.8 %copy-start.3 = (bf16[192,768]{1,0:T(8,128)(2,1)S(1)}, bf16[192,768]{1,0:T(8,128)(2,1)}, u32[]{:S(2)}) copy-start(bf16[192,768]{1,0:T(8,128)(2,1)} %param.6) | copy-start | bytes 884740
  7.2 49.1 %all-gather.2.cloned.1.call-start = ((), (), s32[]{:S(2)}) async-start(), calls=%async_computation.6 | async-start | bytes 1327104 | tf_op jit(solution)/shard_map/all_gather | solution.py:176
  9.1 12.6 %all-to-all-start = ((bf16[4,24,768]{2,1,0:T(8,128)(2,1)}), bf16[4,24,768]{2,1,0:T(8,128)(2,1)S(1)}, u32[]{:S(2)}, u32[]{:S(2)}) async-start(bf16[4,24,768]{2,1,0:T(8,128)(2,1)} %bitcast.13), calls=%async_computation | async-start | bytes 294912 | tf_op jit(solution)/shard_map/all_to_all | solution.py:67
  16.9 94.5 %reduce-scatter.2.cloned.1.call-start = ((), (), s32[]{:S(2)}) async-start(), calls=%async_computation.5 | async-start | bytes 1327104 | tf_op jit(solution)/shard_map/reduce_scatter | solution.py:201
  21.7 9.0 %copy-start.1 = (bf16[4,24,768]{2,1,0:T(8,128)(2,1)}, bf16[4,24,768]{2,1,0:T(8,128)(2,1)S(1)}, u32[]{:S(2)}) copy-start(bf16[4,24,768]{2,1,0:T(8,128)(2,1)S(1)} %all-to-all-done.blocks) | copy-start | bytes 442372
  21.8 32.3 %collective-permute-start = (bf16[192,768]{1,0:T(8,128)(2,1)S(1)}, bf16[192,768]{1,0:T(8,128)(2,1)S(1)}, u32[]{:S(2)}, u32[]{:S(2)}) collective-permute-start(bf16[192,768]{1,0:T(8,128)(2,1)S(1)} %fusion.14.refs_0_), channel_id=1, source_target_pairs={{0,128},{1,129},{2,130},{3,131},{4,132},{5,133},{6,134},{7,135},{8... | collective-permute-start | bytes 884744 | tf_op jit(solution)/shard_map/ppermute | solution.py:46
  24.7 29.3 %collective-permute-start.1 = (bf16[192,768]{1,0:T(8,128)(2,1)S(1)}, bf16[192,768]{1,0:T(8,128)(2,1)S(1)}, u32[]{:S(2)}, u32[]{:S(2)}) collective-permute-start(bf16[192,768]{1,0:T(8,128)(2,1)S(1)} %fusion.14.refs_0_), channel_id=1, source_target_pairs={{0,256},{1,257},{2,258},{3,259},{4,260},{5,261},{6,262},{7,263},{8... | collective-permute-start | bytes 884744 | tf_op jit(solution)/shard_map/ppermute | solution.py:46
  27.3 26.7 %collective-permute-start.2 = (bf16[192,768]{1,0:T(8,128)(2,1)S(1)}, bf16[192,768]{1,0:T(8,128)(2,1)S(1)}, u32[]{:S(2)}, u32[]{:S(2)}) collective-permute-start(bf16[192,768]{1,0:T(8,128)(2,1)S(1)} %fusion.14.refs_0_), channel_id=1, source_target_pairs={{0,384},{1,385},{2,386},{3,387},{4,388},{5,389},{6,390},{7,391},{8... | collective-permute-start | bytes 884744 | tf_op jit(solution)/shard_map/ppermute | solution.py:46
  58.7 5.6 %collective-permute-start.3 = (bf16[4,4,48,384]{3,2,1,0:T(8,128)(2,1)S(1)}, bf16[4,4,48,384]{3,2,1,0:T(8,128)(2,1)S(1)}, u32[]{:S(2)}, u32[]{:S(2)}) collective-permute-start(bf16[4,4,48,384]{3,2,1,0:T(8,128)(2,1)S(1)} %shard_map.61), channel_id=1, source_target_pairs={{0,1},{1,0},{2,3},{3,2},{4,5},{5,4},{6,7},{7,6},{8,9},{9,8},{10,11... | collective-permute-start | bytes 1769480 | tf_op jit(solution)/shard_map/ppermute | solution.py:46
  105.2 7.8 %collective-permute-start.4 = (bf16[4,4,48,384]{3,2,1,0:T(8,128)(2,1)S(1)}, bf16[4,4,48,384]{3,2,1,0:T(8,128)(2,1)S(1)}, u32[]{:S(2)}, u32[]{:S(2)}) collective-permute-start(bf16[4,4,48,384]{3,2,1,0:T(8,128)(2,1)S(1)} %all_to_all.22.mine), channel_id=1, source_target_pairs={{0,1},{1,0},{2,3},{3,2},{4,5},{5,4},{6,7},{7,6},{8,9},{9,8},{10,11... | collective-permute-start | bytes 1769480 | tf_op jit(solution)/shard_map/ppermute | solution.py:46
Sparse Core Ops, SparseCore 0:
  10.1 42.9 all-gather.1
  62.0 36.4 reduce-scatter.1

commit v8 on v6

--- a/solution.py
+++ b/solution.py
@@ -83,17 +83,25 @@
 
 
 def input_parts_kernel(place, *refs):
-    blocks, weight, outs = refs[:Z_LO], refs[Z_LO], refs[Z_LO + 1 :]
+    blocks, weight, outs = refs[:Z_LO], refs[Z_LO], refs[Z_LO + 1 : Z_LO + 1 + CORE]
+    chosen, arrived = refs[-2], refs[-1]
     rows = blocks[0].shape[0]
     piece = rows // X
-    half = weight.shape[0] // CORE
+    half = chosen.shape[1]
+    copies = [
+        pltpu.make_async_copy(
+            weight.at[pl.ds(pl.multiple_of(which * half, half), half)], chosen.at[i], arrived.at[i]
+        )
+        for i, which in enumerate((1 - place[1], place[1]))
+    ]
+    copies[0].start()
     lhs = jnp.concatenate([block[...] for block in blocks], axis=0)
-    for out, which in zip(outs, (1 - place[1], place[1])):
+    for i, out in enumerate(outs):
+        copies[i].wait()
+        if i + 1 < len(copies):
+            copies[i + 1].start()
         result = lax.dot_general(
-            lhs,
-            weight[pl.ds(pl.multiple_of(which * half, half), half), :],
-            (((1,), (1,)), ((), ())),
-            preferred_element_type=jnp.float32,
+            lhs, chosen[i], (((1,), (1,)), ((), ())), preferred_element_type=jnp.float32
         )
         for k in range(Z_LO):
             owner = jnp.bitwise_and(place[0] + (Z_LO - k), Z_LO - 1)
@@ -109,16 +117,21 @@
     return pl.pallas_call(
         input_parts_kernel,
         in_specs=[pl.BlockSpec(memory_space=pltpu.SMEM)]
-        + [pl.BlockSpec(memory_space=pltpu.VMEM)] * (Z_LO + 1),
-        out_specs=[pl.BlockSpec(memory_space=pltpu.VMEM)] * 2,
-        out_shape=[out, out],
+        + [pl.BlockSpec(memory_space=pltpu.VMEM)] * Z_LO
+        + [pl.BlockSpec(memory_space=pltpu.HBM)],
+        out_specs=[pl.BlockSpec(memory_space=pltpu.VMEM)] * CORE,
+        out_shape=[out] * CORE,
+        scratch_shapes=[
+            pltpu.VMEM((CORE, half, units), jnp.bfloat16),
+            pltpu.SemaphoreType.DMA((CORE,)),
+        ],
         compiler_params=pltpu.CompilerParams(vmem_limit_bytes=32 * 1024 * 1024),
         cost_estimate=pl.CostEstimate(
             flops=4 * Z_LO * rows * units * half,
             bytes_accessed=2 * (Z_LO * rows * units + 2 * half * units + 2 * Z_LO * rows * half),
             transcendentals=0,
         ),
-    )(place, *blocks, weight)
+    )(place, *blocks, pltpu.with_memory_space_constraint(weight, pltpu.HBM))
 
 
 def joined_kernel(core, mine, theirs, out):

time: 121 us -> 122 us (level)
  Pallas kernels: 4.63 us -> 6.21 us
  local copies, waits for them, and re-layouts: 2.59 us -> 1.32 us
    pallas_call x1, Pallas kernels: 1.93 us -> 3.5 us  [input_parts(): pl.pallas_call(input_parts_kernel, in_specs=[pl.BlockSpec(memory_space=pl...]
    unnamed x10 -> x8, local copies, waits for them, and re-layouts: 1.79 us -> 0.52 us
  transfers between devices with their start and end apart: 8 -> 8, of which waited for: 2 -> 2; matrix products, arithmetic and copies ran while one was open for 5% -> 4% of each run, Pallas kernels for 1% -> 1%
where the time goes in v8:
time: 122 us; the launch traced here: 121 us
  blocking collectives  61.6 us (50%)
  starting transfers between devices  26.4 us (22%)
  between operations  14.2 us (12%)
  waiting for transfers between devices  6.63 us (5%)
  Pallas kernels  6.21 us (5%)
  other arithmetic  2.5 us (2%)
  matrix products  2.14 us (2%)
  local copies, waits for them, and re-layouts  1.32 us (1%)
    all_to_all x3, blocking collectives, swap(): lax.all_to_all(blocks, axis, 0, 0, axis_index_groups=groups, tiled=True)  40 us
    ppermute x5, starting transfers between devices, moved(): return lax.ppermute(value, AXES, pairs)  18.6 us
    all_gather x1, blocking collectives, shards(): lax.all_gather(mine, 'mp', axis=1, axis_index_groups=X_GROUPS, tiled=True)  11.3 us
    all_gather x2, blocking collectives, shards(): lax.all_gather(mine[k:k + 2], 'mp', axis=1, axis_index_groups=C_GROUPS, t...  10.3 us
    all_to_all x1, starting transfers between devices, swap(): lax.all_to_all(blocks, axis, 0, 0, axis_index_groups=groups, tiled=True)  7.81 us
    all_to_all x1, waiting for transfers between devices, swap(): lax.all_to_all(blocks, axis, 0, 0, axis_index_groups=groups, tiled=True)  4.31 us
    pallas_call x1, Pallas kernels, input_parts(): pl.pallas_call(input_parts_kernel, in_specs=[pl.BlockSpec(memory_space=pl...  3.5 us
  transfers between devices with their start and end apart: 8, of which 2 were waited for; matrix products, arithmetic and copies ran while one was open for 4% of the time, Pallas kernels for 1%

profile of v8, /device:TPU:1, one launch (start us, length us, event | category | flops | bytes accessed | tf_op | source)
XLA Modules:
  0.0 121.0 jit_solution(1312564093502181622)
XLA Ops:
  7.2 0.0 copy-start
  7.2 0.0 copy-start.2
  7.2 0.0 copy-start.3
  7.2 0.0 all-gather.2.cloned.1.call-start
  7.2 0.7 all-gather.2.cloned.1.call-update
  7.9 0.5 copy-done
  8.5 0.7 copy.10
  9.1 7.8 %all-to-all-start = ((bf16[4,24,768]{2,1,0:T(8,128)(2,1)}), bf16[4,24,768]{2,1,0:T(8,128)(2,1)S(1)}, u32[]{:S(2)}, u32[]{:S(2)}) async-start(bf16[4,24,768]{2,1,0:T(8,128)(2,1)} %bitcast.12), calls=%async_computation | async-start | bytes 294912 | tf_op jit(solution)/shard_map/all_to_all | solution.py:67
  16.9 0.0 reduce-scatter.2.cloned.1.call-start
  16.9 0.1 pad_add_fusion.place
  17.0 0.0 copy-done.2
  17.0 0.0 copy-done.3
  17.0 0.4 fusion.14.refs_0_
  17.4 4.3 %all-to-all-done.blocks = bf16[4,24,768]{2,1,0:T(8,128)(2,1)S(1)} async-done(((bf16[4,24,768]{2,1,0:T(8,128)(2,1)}), bf16[4,24,768]{2,1,0:T(8,128)(2,1)S(1)}, u32[]{:S(2)}, u32[]{:S(2)}) %all-to-all-start) | async-done | bytes 147488 | tf_op jit(solution)/shard_map/all_to_all | solution.py:67
  21.7 0.0 copy-start.1
  21.8 3.0 %collective-permute-start = (bf16[192,768]{1,0:T(8,128)(2,1)S(1)}, bf16[192,768]{1,0:T(8,128)(2,1)S(1)}, u32[]{:S(2)}, u32[]{:S(2)}) collective-permute-start(bf16[192,768]{1,0:T(8,128)(2,1)S(1)} %fusion.14.refs_0_), channel_id=1, source_target_pairs={{0,128},{1,129},{2,130},{3,131},{4,132},{5,133},{6,134},{7,135},{8... | collective-permute-start | bytes 884744 | tf_op jit(solution)/shard_map/ppermute | solution.py:46
  24.7 2.6 %collective-permute-start.1 = (bf16[192,768]{1,0:T(8,128)(2,1)S(1)}, bf16[192,768]{1,0:T(8,128)(2,1)S(1)}, u32[]{:S(2)}, u32[]{:S(2)}) collective-permute-start(bf16[192,768]{1,0:T(8,128)(2,1)S(1)} %fusion.14.refs_0_), channel_id=1, source_target_pairs={{0,256},{1,257},{2,258},{3,259},{4,260},{5,261},{6,262},{7,263},{8... | collective-permute-start | bytes 884744 | tf_op jit(solution)/shard_map/ppermute | solution.py:46
  27.3 3.4 %collective-permute-start.2 = (bf16[192,768]{1,0:T(8,128)(2,1)S(1)}, bf16[192,768]{1,0:T(8,128)(2,1)S(1)}, u32[]{:S(2)}, u32[]{:S(2)}) collective-permute-start(bf16[192,768]{1,0:T(8,128)(2,1)S(1)} %fusion.14.refs_0_), channel_id=1, source_target_pairs={{0,384},{1,385},{2,386},{3,387},{4,388},{5,389},{6,390},{7,391},{8... | collective-permute-start | bytes 884744 | tf_op jit(solution)/shard_map/ppermute | solution.py:46
  30.8 0.0 copy-done.1
  30.8 1.6 %shard_map.59 = bf16[4,24,768]{2,1,0:T(8,128)(2,1)} custom-call(s32[1]{0:T(128)} %bitcast.place, bf16[4,24,768]{2,1,0:T(8,128)(2,1)} %copy-done.1), custom_call_target="tpu_custom_call" | custom-call | bytes 294912 | tf_op jit(solution)/shard_map/pallas_call | solution.py:76
  32.4 11.3 %all_gather.12 = bf16[4,96,768]{2,1,0:T(8,128)(2,1)S(1)} all-gather(bf16[4,24,768]{2,1,0:T(8,128)(2,1)} %shard_map.59), channel_id=1, replica_groups={{0,4,8,12},{1,5,9,13},{2,6,10,14},{3,7,11,15},{16,20,24,28},{17,21,25,2..., dimensions={1}, use_global_device_ids=true | all-gather | bytes 737280 | tf_op jit(solution)/shard_map/all_gather | solution.py:196
  43.7 8.1 %all_gather.13 = bf16[2,192,768]{2,1,0:T(8,128)(2,1)S(1)} all-gather(bf16[2,96,768]{2,1,0:T(8,128)(2,1)S(1)} %get-tuple-element.33), channel_id=1, replica_groups={{0,1},{2,3},{4,5},{6,7},{8,9},{10,11},{12,13},{14,15},{16,17},{18,19},{..., dimensions={1}, use_global_device_ids=true | all-gather | bytes 884736 | tf_op jit(solution)/shard_map/all_gather | solution.py:198
  51.8 2.2 %all_gather.14 = bf16[2,192,768]{2,1,0:T(8,128)(2,1)S(1)} all-gather(bf16[2,96,768]{2,1,0:T(8,128)(2,1)S(1)} %get-tuple-element.32), channel_id=1, replica_groups={{0,1},{2,3},{4,5},{6,7},{8,9},{10,11},{12,13},{14,15},{16,17},{18,19},{..., dimensions={1}, use_global_device_ids=true | all-gather | bytes 884736 | tf_op jit(solution)/shard_map/all_gather | solution.py:198
  54.0 0.0 collective-permute-done.refs_1_
  54.0 0.0 collective-permute-done.1.refs_2_
  54.0 0.0 collective-permute-done.2.refs_3_
  54.0 0.1 pad_maximum_fusion
  54.1 2.1 %convolution_convert_fusion = bf16[768,768]{1,0:T(8,128)(2,1)} fusion(bf16[768,768]{1,0:T(8,128)(2,1)S(1)} %bitcast.13, bf16[192,768]{1,0:T(8,128)(2,1)S(1)} %collective-permute-done.2.refs_3_, bf16[192,768]{1,0:T(8,128)(2,1)S(1)} %collective-permute-done.1.refs_2_, bf16[192,768]{1,0:T(8,128)(2,1)S(1)} %collective-permute-done.refs_1_, ...), kind=kOutput, calls=%fused_computation | convolution fusion | flops 911278080 | bytes 3538944 | tf_op jit(solution)/shard_map/dot_general | solution.py:204
  56.3 0.0 all-gather.2.cloned.1.call-done.refs_4_
  56.3 3.5 %shard_map.60 = (bf16[4,4,48,384]{3,2,1,0:T(8,128)(2,1)S(1)}, bf16[4,4,48,384]{3,2,1,0:T(8,128)(2,1)S(1)}) custom-call(s32[2]{0:T(128)S(1)} %pad_add_fusion.place, bf16[192,768]{1,0:T(8,128)(2,1)S(1)} %fusion.14.refs_0_, bf16[192,768]{1,0:T(8,128)(2,1)S(1)} %collective-permute-done.refs_1_, bf16[192,768]{1,0:T(8,128)(2,1)S(1)} %collective-permute-done.1.refs_2_, ...), custom_call_target="tpu_custom_call" | custom-call | flops 905969664 | bytes 3538944 | tf_op jit(solution)/shard_map/pallas_call | solution.py:117
  59.8 3.1 %collective-permute-start.3 = (bf16[4,4,48,384]{3,2,1,0:T(8,128)(2,1)S(1)}, bf16[4,4,48,384]{3,2,1,0:T(8,128)(2,1)S(1)}, u32[]{:S(2)}, u32[]{:S(2)}) collective-permute-start(bf16[4,4,48,384]{3,2,1,0:T(8,128)(2,1)S(1)} %get-tuple-element.31), channel_id=1, source_target_pairs={{0,1},{1,0},{2,3},{3,2},{4,5},{5,4},{6,7},{7,6},{8,9},{9,8},{10,11... | collective-permute-start | bytes 1769480 | tf_op jit(solution)/shard_map/ppermute | solution.py:46
  62.9 0.0 reduce-scatter.2.cloned.1.call-update
  62.9 1.6 %collective-permute-done.3 = bf16[4,4,48,384]{3,2,1,0:T(8,128)(2,1)S(1)} collective-permute-done((bf16[4,4,48,384]{3,2,1,0:T(8,128)(2,1)S(1)}, bf16[4,4,48,384]{3,2,1,0:T(8,128)(2,1)S(1)}, u32[]{:S(2)}, u32[]{:S(2)}) %collective-permute-start.3) | collective-permute-done | bytes 589856 | tf_op jit(solution)/shard_map/ppermute | solution.py:46
  64.5 0.2 add_convert_fusion
  64.7 13.4 %all_to_all.20 = bf16[4,4,48,384]{3,2,1,0:T(8,128)(2,1)S(1)} all-to-all(bf16[4,4,48,384]{3,2,1,0:T(8,128)(2,1)S(1)} %add_convert_fusion), channel_id=1, replica_groups={{0,4,8,12},{1,5,9,13},{2,6,10,14},{3,7,11,15},{16,20,24,28},{17,21,25,2..., dimensions={0} | all-to-all | bytes 1179648 | tf_op jit(solution)/shard_map/all_to_all | solution.py:67
  78.0 0.1 reduce_sum.24
  78.2 17.0 %all_to_all.21 = bf16[8,48,384]{2,1,0:T(8,128)(2,1)S(1)} all-to-all(bf16[8,48,384]{2,1,0:T(8,128)(2,1)S(1)} %bitcast.15), channel_id=1, replica_groups={{0,128,256,384,2,130,258,386},{1,129,257,385,3,131,259,387},{4,132,260,..., dimensions={0} | all-to-all | bytes 589824 | tf_op jit(solution)/shard_map/all_to_all | solution.py:67
  95.1 0.1 reduce_sum.25
  95.2 0.1 broadcast_in_dim.5
  95.3 9.7 %all_to_all.22.mine = bf16[4,4,48,384]{3,2,1,0:T(8,128)(2,1)S(1)} all-to-all(bf16[4,4,48,384]{3,2,1,0:T(8,128)(2,1)S(1)} %broadcast_in_dim.5), channel_id=1, replica_groups={{0,4,8,12},{1,5,9,13},{2,6,10,14},{3,7,11,15},{16,20,24,28},{17,21,25,2..., dimensions={0} | all-to-all | bytes 1179648 | tf_op jit(solution)/shard_map/all_to_all | solution.py:67
  104.9 6.5 %collective-permute-start.4 = (bf16[4,4,48,384]{3,2,1,0:T(8,128)(2,1)S(1)}, bf16[4,4,48,384]{3,2,1,0:T(8,128)(2,1)S(1)}, u32[]{:S(2)}, u32[]{:S(2)}) collective-permute-start(bf16[4,4,48,384]{3,2,1,0:T(8,128)(2,1)S(1)} %all_to_all.22.mine), channel_id=1, source_target_pairs={{0,1},{1,0},{2,3},{3,2},{4,5},{5,4},{6,7},{7,6},{8,9},{9,8},{10,11... | collective-permute-start | bytes 1769480 | tf_op jit(solution)/shard_map/ppermute | solution.py:46
  111.4 0.0 reduce-scatter.2.cloned.1.call-done
  111.5 1.6 %multiply_convert_fusion = bf16[96,768]{1,0:T(8,128)(2,1)} fusion(bf16[96,768]{1,0:T(8,128)(2,1)} %reduce-scatter.2.cloned.1.call-done), kind=kLoop, calls=%fused_computation.26 | loop fusion | flops 221184 | bytes 294912 | tf_op jit(solution)/shard_map/convert_element_type | solution.py:214
  113.1 0.0 collective-permute-done.4.theirs
  113.1 1.1 shard_map.61
  (3 shorter events, 0.1 us)
Async XLA Ops:
  7.2 1.3 %copy-start = (bf16[192,3072]{1,0:T(8,128)(2,1)S(1)}, bf16[192,3072]{1,0:T(8,128)(2,1)}, u32[]{:S(2)}) copy-start(bf16[192,3072]{1,0:T(8,128)(2,1)} %param.4) | copy-start | bytes 3538948
  7.2 9.8 %copy-start.2 = (bf16[192,768]{1,0:T(8,128)(2,1)S(1)}, bf16[192,768]{1,0:T(8,128)(2,1)}, u32[]{:S(2)}) copy-start(bf16[192,768]{1,0:T(8,128)(2,1)} %param.5) | copy-start | bytes 884740
  7.2 9.8 %copy-start.3 = (bf16[192,768]{1,0:T(8,128)(2,1)S(1)}, bf16[192,768]{1,0:T(8,128)(2,1)}, u32[]{:S(2)}) copy-start(bf16[192,768]{1,0:T(8,128)(2,1)} %param.6) | copy-start | bytes 884740
  7.2 49.1 %all-gather.2.cloned.1.call-start = ((), (), s32[]{:S(2)}) async-start(), calls=%async_computation.6 | async-start | bytes 1327104 | tf_op jit(solution)/shard_map/all_gather | solution.py:186
  9.1 12.6 %all-to-all-start = ((bf16[4,24,768]{2,1,0:T(8,128)(2,1)}), bf16[4,24,768]{2,1,0:T(8,128)(2,1)S(1)}, u32[]{:S(2)}, u32[]{:S(2)}) async-start(bf16[4,24,768]{2,1,0:T(8,128)(2,1)} %bitcast.12), calls=%async_computation | async-start | bytes 294912 | tf_op jit(solution)/shard_map/all_to_all | solution.py:67
  16.9 94.5 %reduce-scatter.2.cloned.1.call-start = ((), (), s32[]{:S(2)}) async-start(), calls=%async_computation.5 | async-start | bytes 1327104 | tf_op jit(solution)/shard_map/reduce_scatter | solution.py:211
  21.7 9.0 %copy-start.1 = (bf16[4,24,768]{2,1,0:T(8,128)(2,1)}, bf16[4,24,768]{2,1,0:T(8,128)(2,1)S(1)}, u32[]{:S(2)}) copy-start(bf16[4,24,768]{2,1,0:T(8,128)(2,1)S(1)} %all-to-all-done.blocks) | copy-start | bytes 442372
  21.8 32.3 %collective-permute-start = (bf16[192,768]{1,0:T(8,128)(2,1)S(1)}, bf16[192,768]{1,0:T(8,128)(2,1)S(1)}, u32[]{:S(2)}, u32[]{:S(2)}) collective-permute-start(bf16[192,768]{1,0:T(8,128)(2,1)S(1)} %fusion.14.refs_0_), channel_id=1, source_target_pairs={{0,128},{1,129},{2,130},{3,131},{4,132},{5,133},{6,134},{7,135},{8... | collective-permute-start | bytes 884744 | tf_op jit(solution)/shard_map/ppermute | solution.py:46
  24.7 29.3 %collective-permute-start.1 = (bf16[192,768]{1,0:T(8,128)(2,1)S(1)}, bf16[192,768]{1,0:T(8,128)(2,1)S(1)}, u32[]{:S(2)}, u32[]{:S(2)}) collective-permute-start(bf16[192,768]{1,0:T(8,128)(2,1)S(1)} %fusion.14.refs_0_), channel_id=1, source_target_pairs={{0,256},{1,257},{2,258},{3,259},{4,260},{5,261},{6,262},{7,263},{8... | collective-permute-start | bytes 884744 | tf_op jit(solution)/shard_map/ppermute | solution.py:46
  27.3 26.7 %collective-permute-start.2 = (bf16[192,768]{1,0:T(8,128)(2,1)S(1)}, bf16[192,768]{1,0:T(8,128)(2,1)S(1)}, u32[]{:S(2)}, u32[]{:S(2)}) collective-permute-start(bf16[192,768]{1,0:T(8,128)(2,1)S(1)} %fusion.14.refs_0_), channel_id=1, source_target_pairs={{0,384},{1,385},{2,386},{3,387},{4,388},{5,389},{6,390},{7,391},{8... | collective-permute-start | bytes 884744 | tf_op jit(solution)/shard_map/ppermute | solution.py:46
  59.8 4.7 %collective-permute-start.3 = (bf16[4,4,48,384]{3,2,1,0:T(8,128)(2,1)S(1)}, bf16[4,4,48,384]{3,2,1,0:T(8,128)(2,1)S(1)}, u32[]{:S(2)}, u32[]{:S(2)}) collective-permute-start(bf16[4,4,48,384]{3,2,1,0:T(8,128)(2,1)S(1)} %get-tuple-element.31), channel_id=1, source_target_pairs={{0,1},{1,0},{2,3},{3,2},{4,5},{5,4},{6,7},{7,6},{8,9},{9,8},{10,11... | collective-permute-start | bytes 1769480 | tf_op jit(solution)/shard_map/ppermute | solution.py:46
  104.9 8.1 %collective-permute-start.4 = (bf16[4,4,48,384]{3,2,1,0:T(8,128)(2,1)S(1)}, bf16[4,4,48,384]{3,2,1,0:T(8,128)(2,1)S(1)}, u32[]{:S(2)}, u32[]{:S(2)}) collective-permute-start(bf16[4,4,48,384]{3,2,1,0:T(8,128)(2,1)S(1)} %all_to_all.22.mine), channel_id=1, source_target_pairs={{0,1},{1,0},{2,3},{3,2},{4,5},{5,4},{6,7},{7,6},{8,9},{9,8},{10,11... | collective-permute-start | bytes 1769480 | tf_op jit(solution)/shard_map/ppermute | solution.py:46
Sparse Core Ops, SparseCore 0:
  10.1 42.9 all-gather.1
  63.0 36.2 reduce-scatter.1
